TPU v7x, 32 devices: a whole 2x2x4 slice. The times are simulated.
32 devices in a mesh: outer: 4 (over y, core), inner: 8 (over z, x).
Axes of the slice: x: 2, y: 2, z: 4, core: 2. Of those that a mesh axis runs over, the one named last changes fastest.
Arguments:
- queries: bfloat16 [4096, 2048], P(('outer', 'inner')), may hold values from -6 to 6
- key_vectors: bfloat16 [4096, 2048], P(('outer', 'inner')), may hold values from -6 to 6
- value_vectors: bfloat16 [4096, 2048], P(('outer', 'inner')), may hold values from -6 to 6
- segment_ids: int32 [4096], P(('outer', 'inner')), may hold values from 0 to 15, never falling along the last dimension, each value on 1 to 1024 neighbouring positions
- ridge_weight: float32 [16], replicated, may hold values from 2 to 32
Outputs:
- readout: float32 [4096, 2048], P(('outer', 'inner'))
Inputs may be any that keep to these rules, and one draw needn't show every extreme that they name: `segment_ids`: segment ids never fall along the sequence; each document has 1 to 1024 tokens and one has exactly 1024.
All inputs are finite; a program needn't handle non-finite values.
Results may differ from a plain program's by a relative error of at most 0.0003.
Values sent between devices are 32-bit elements; how exact they have to be, the bound alone decides.
No kernel may reach another device: no remote copies, remote signals or barrier semaphores. Data moves between devices by JAX's collectives and lax.ppermute only.
A program may use at most 128 MiB of HBM per device.

v0:
```python
import jax
import jax.numpy as jnp
from jax import lax
from jax.sharding import PartitionSpec as P

CG_ITERS = 3


highest = lax.Precision.HIGHEST


def prefix_2(value, axis, join, neutral):
    count, mine = (lax.axis_size(axis), lax.axis_index(axis))
    pieces = jax.tree.map(lambda part: lax.all_gather(part, axis), value)
    running = jax.tree.map(
        lambda part, zero: jnp.full_like(part, 0) + jnp.asarray(zero, part.dtype), value, neutral
    )

    def hop(position, running):
        longer = join(running, jax.tree.map(lambda part: part[position], pieces))
        return jax.tree.map(lambda new, old: jnp.where(position < mine, new, old), longer, running)

    return lax.fori_loop(0, count - 1, hop, running)


def normed(values_in):
    widened = values_in.astype(jnp.float32)
    return widened * lax.rsqrt(jnp.sum(widened * widened, -1, keepdims=True) + 1e-06)


def combine_stacked(earlier, latter):
    early_last, early_state = earlier
    late_last, late_state = latter
    keep_mask = jnp.logical_or(early_last == late_last, late_last < 0).astype(jnp.float32)
    return (
        jnp.where(late_last < 0, early_last, late_last),
        late_state + keep_mask[..., None, None, None] * early_state,
    )


def summarize(key_rows, value_rows, segment):
    last_value = segment[-1]
    weight = (segment == last_value).astype(jnp.float32)[None, :, None]
    gram = jnp.einsum("hbe,hbf->hef", key_rows * weight, key_rows, precision=highest)
    cross = jnp.einsum("hbv,hbk->hvk", value_rows * weight, key_rows, precision=highest)
    return (last_value.astype(jnp.float32), gram, cross)


def span_solve(query_rows, key_rows, value_rows, segment, prefix, ridge_weight):
    prev_last, gram_in, cross_in = prefix
    segment_value = segment.astype(jnp.float32)
    carried = (segment_value == prev_last).astype(jnp.float32)[None, :, None]
    position = jnp.arange(segment.shape[0])
    within = jnp.logical_and(
        position[:, None] >= position[None, :], segment[:, None] == segment[None, :]
    ).astype(jnp.float32)[None]
    solved = jnp.zeros_like(query_rows)
    remain = query_rows
    search = query_rows
    remain_square = jnp.sum(remain * remain, -1, keepdims=True)
    for _ in range(CG_ITERS):
        apply_from_state = jnp.einsum("hbf,hef->hbe", search, gram_in, precision=highest) * carried
        apply_scores = jnp.einsum("hte,hse->hts", search, key_rows, precision=highest) * within
        local_part = jnp.einsum("hts,hse->hte", apply_scores, key_rows, precision=highest)
        applied = apply_from_state + local_part + ridge_weight[:, None, None] * search
        stepsize = remain_square / jnp.sum(search * applied, -1, keepdims=True)
        solved = solved + stepsize * search
        remain = remain - stepsize * applied
        next_square = jnp.sum(remain * remain, -1, keepdims=True)
        search = remain + next_square / remain_square * search
        remain_square = next_square
    from_state = jnp.einsum("hbk,hvk->hbv", solved, cross_in, precision=highest) * carried
    scores = jnp.einsum("hte,hse->hts", solved, key_rows, precision=highest) * within
    return from_state + jnp.einsum("hts,hsv->htv", scores, value_rows, precision=highest)


def on_device(queries, key_vectors, value_vectors, segment_ids, ridge_weight):
    row_count = queries.shape[0]
    head_count = ridge_weight.shape[0]
    head_width = queries.shape[1] // head_count

    def split_heads(values_in):
        return values_in.reshape(row_count, head_count, head_width).transpose(1, 0, 2)

    query_rows = normed(split_heads(queries))
    key_rows = normed(split_heads(key_vectors))
    value_rows = split_heads(value_vectors).astype(jnp.float32)
    own = summarize(key_rows, value_rows, segment_ids)
    group_size = lax.axis_size("inner")
    share = head_count // group_size
    own_last = jnp.full((1, head_count), own[0], jnp.float32)
    own_state = jnp.stack([own[1], own[2]], 1)[None]
    shard_last, shard_state = (
        lax.all_to_all(own_last, "inner", split_axis=1, concat_axis=0, tiled=True),
        lax.all_to_all(own_state, "inner", split_axis=1, concat_axis=0, tiled=True),
    )
    run_last, run_state = lax.associative_scan(combine_stacked, (shard_last, shard_state), axis=0)
    first_last = jnp.full((1, share), -1.0, jnp.float32)
    first_state = jnp.zeros((1, share, 2, head_width, head_width), jnp.float32)
    excl_last = jnp.concatenate([first_last, run_last[:-1]], 0)
    excl_state = jnp.concatenate([first_state, run_state[:-1]], 0)
    outer_identity = (
        jnp.full((share,), -1.0, jnp.float32),
        jnp.zeros((share, 2, head_width, head_width), jnp.float32),
    )
    before_last, before_state = prefix_2(
        (run_last[-1], run_state[-1]), "outer", combine_stacked, outer_identity
    )
    full_last, full_state = combine_stacked(
        (before_last[None], before_state[None]), (excl_last, excl_state)
    )
    back_last, back_state = (
        lax.all_to_all(full_last, "inner", split_axis=0, concat_axis=1, tiled=True),
        lax.all_to_all(full_state, "inner", split_axis=0, concat_axis=1, tiled=True),
    )
    prefix = (back_last[0, 0], back_state[0, :, 0], back_state[0, :, 1])
    result = span_solve(query_rows, key_rows, value_rows, segment_ids, prefix, ridge_weight)
    return result.transpose(1, 0, 2).reshape(row_count, head_count * head_width)


def solution(mesh):
    in_specs = (
        P(("outer", "inner"), None),
        P(("outer", "inner"), None),
        P(("outer", "inner"), None),
        P(("outer", "inner")),
        P(),
    )
    out_specs = P(("outer", "inner"), None)
    return jax.shard_map(
        on_device, mesh=mesh, in_specs=in_specs, out_specs=out_specs, check_vma=False
    )
```

profile of v0, /device:TPU:0, one launch (start us, length us, event | category | flops | bytes accessed | tf_op | source)
XLA Modules:
  0.0 239.7 jit_solution(12394551952472181201)
XLA Ops:
  6.5 1.4 slice.108
  8.6 0.6 broadcast_in_dim.12
  9.2 7.3 %all-to-all-start.1 = ((f32[1,8,2]{2,0,1:T(1,128)}), f32[1,8,2]{2,0,1:T(1,128)S(1)}, u32[]{:S(2)}, u32[]{:S(2)}) async-start(f32[1,8,2]{2,0,1:T(1,128)} %broadcast_in_dim.12), calls=%async_computation.1 | async-start | bytes 8192 | tf_op jit(solution)/shard_map/all_to_all | solution.py:94
  16.5 1.3 compare_convert_fusion.1
  17.8 1.2 copy.97
  19.2 0.3 copy.98
  19.5 2.3 fusion.4
  21.7 2.3 convolution_bitcast_fusion
  24.0 0.2 maximum_bitcast_fusion
  24.2 1.5 copy.59
  25.7 6.0 %all-to-all-start = ((f32[1,16,2,128,128]{4,3,2,0,1:T(8,128)}), f32[1,16,2,128,128]{4,3,2,0,1:T(8,128)S(1)}, u32[]{:S(2)}, u32[]{:S(2)}) async-start(f32[1,16,2,128,128]{4,3,2,0,1:T(8,128)} %copy.59), calls=%async_computation | async-start | bytes 4194304 | tf_op jit(solution)/shard_map/all_to_all | solution.py:95
  32.6 0.2 compare_select_fusion.3
  33.3 46.1 %all-to-all-done = f32[1,16,2,128,128]{4,3,2,0,1:T(8,128)S(1)} async-done(((f32[1,16,2,128,128]{4,3,2,0,1:T(8,128)}), f32[1,16,2,128,128]{4,3,2,0,1:T(8,128)S(1)}, u32[]{:S(2)}, u32[]{:S(2)}) %all-to-all-start) | async-done | bytes 2097184 | tf_op jit(solution)/shard_map/all_to_all | solution.py:95
  79.4 0.2 multiply_add_fusion.4
  79.6 1.0 copy-done.1
  80.8 0.7 copy-done.4
  81.6 0.8 pad_add_fusion
  82.4 5.7 %pad.47 = f32[4,2,2,128,128]{4,3,2,1,0:T(8,128)} pad(f32[2,2,2,128,128]{4,3,2,1,0:T(8,128)} %pad_add_fusion, f32[]{:T(128)} %constant.45.clone.1), padding=1_0_1x0_0_0x0_0_0x0_0_0x0_0_0 | pad | bytes 1572868 | tf_op jit(solution)/shard_map/pad | solution.py:97
  88.1 1.2 fusion.53
  89.4 0.8 pad_maximum_fusion.1
  90.2 5.7 %pad.46 = f32[4,2,2,128,128]{4,3,2,1,0:T(8,128)} pad(f32[2,2,2,128,128]{4,3,2,1,0:T(8,128)} %pad_maximum_fusion.1, f32[]{:T(128)} %constant.45.clone.1), padding=0_1_1x0_0_0x0_0_0x0_0_0x0_0_0 | pad | bytes 1572868 | tf_op jit(solution)/shard_map/pad | solution.py:97
  95.9 2.7 %add.155 = f32[4,2,2,128,128]{4,3,2,1,0:T(8,128)} add(f32[4,2,2,128,128]{4,3,2,1,0:T(8,128)} %pad.46, f32[4,2,2,128,128]{4,3,2,1,0:T(8,128)} %pad.47) | non-fusion elementwise | flops 262144 | bytes 3145728 | tf_op jit(solution)/shard_map/add | solution.py:97
  98.5 10.1 %pad.91 = f32[7,2,2,128,128]{4,3,2,1,0:T(8,128)} pad(f32[4,2,2,128,128]{4,3,2,1,0:T(8,128)} %add.155, f32[]{:T(128)} %constant.45.clone.1), padding=0_0_1x0_0_0x0_0_0x0_0_0x0_0_0 | pad | bytes 2883588
  108.6 1.7 slice.196
  110.4 0.5 broadcast.160
  110.8 0.6 reduce.12
  111.8 5.0 %all-gather = f32[4,1,2]{2,1,0:T(1,128)S(1)} all-gather(f32[1,1,2]{2,1,0:T(1,128)S(1)} %bitcast.106), channel_id=1, replica_groups=mesh['outer'=4,'inner'=8] {'outer'}, dimensions={0}, use_global_device_ids=true | all-gather | bytes 40 | tf_op jit(solution)/shard_map/all_gather | solution.py:14
  117.0 10.2 %pad.49 = f32[8,2,2,128,128]{4,3,2,1,0:T(8,128)} pad(f32[4,2,2,128,128]{4,3,2,1,0:T(8,128)} %add.155, f32[]{:T(128)} %constant.45.clone.1), padding=1_0_1x0_0_0x0_0_0x0_0_0x0_0_0 | pad | bytes 3145732 | tf_op jit(solution)/shard_map/pad | solution.py:97
  127.2 1.5 fusion.14
  128.7 1.0 pad_maximum_fusion
  129.8 10.2 %pad.48 = f32[8,2,2,128,128]{4,3,2,1,0:T(8,128)} pad(f32[4,2,2,128,128]{4,3,2,1,0:T(8,128)} %pad_maximum_fusion, f32[]{:T(128)} %constant.45.clone.1), padding=0_1_1x0_0_0x0_0_0x0_0_0x0_0_0 | pad | bytes 3145732 | tf_op jit(solution)/shard_map/pad | solution.py:97
  139.9 3.0 %slice_add_fusion = f32[7,2,2,128,128]{4,3,2,1,0:T(8,128)} fusion(f32[8,2,2,128,128]{4,3,2,1,0:T(8,128)S(1)} %copy-done, f32[8,2,2,128,128]{4,3,2,1,0:T(8,128)} %pad.48), kind=kLoop, calls=%fused_computation.10 | loop fusion | flops 458752 | bytes 5505024 | tf_op jit(solution)/shard_map/add | solution.py:97
  142.9 3.3 %while.16 = (s32[]{:T(128)}, f32[2]{0:T(128)S(1)}, f32[2,2,128,128]{3,2,1,0:T(8,128)S(1)}, s32[]{:T(128)}, f32[4,2]{1,0:T(4,128)S(1)}, /*index=5*/f32[4,2,2,128,128]{4,3,2,1,0:T(8,128)}, s32[]{:T(128)}, s32[]{:T(128)}) while((s32[]{:T(128)}, f32[2]{0:T(128)S(1)}, f32[2,2,128,128]{3,2,1,0:T(8,128)S(1)}, s32[]{:T(128)}, ...), condition=%wide.region_4.5_spmd.clone, body=%wide.region_3.4_spmd.clone.sunk | while | flops 262166 | bytes 786608 | solution.py:23
  142.9 1.1 fusion.69
  144.0 1.1 fusion.69
  145.1 1.1 fusion.69
  146.4 0.7 copy.70
  147.1 3.6 %all-to-all-start.3 = ((f32[8,1,2]{2,1,0:T(1,128)}), f32[8,1,2]{2,1,0:T(1,128)S(1)}, u32[]{:S(2)}, u32[]{:S(2)}) async-start(f32[8,1,2]{2,1,0:T(1,128)} %copy.70), calls=%async_computation.3 | async-start | bytes 8192 | tf_op jit(solution)/shard_map/all_to_all | solution.py:113
  150.8 3.2 %multiply_add_fusion = f32[8,2,2,128,128]{4,3,2,1,0:T(8,128)} fusion(f32[7,2,2,128,128]{4,3,2,1,0:T(8,128)} %slice_add_fusion, f32[2,2,128,128]{3,2,1,0:T(8,128)S(1)} %get-tuple-element.116, f32[8,2]{1,0:T(8,128)S(1)} %copy.67), kind=kLoop, calls=%fused_computation.9 | loop fusion | flops 1048576 | bytes 4194368 | tf_op jit(solution)/shard_map/add | solution.py:37
  154.0 3.2 %all-to-all-done.3 = f32[8,1,2]{2,1,0:T(1,128)S(1)} async-done(((f32[8,1,2]{2,1,0:T(1,128)}), f32[8,1,2]{2,1,0:T(1,128)S(1)}, u32[]{:S(2)}, u32[]{:S(2)}) %all-to-all-start.3) | async-done | bytes 96 | tf_op jit(solution)/shard_map/all_to_all | solution.py:113
  157.2 4.6 %all-to-all-start.2 = ((f32[8,2,2,128,128]{4,3,2,1,0:T(8,128)}), f32[8,2,2,128,128]{4,3,2,1,0:T(8,128)}, u32[]{:S(2)}, u32[]{:S(2)}) async-start(f32[8,2,2,128,128]{4,3,2,1,0:T(8,128)} %multiply_add_fusion), calls=%async_computation.2 | async-start | bytes 4194304 | tf_op jit(solution)/shard_map/all_to_all | solution.py:114
  161.7 0.2 copy.54
  162.1 0.3 copy-done.9
  162.5 1.9 convolution_multiply_fusion.6
  164.3 0.6 reduce.13
  165.0 44.1 %all-to-all-done.2 = f32[8,2,2,128,128]{4,3,2,1,0:T(8,128)} async-done(((f32[8,2,2,128,128]{4,3,2,1,0:T(8,128)}), f32[8,2,2,128,128]{4,3,2,1,0:T(8,128)}, u32[]{:S(2)}, u32[]{:S(2)}) %all-to-all-start.2) | async-done | bytes 2097184 | tf_op jit(solution)/shard_map/all_to_all | solution.py:114
  209.1 1.7 copy.68
  210.8 1.2 convolution_multiply_fusion.7
  212.0 2.4 %multiply_reduce_fusion.3 = (f32[16,128]{1,0:T(8,128)S(1)}, f32[16,128]{1,0:T(8,128)S(1)}, f32[16,128,128]{1,2,0:T(8,128)S(1)}) fusion(f32[16,128]{1,0:T(8,128)S(1)} %add_rsqrt_fusion.1, f32[128,2048]{0,1:T(8,128)S(1)} %copy.54, f32[16,128,128]{1,2,0:T(8,128)S(1)} %bitcast.88, f32[16]{0:T(128)S(1)} %copy-done.8, ...), kind=kOutput, calls=%fused_computation.43 | convolution fusion | flops 405270528 | bytes 6324288 | tf_op jit(solution)/shard_map/hts,hse->hte/dot_general | solution.py:64
  214.5 0.2 multiply_reduce_fusion.2
  214.8 0.2 multiply_add_fusion.3
  214.9 1.9 convolution_multiply_fusion.4
  216.9 1.1 convolution_multiply_fusion.5
  218.0 2.4 multiply_reduce_fusion.1
  220.4 0.2 multiply_reduce_fusion
  220.7 0.5 multiply_add_fusion.2
  221.1 2.1 convolution_multiply_fusion.2
  223.3 1.1 convolution_multiply_fusion.3
  224.4 2.4 fusion.11
  226.8 0.5 multiply_add_fusion.1
  227.3 1.9 convolution_multiply_fusion
  229.2 1.1 convolution_multiply_fusion.1
  230.4 1.2 convolution_add_fusion
  231.6 1.3 copy.82
  (75 shorter events, 3.1 us)
Async XLA Ops:
  6.5 12.6 %copy-start.7 = (bf16[128,2048]{1,0:T(8,128)(2,1)S(1)}, bf16[128,2048]{1,0:T(8,128)(2,1)}, u32[]{:S(2)}) copy-start(bf16[128,2048]{1,0:T(8,128)(2,1)} %param.9) | copy-start | bytes 1572868
  9.2 16.5 %all-to-all-start.1 = ((f32[1,8,2]{2,0,1:T(1,128)}), f32[1,8,2]{2,0,1:T(1,128)S(1)}, u32[]{:S(2)}, u32[]{:S(2)}) async-start(f32[1,8,2]{2,0,1:T(1,128)} %broadcast_in_dim.12), calls=%async_computation.1 | async-start | bytes 8192 | tf_op jit(solution)/shard_map/all_to_all | solution.py:94
  19.4 4.6 %copy-start.2 = (bf16[128,2048]{0,1:T(8,128)(2,1)}, bf16[128,2048]{0,1:T(8,128)(2,1)S(1)}, u32[]{:S(2)}) copy-start(bf16[128,2048]{0,1:T(8,128)(2,1)S(1)} %copy.98) | copy-start | bytes 1572868
  25.7 53.7 %all-to-all-start = ((f32[1,16,2,128,128]{4,3,2,0,1:T(8,128)}), f32[1,16,2,128,128]{4,3,2,0,1:T(8,128)S(1)}, u32[]{:S(2)}, u32[]{:S(2)}) async-start(f32[1,16,2,128,128]{4,3,2,0,1:T(8,128)} %copy.59), calls=%async_computation | async-start | bytes 4194304 | tf_op jit(solution)/shard_map/all_to_all | solution.py:95
  31.7 111.2 %all-gather.3.cloned.1.call-start = ((), (), s32[]{:S(2)}) async-start(), calls=%async_computation.4 | async-start | bytes 1310720 | tf_op jit(solution)/shard_map/all_gather | solution.py:14
  79.6 1.0 copy-start.1
  80.8 0.7 copy-start.4
  80.8 0.8 copy-start.5
  129.7 10.2 %copy-start = (f32[8,2,2,128,128]{4,3,2,1,0:T(8,128)S(1)}, f32[8,2,2,128,128]{4,3,2,1,0:T(8,128)}, u32[]{:S(2)}) copy-start(f32[8,2,2,128,128]{4,3,2,1,0:T(8,128)} %pad.49) | copy-start | bytes 6291460
  147.1 10.0 %all-to-all-start.3 = ((f32[8,1,2]{2,1,0:T(1,128)}), f32[8,1,2]{2,1,0:T(1,128)S(1)}, u32[]{:S(2)}, u32[]{:S(2)}) async-start(f32[8,1,2]{2,1,0:T(1,128)} %copy.70), calls=%async_computation.3 | async-start | bytes 8192 | tf_op jit(solution)/shard_map/all_to_all | solution.py:113
  154.0 7.7 %copy-start.6 = (bf16[128,2048]{1,0:T(8,128)(2,1)S(1)}, bf16[128,2048]{1,0:T(8,128)(2,1)}, u32[]{:S(2)}) copy-start(bf16[128,2048]{1,0:T(8,128)(2,1)} %param.7) | copy-start | bytes 1572868
  157.2 51.9 %all-to-all-start.2 = ((f32[8,2,2,128,128]{4,3,2,1,0:T(8,128)}), f32[8,2,2,128,128]{4,3,2,1,0:T(8,128)}, u32[]{:S(2)}, u32[]{:S(2)}) async-start(f32[8,2,2,128,128]{4,3,2,1,0:T(8,128)} %multiply_add_fusion), calls=%async_computation.2 | async-start | bytes 4194304 | tf_op jit(solution)/shard_map/all_to_all | solution.py:114
  161.7 0.7 copy-start.9
  210.8 1.2 copy-start.8
  229.2 1.1 copy-start.3
Sparse Core Ops, SparseCore 0:
  110.4 15.8 all-gather.2
where the time goes:
time: 243 us; the launch traced here: 240 us
  waiting for transfers between devices  93.4 us (38%)
  local copies, waits for them, and re-layouts  56.6 us (23%)
  matrix products  25.3 us (10%)
  other arithmetic  23.4 us (10%)
  starting transfers between devices  21.5 us (9%)
  between operations  14.6 us (6%)
  blocking collectives  5.04 us (2%)
    all_to_all x1, waiting for transfers between devices, on_device(): lax.all_to_all(own_state, 'inner', split_axis=1, concat_axis=0, tiled=True)  46.1 us
    all_to_all x1, waiting for transfers between devices, on_device(): lax.all_to_all(full_state, 'inner', split_axis=0, concat_axis=1, tiled=True)  44.1 us
    pad x8, local copies, waits for them, and re-layouts, on_device(): lax.associative_scan(combine_stacked, (shard_last, shard_state), axis=0)  32.1 us
    unnamed x21, local copies, waits for them, and re-layouts  12.2 us
    all_to_all x1, starting transfers between devices, on_device(): lax.all_to_all(own_last, 'inner', split_axis=1, concat_axis=0, tiled=True)  7.25 us
    dot_general x3, matrix products, span_solve(): jnp.einsum('hts,hse->hte', apply_scores, key_rows, precision=highest)  7.19 us
    add x6, other arithmetic, on_device(): lax.associative_scan(combine_stacked, (shard_last, shard_state), axis=0)  6.53 us
    all_to_all x1, starting transfers between devices, on_device(): lax.all_to_all(own_state, 'inner', split_axis=1, concat_axis=0, tiled=True)  6 us
  transfers between devices with their start and end apart: 5, of which 3 were waited for; matrix products, arithmetic and copies ran while one was open for 18% of the time, Pallas kernels for 0%

commit v1 on v0

v1 whole, which is shorter than its diff:
```python
import functools

import jax
import jax.numpy as jnp
from jax import lax
from jax.experimental import pallas as pl
from jax.experimental.pallas import tpu as pltpu
from jax.sharding import Mesh
from jax.sharding import PartitionSpec as P

CG_ITERS = 3
DOC_SHARE = 4
EXTRA = 8


def split(x):
    high = x.astype(jnp.bfloat16)
    low = (x - high.astype(jnp.float32)).astype(jnp.bfloat16)
    return high, low


def dot(a, b):
    return lax.dot_general(a, b, (((1,), (0,)), ((), ())), preferred_element_type=jnp.float32)


def dot_rows(a, b):
    return lax.dot_general(a, b, (((0,), (0,)), ((), ())), preferred_element_type=jnp.float32)


def grid_ids(width):
    row = lax.broadcasted_iota(jnp.int32, (width, width), 0)
    col = lax.broadcasted_iota(jnp.int32, (width, width), 1)
    return row, col


def own_kernel(base, width, pairs, me_ref, k_ref, v_ref, weight_ref, ids_ref, *outs):
    row, col = grid_ids(width)
    upper, diagonal = row <= col, row == col
    weight = weight_ref[...]
    for slot, out in enumerate(outs):
        part = me_ref[0] ^ slot
        for pair in range(pairs):
            top = pair * (3 * width + EXTRA)
            grams = []
            for side in range(2):
                head = base + (part * pairs + pair) * 2 + side
                lanes = pl.ds(pl.multiple_of(head * width, width), width)
                keys = k_ref[:, lanes]
                wide = keys.astype(jnp.float32)
                scale = lax.rsqrt(jnp.sum(wide * wide, -1, keepdims=True) + 1e-06)
                light = weight * scale
                k_high, k_low = split(light * scale * wide)
                v_high, v_low = split(light * v_ref[:, lanes].astype(jnp.float32))
                right = jnp.concatenate(
                    [jnp.concatenate([k_high, v_high], 1), jnp.concatenate([k_low, v_low], 1)], 0
                )
                both = dot_rows(jnp.concatenate([keys, keys], 0), right)
                grams.append(both[:, :width])
                out[pl.ds(top + (1 + side) * width, width), :] = both[:, width:]
            out[pl.ds(top, width), :] = jnp.where(upper, grams[0], grams[1])
            second = jnp.sum(jnp.where(diagonal, grams[1], 0.0), 0, keepdims=True)
            out[pl.ds(top + 3 * width, EXTRA), :] = jnp.concatenate(
                [second, ids_ref[...], jnp.zeros((EXTRA - 3, width), jnp.float32)], 0
            )


def total_kernel(width, pairs, *refs):
    slots, out = refs[:-1], refs[-1]
    first_row = 3 * width + 1
    last = [slot[pl.ds(first_row + 1, 1), :] for slot in slots]
    newest = functools.reduce(jnp.maximum, last)
    keep = [(one == newest).astype(jnp.float32) for one in last]
    out[...] = functools.reduce(lambda a, b: a + b, [slot[...] * k for slot, k in zip(slots, keep)])
    for pair in range(pairs):
        out[pl.ds(pair * (3 * width + EXTRA) + first_row, 2), :] = jnp.concatenate([newest, newest], 0)


def prefix_kernel(width, slot_count, me_ref, *refs):
    slots, carries, outs = refs[:slot_count], refs[slot_count:-slot_count], refs[-slot_count:]
    first_row = 3 * width + 1
    first = [slot[pl.ds(first_row, 1), :] for slot in slots]
    last = [slot[pl.ds(first_row + 1, 1), :] for slot in slots]
    oldest = functools.reduce(jnp.minimum, first)
    carry = None
    for one in carries:
        term = one[...] * (one[pl.ds(first_row + 1, 1), :] == oldest).astype(jnp.float32)
        carry = term if carry is None else carry + term
    me = me_ref[0]
    for target, out in enumerate(outs):
        total = carry * (first[target] == oldest).astype(jnp.float32)
        for source in range(slot_count):
            if source != target:
                before = jnp.where((me ^ source) < (me ^ target), 1.0, 0.0)
                total = total + slots[source][...] * ((last[source] == first[target]).astype(jnp.float32) * before)
        out[...] = total


def solve_heads(heads, within, carried):
    prepared = []
    for queries, keys, values, gram, cross, ridge in heads:
        wide = queries.astype(jnp.float32)
        query = wide * lax.rsqrt(jnp.sum(wide * wide, -1, keepdims=True) + 1e-06)
        turned = keys.astype(jnp.float32).T
        scale = lax.rsqrt(jnp.sum(turned * turned, 0, keepdims=True) + 1e-06)
        turned = turned.astype(jnp.bfloat16)
        g_high, g_low = split(gram)
        c_high, c_low = split(cross)
        state = jnp.concatenate([g_high, turned], 1)
        final = jnp.concatenate([c_high, turned], 1)
        prepared.append(
            dict(
                state=jnp.concatenate([state, state], 0),
                state_low=g_low,
                final=jnp.concatenate([final, final], 0),
                final_low=c_low,
                keys=jnp.concatenate([keys, keys], 0),
                values=jnp.concatenate([values, values], 0),
                once=within * scale,
                twice=within * (scale * scale),
                ridge=ridge,
                solved=None,
                remain=query,
                search=query,
                square=jnp.sum(query * query, -1, keepdims=True),
            )
        )
    width = heads[0][3].shape[0]

    def product(vector, both, low, mask, rows):
        high_part, low_part = split(vector)
        wide = dot(jnp.concatenate([high_part, low_part], 1), both)
        from_state = (wide[:, :width] + dot(high_part, low)) * carried
        high_score, low_score = split(wide[:, width:] * mask)
        return from_state + dot(jnp.concatenate([high_score, low_score], 1), rows)

    for step in range(CG_ITERS):
        for h in prepared:
            search = h["search"]
            applied = product(search, h["state"], h["state_low"], h["twice"], h["keys"]) + h["ridge"] * search
            size = h["square"] / jnp.sum(search * applied, -1, keepdims=True)
            h["solved"] = size * search if step == 0 else h["solved"] + size * search
            if step < CG_ITERS - 1:
                remain = h["remain"] - size * applied
                square = jnp.sum(remain * remain, -1, keepdims=True)
                h["search"] = remain + square / h["square"] * search
                h["remain"], h["square"] = remain, square
    return [product(h["solved"], h["final"], h["final_low"], h["once"], h["values"]) for h in prepared]


def solve_kernel(base, width, pairs, slot_count, me_ref, ridge_ref, q_ref, k_ref, v_ref, within_ref, carried_ref, *refs):
    slots, out = refs[:slot_count], refs[-1]
    row, col = grid_ids(width)
    upper, diagonal = row <= col, row == col
    within, carried = within_ref[...], carried_ref[...]
    for slot, state in enumerate(slots):
        part = me_ref[0] ^ slot
        for pair in range(pairs):
            top = pair * (3 * width + EXTRA)
            packed = state[pl.ds(top, width), :]
            turned = packed.T
            second = state[pl.ds(top + 3 * width, 1), :]
            grams = [
                jnp.where(upper, packed, turned),
                jnp.where(diagonal, second, jnp.where(upper, turned, packed)),
            ]
            heads = []
            for side in range(2):
                local = (part * pairs + pair) * 2 + side
                lanes = pl.ds(pl.multiple_of((base + local) * width, width), width)
                cross = state[pl.ds(top + (1 + side) * width, width), :]
                heads.append((q_ref[:, lanes], k_ref[:, lanes], v_ref[:, lanes], grams[side], cross, ridge_ref[base + local]))
            for side, result in enumerate(solve_heads(heads, within, carried)):
                local = (part * pairs + pair) * 2 + side
                out[:, pl.ds(pl.multiple_of(local * width, width), width)] = result


VMEM = pl.BlockSpec(memory_space=pltpu.VMEM)
SMEM = pl.BlockSpec(memory_space=pltpu.SMEM)
PARAMS = pltpu.CompilerParams(vmem_limit_bytes=48 * 1024 * 1024)


def on_device(queries, key_vectors, value_vectors, segment_ids, ridge_weight, *, pieces):
    row_count, columns = queries.shape
    head_count = ridge_weight.shape[0]
    width = columns // head_count
    outer, half, near = lax.axis_size("outer"), lax.axis_size("half"), lax.axis_size("near")
    blocks = outer * half
    pairs = head_count // (2 * pieces * near)
    rows = pairs * (3 * width + EXTRA)
    back = -(-(row_count * near * blocks // DOC_SHARE - 1) // (row_count * near))

    me = lax.axis_index("near").astype(jnp.int32).reshape(1)
    segment = segment_ids.astype(jnp.float32)
    weight = (segment == segment[-1]).astype(jnp.float32)[:, None]
    carried = (segment == segment[0]).astype(jnp.float32)[:, None]
    ids = jnp.broadcast_to(jnp.stack([segment[0], segment[-1]])[:, None] + 1.0, (2, width))
    position = jnp.arange(row_count)
    within = jnp.logical_and(
        position[:, None] >= position[None, :], segment[:, None] == segment[None, :]
    ).astype(jnp.float32)

    def exchange(slots):
        return [slots[0]] + [
            lax.ppermute(slots[j], "near", [(i, i ^ j) for i in range(near)]) for j in range(1, near)
        ]

    shape = jax.ShapeDtypeStruct((rows, width), jnp.float32)
    prefixes = []
    for piece in range(pieces):
        base = piece * pairs * near * 2
        own = pl.pallas_call(
            functools.partial(own_kernel, base, width, pairs),
            out_shape=[shape] * near,
            in_specs=[SMEM, VMEM, VMEM, VMEM, VMEM],
            out_specs=[VMEM] * near,
            compiler_params=PARAMS,
            name="own_sums",
        )(me, key_vectors, value_vectors, weight, ids)
        slots = exchange(own)
        total = pl.pallas_call(
            functools.partial(total_kernel, width, pairs),
            out_shape=shape,
            in_specs=[VMEM] * near,
            out_specs=VMEM,
            compiler_params=PARAMS,
            name="block_total",
        )(*slots)
        carries = [
            lax.ppermute(total, ("outer", "half"), [(i, i + step) for i in range(blocks - step)])
            for step in range(1, min(back, blocks - 1) + 1)
        ]
        prefix = pl.pallas_call(
            functools.partial(prefix_kernel, width, near),
            out_shape=[shape] * near,
            in_specs=[SMEM] + [VMEM] * (near + len(carries)),
            out_specs=[VMEM] * near,
            compiler_params=PARAMS,
            name="prefixes",
        )(me, *slots, *carries)
        prefixes.append(exchange(prefix))
    out = None
    for piece in range(pieces):
        base = piece * pairs * near * 2
        span = pairs * near * 2 * width
        arguments = [me, ridge_weight, queries, key_vectors, value_vectors, within, carried, *prefixes[piece]]
        in_specs = [SMEM, SMEM, VMEM, VMEM, VMEM, VMEM, VMEM] + [VMEM] * near
        aliases = {}
        if out is not None:
            aliases = {len(arguments): 0}
            arguments.append(out)
            in_specs.append(pl.BlockSpec(memory_space=pl.ANY))
        out = pl.pallas_call(
            functools.partial(solve_kernel, base, width, pairs, near),
            grid=(1,),
            out_shape=jax.ShapeDtypeStruct((row_count, columns), jnp.float32),
            in_specs=in_specs,
            out_specs=pl.BlockSpec((row_count, span), functools.partial(lambda p, i: (0, p), piece)),
            input_output_aliases=aliases,
            compiler_params=PARAMS,
            name="solve",
        )(*arguments)
    return out


def solution(mesh):
    outer, inner = mesh.shape["outer"], mesh.shape["inner"]
    near = inner // 2
    finer = Mesh(mesh.devices.reshape(outer, 2, near), ("outer", "half", "near"))
    tokens = ("outer", "half", "near")

    def run(queries, key_vectors, value_vectors, segment_ids, ridge_weight):
        pieces = max(1, min(2, ridge_weight.shape[0] // (2 * near)))
        return jax.shard_map(
            functools.partial(on_device, pieces=pieces),
            mesh=finer,
            in_specs=(P(tokens, None), P(tokens, None), P(tokens, None), P(tokens), P()),
            out_specs=P(tokens, None),
            check_vma=False,
        )(queries, key_vectors, value_vectors, segment_ids, ridge_weight)

    return run
```

time: 243 us -> 79.6 us (0.33)
  the two profiles are of different devices: /device:TPU:0 before, /device:TPU:1 now
where the time goes in v1:
time: 79.6 us; the launch traced here: 79.3 us
  starting transfers between devices  32.7 us (41%)
  waiting for transfers between devices  23.3 us (29%)
  Pallas kernels  16.8 us (21%)
  local copies, waits for them, and re-layouts  3.64 us (5%)
  other arithmetic  2.71 us (3%)
    ppermute x4, starting transfers between devices, on_device(): lax.ppermute(total, ('outer', 'half'), [(i, i + step) for i in range(bloc...  20.3 us
    ppermute x12, waiting for transfers between devices, exchange(): lax.ppermute(slots[j], 'near', [(i, i ^ j) for i in range(near)])  18.5 us
    pallas_call x2, Pallas kernels, on_device(): pl.pallas_call(functools.partial(solve_kernel, base, width, pairs, near),...  14.5 us
    ppermute x12, starting transfers between devices, exchange(): lax.ppermute(slots[j], 'near', [(i, i ^ j) for i in range(near)])  12.4 us
    ppermute x4, waiting for transfers between devices, on_device(): lax.ppermute(total, ('outer', 'half'), [(i, i + step) for i in range(bloc...  4.85 us
    unnamed x14, local copies, waits for them, and re-layouts  2.76 us
  transfers between devices with their start and end apart: 16, of which 4 were waited for; matrix products, arithmetic and copies ran while one was open for 0% of the time, Pallas kernels for 11%

profile of v1, /device:TPU:1, one launch (start us, length us, event | category | flops | bytes accessed | tf_op | source)
XLA Modules:
  0.0 79.3 jit_solution(15938362992507439914)
XLA Ops:
  0.0 0.0 copy-start.6
  0.0 0.7 copy-done.6
  0.7 0.6 fusion.4
  1.2 1.4 %maximum_add_fusion = f32[2]{0:T(128)S(1)} fusion(f32[1]{0:T(128)} %get-tuple-element.39, f32[1]{0:T(128)} %get-tuple-element.40), kind=kLoop, calls=%fused_computation.7 | loop fusion | flops 4 | bytes 16 | tf_op jit(solution)/shard_map/add | solution.py:196
  2.6 1.3 %fusion.3 = (f32[128,1]{0,1:T(1,128)S(1)}, f32[128,1]{0,1:T(1,128)S(1)}) fusion(f32[]{:T(128)} %bitcast.3, s32[128]{0:T(128)S(1)} %copy-done.6, f32[]{:T(128)} %bitcast.1), kind=kLoop, calls=%fused_computation.6 | loop fusion | flops 640 | bytes 1544 | tf_op jit(solution)/shard_map/broadcast_in_dim | solution.py:194
  3.9 0.1 copy.7.weight_ref
  4.0 0.1 broadcast_in_dim.24.ids_ref
  4.1 0.0 copy-start
  4.1 1.0 %copy-done = bf16[128,2048]{1,0:T(8,128)(2,1)S(1)} copy-done((bf16[128,2048]{1,0:T(8,128)(2,1)S(1)}, bf16[128,2048]{1,0:T(8,128)(2,1)}, u32[]{:S(2)}) %copy-start) | copy-done | bytes 524312
  5.1 0.0 copy-start.2
  5.1 1.0 %copy-done.2 = bf16[128,2048]{1,0:T(8,128)(2,1)S(1)} copy-done((bf16[128,2048]{1,0:T(8,128)(2,1)S(1)}, bf16[128,2048]{1,0:T(8,128)(2,1)}, u32[]{:S(2)}) %copy-start.2) | copy-done | bytes 524312
  6.2 0.8 own_sums.3
  6.9 2.1 %collective-permute-start.8 = (f32[392,128]{1,0:T(8,128)S(1)}, f32[392,128]{1,0:T(8,128)S(1)}, u32[]{:S(2)}, u32[]{:S(2)}) collective-permute-start(f32[392,128]{1,0:T(8,128)S(1)} %get-tuple-element.30), channel_id=1, source_target_pairs={{0,1},{1,0},{2,3},{3,2},{4,5},{5,4},{6,7},{7,6},{8,9},{9,8},{10,11... | collective-permute-start | bytes 602120 | tf_op jit(solution)/shard_map/ppermute | solution.py:204
  9.0 1.3 %collective-permute-start.9 = (f32[392,128]{1,0:T(8,128)S(1)}, f32[392,128]{1,0:T(8,128)S(1)}, u32[]{:S(2)}, u32[]{:S(2)}) collective-permute-start(f32[392,128]{1,0:T(8,128)S(1)} %get-tuple-element.31), channel_id=1, source_target_pairs={{0,2},{1,3},{2,0},{3,1},{4,6},{5,7},{6,4},{7,5},{8,10},{9,11},{10,... | collective-permute-start | bytes 602120 | tf_op jit(solution)/shard_map/ppermute | solution.py:204
  10.3 0.0 collective-permute-start.10
  10.3 0.8 own_sums.2
  11.1 1.4 %collective-permute-start = (f32[392,128]{1,0:T(8,128)S(1)}, f32[392,128]{1,0:T(8,128)S(1)}, u32[]{:S(2)}, u32[]{:S(2)}) collective-permute-start(f32[392,128]{1,0:T(8,128)S(1)} %get-tuple-element.22), channel_id=1, source_target_pairs={{0,1},{1,0},{2,3},{3,2},{4,5},{5,4},{6,7},{7,6},{8,9},{9,8},{10,11... | collective-permute-start | bytes 602120 | tf_op jit(solution)/shard_map/ppermute | solution.py:204
  12.5 1.3 %collective-permute-start.1 = (f32[392,128]{1,0:T(8,128)S(1)}, f32[392,128]{1,0:T(8,128)S(1)}, u32[]{:S(2)}, u32[]{:S(2)}) collective-permute-start(f32[392,128]{1,0:T(8,128)S(1)} %get-tuple-element.23), channel_id=1, source_target_pairs={{0,2},{1,3},{2,0},{3,1},{4,6},{5,7},{6,4},{7,5},{8,10},{9,11},{10,... | collective-permute-start | bytes 602120 | tf_op jit(solution)/shard_map/ppermute | solution.py:204
  13.8 0.0 collective-permute-done.8.refs_1_
  13.8 2.1 %collective-permute-start.2 = (f32[392,128]{1,0:T(8,128)S(1)}, f32[392,128]{1,0:T(8,128)S(1)}, u32[]{:S(2)}, u32[]{:S(2)}) collective-permute-start(f32[392,128]{1,0:T(8,128)S(1)} %get-tuple-element.24), channel_id=1, source_target_pairs={{0,3},{1,2},{2,1},{3,0},{4,7},{5,6},{6,5},{7,4},{8,11},{9,10},{10,... | collective-permute-start | bytes 602120 | tf_op jit(solution)/shard_map/ppermute | solution.py:204
  15.9 0.0 collective-permute-done.9.refs_2_
  15.9 3.1 %collective-permute-done.10.refs_3_ = f32[392,128]{1,0:T(8,128)S(1)} collective-permute-done((f32[392,128]{1,0:T(8,128)S(1)}, f32[392,128]{1,0:T(8,128)S(1)}, u32[]{:S(2)}, u32[]{:S(2)}) %collective-permute-start.10) | collective-permute-done | bytes 200736 | tf_op jit(solution)/shard_map/ppermute | solution.py:204
  19.0 0.1 block_total.3
  19.1 4.1 %collective-permute-start.11 = (f32[392,128]{1,0:T(8,128)S(1)}, f32[392,128]{1,0:T(8,128)S(1)}, u32[]{:S(2)}, u32[]{:S(2)}) collective-permute-start(f32[392,128]{1,0:T(8,128)S(1)} %block_total.3), channel_id=1, source_target_pairs={{0,4},{4,8},{8,12},{12,16},{16,20},{20,24},{24,28},{1,5},{5,9},{9,... | collective-permute-start | bytes 602120 | tf_op jit(solution)/shard_map/ppermute | solution.py:229
  23.2 6.6 %collective-permute-start.12 = (f32[392,128]{1,0:T(8,128)S(1)}, f32[392,128]{1,0:T(8,128)S(1)}, u32[]{:S(2)}, u32[]{:S(2)}) collective-permute-start(f32[392,128]{1,0:T(8,128)S(1)} %block_total.3), channel_id=1, source_target_pairs={{0,8},{4,12},{8,16},{12,20},{16,24},{20,28},{1,9},{5,13},{9,17},{1... | collective-permute-start | bytes 602120 | tf_op jit(solution)/shard_map/ppermute | solution.py:229
  29.9 0.0 collective-permute-done.refs_1_
  29.9 0.0 collective-permute-done.1.refs_2_
  29.9 0.0 collective-permute-done.2.refs_3_
  29.9 0.1 block_total.2
  30.0 4.0 %collective-permute-start.3 = (f32[392,128]{1,0:T(8,128)S(1)}, f32[392,128]{1,0:T(8,128)S(1)}, u32[]{:S(2)}, u32[]{:S(2)}) collective-permute-start(f32[392,128]{1,0:T(8,128)S(1)} %block_total.2), channel_id=1, source_target_pairs={{0,4},{4,8},{8,12},{12,16},{16,20},{20,24},{24,28},{1,5},{5,9},{9,... | collective-permute-start | bytes 602120 | tf_op jit(solution)/shard_map/ppermute | solution.py:229
  33.9 5.6 %collective-permute-start.4 = (f32[392,128]{1,0:T(8,128)S(1)}, f32[392,128]{1,0:T(8,128)S(1)}, u32[]{:S(2)}, u32[]{:S(2)}) collective-permute-start(f32[392,128]{1,0:T(8,128)S(1)} %block_total.2), channel_id=1, source_target_pairs={{0,8},{4,12},{8,16},{12,20},{16,24},{20,28},{1,9},{5,13},{9,17},{1... | collective-permute-start | bytes 602120 | tf_op jit(solution)/shard_map/ppermute | solution.py:229
  39.5 0.0 collective-permute-done.11.refs_4_
  39.5 0.0 collective-permute-done.12.refs_5_
  39.5 0.0 copy-start.4
  39.6 0.3 prefixes.3
  39.8 0.1 collective-permute-start.13
  39.9 0.1 copy.10.carried_ref
  40.0 0.0 copy-start.1
  40.0 0.0 copy-start.3
  40.0 4.8 %collective-permute-done.3.refs_4_ = f32[392,128]{1,0:T(8,128)S(1)} collective-permute-done((f32[392,128]{1,0:T(8,128)S(1)}, f32[392,128]{1,0:T(8,128)S(1)}, u32[]{:S(2)}, u32[]{:S(2)}) %collective-permute-start.3) | collective-permute-done | bytes 200736 | tf_op jit(solution)/shard_map/ppermute | solution.py:229
  44.9 0.0 collective-permute-done.4.refs_5_
  44.9 0.3 prefixes.2
  45.2 0.1 collective-permute-start.5
  45.3 0.4 collective-permute-start.6
  45.7 2.2 %collective-permute-start.7 = (f32[392,128]{1,0:T(8,128)S(1)}, f32[392,128]{1,0:T(8,128)S(1)}, u32[]{:S(2)}, u32[]{:S(2)}) collective-permute-start(f32[392,128]{1,0:T(8,128)S(1)} %get-tuple-element.28), channel_id=1, source_target_pairs={{0,3},{1,2},{2,1},{3,0},{4,7},{5,6},{6,5},{7,4},{8,11},{9,10},{10,... | collective-permute-start | bytes 602120 | tf_op jit(solution)/shard_map/ppermute | solution.py:204
  47.9 0.0 collective-permute-start.14
  47.9 0.0 collective-permute-done.13.refs_1_
  47.9 1.4 %collective-permute-start.15 = (f32[392,128]{1,0:T(8,128)S(1)}, f32[392,128]{1,0:T(8,128)S(1)}, u32[]{:S(2)}, u32[]{:S(2)}) collective-permute-start(f32[392,128]{1,0:T(8,128)S(1)} %get-tuple-element.36), channel_id=1, source_target_pairs={{0,3},{1,2},{2,1},{3,0},{4,7},{5,6},{6,5},{7,4},{8,11},{9,10},{10,... | collective-permute-start | bytes 602120 | tf_op jit(solution)/shard_map/ppermute | solution.py:204
  49.3 0.1 fusion.1.within_ref
  49.4 0.0 copy-start.5
  49.4 11.5 %collective-permute-done.14.refs_2_ = f32[392,128]{1,0:T(8,128)S(1)} collective-permute-done((f32[392,128]{1,0:T(8,128)S(1)}, f32[392,128]{1,0:T(8,128)S(1)}, u32[]{:S(2)}, u32[]{:S(2)}) %collective-permute-start.14) | collective-permute-done | bytes 200736 | tf_op jit(solution)/shard_map/ppermute | solution.py:204
  61.0 3.8 %collective-permute-done.15.refs_3_ = f32[392,128]{1,0:T(8,128)S(1)} collective-permute-done((f32[392,128]{1,0:T(8,128)S(1)}, f32[392,128]{1,0:T(8,128)S(1)}, u32[]{:S(2)}, u32[]{:S(2)}) %collective-permute-start.15) | collective-permute-done | bytes 200736 | tf_op jit(solution)/shard_map/ppermute | solution.py:204
  64.7 0.0 copy-done.4
  64.7 0.0 copy-done.1
  64.7 0.0 copy-done.3
  64.7 0.0 copy-done.5
  64.8 7.3 %solve.2.refs_4_ = f32[128,2048]{1,0:T(8,128)} custom-call(s32[1]{0:T(128)} %bitcast.me_ref, f32[16]{0:T(128)S(1)} %copy-done.5, bf16[128,2048]{1,0:T(8,128)(2,1)S(1)} %copy-done.4, bf16[128,2048]{1,0:T(8,128)(2,1)S(1)} %copy-done.1, bf16[128,2048]{1,0:T(8,128)(2,1)S(1)} %copy-done.3, f32[128,128]{1,0:T(8,128)S(1)} %fusion.1.within_ref, ...), custom_call_target="tpu_custom_call" | custom-call | tf_op jit(solution)/shard_map/solve/pallas_call | solution.py:252
  72.0 0.0 collective-permute-done.5.refs_1_
  72.0 0.0 collective-permute-done.6.refs_2_
  72.0 0.0 collective-permute-done.7.refs_3_
  72.0 7.3 %solve.3 = f32[128,2048]{1,0:T(8,128)} custom-call(s32[1]{0:T(128)} %bitcast.me_ref, f32[16]{0:T(128)S(1)} %copy-done.5, bf16[128,2048]{1,0:T(8,128)(2,1)S(1)} %copy-done.4, bf16[128,2048]{1,0:T(8,128)(2,1)S(1)} %copy-done.1, bf16[128,2048]{1,0:T(8,128)(2,1)S(1)} %copy-done.3, f32[128,128]{1,0:T(8,128)S(1)} %fusion.1.within_ref, ...), custom_call_target="tpu_custom_call", output_to_operand_aliasing={{}: (11, {})} | custom-call | tf_op jit(solution)/shard_map/solve/pallas_call | solution.py:252
  (1 shorter events, 0.0 us)
Async XLA Ops:
  0.0 0.7 copy-start.6
  4.1 1.0 %copy-start = (bf16[128,2048]{1,0:T(8,128)(2,1)S(1)}, bf16[128,2048]{1,0:T(8,128)(2,1)}, u32[]{:S(2)}) copy-start(bf16[128,2048]{1,0:T(8,128)(2,1)} %k_ref.7) | copy-start | bytes 1572868
  5.1 1.0 %copy-start.2 = (bf16[128,2048]{1,0:T(8,128)(2,1)S(1)}, bf16[128,2048]{1,0:T(8,128)(2,1)}, u32[]{:S(2)}) copy-start(bf16[128,2048]{1,0:T(8,128)(2,1)} %v_ref.7) | copy-start | bytes 1572868
  6.9 6.9 %collective-permute-start.8 = (f32[392,128]{1,0:T(8,128)S(1)}, f32[392,128]{1,0:T(8,128)S(1)}, u32[]{:S(2)}, u32[]{:S(2)}) collective-permute-start(f32[392,128]{1,0:T(8,128)S(1)} %get-tuple-element.30), channel_id=1, source_target_pairs={{0,1},{1,0},{2,3},{3,2},{4,5},{5,4},{6,7},{7,6},{8,9},{9,8},{10,11... | collective-permute-start | bytes 602120 | tf_op jit(solution)/shard_map/ppermute | solution.py:204
  9.0 6.9 %collective-permute-start.9 = (f32[392,128]{1,0:T(8,128)S(1)}, f32[392,128]{1,0:T(8,128)S(1)}, u32[]{:S(2)}, u32[]{:S(2)}) collective-permute-start(f32[392,128]{1,0:T(8,128)S(1)} %get-tuple-element.31), channel_id=1, source_target_pairs={{0,2},{1,3},{2,0},{3,1},{4,6},{5,7},{6,4},{7,5},{8,10},{9,11},{10,... | collective-permute-start | bytes 602120 | tf_op jit(solution)/shard_map/ppermute | solution.py:204
  10.3 8.7 %collective-permute-start.10 = (f32[392,128]{1,0:T(8,128)S(1)}, f32[392,128]{1,0:T(8,128)S(1)}, u32[]{:S(2)}, u32[]{:S(2)}) collective-permute-start(f32[392,128]{1,0:T(8,128)S(1)} %get-tuple-element.32), channel_id=1, source_target_pairs={{0,3},{1,2},{2,1},{3,0},{4,7},{5,6},{6,5},{7,4},{8,11},{9,10},{10,... | collective-permute-start | bytes 602120 | tf_op jit(solution)/shard_map/ppermute | solution.py:204
  11.1 18.7 %collective-permute-start = (f32[392,128]{1,0:T(8,128)S(1)}, f32[392,128]{1,0:T(8,128)S(1)}, u32[]{:S(2)}, u32[]{:S(2)}) collective-permute-start(f32[392,128]{1,0:T(8,128)S(1)} %get-tuple-element.22), channel_id=1, source_target_pairs={{0,1},{1,0},{2,3},{3,2},{4,5},{5,4},{6,7},{7,6},{8,9},{9,8},{10,11... | collective-permute-start | bytes 602120 | tf_op jit(solution)/shard_map/ppermute | solution.py:204
  12.5 17.3 %collective-permute-start.1 = (f32[392,128]{1,0:T(8,128)S(1)}, f32[392,128]{1,0:T(8,128)S(1)}, u32[]{:S(2)}, u32[]{:S(2)}) collective-permute-start(f32[392,128]{1,0:T(8,128)S(1)} %get-tuple-element.23), channel_id=1, source_target_pairs={{0,2},{1,3},{2,0},{3,1},{4,6},{5,7},{6,4},{7,5},{8,10},{9,11},{10,... | collective-permute-start | bytes 602120 | tf_op jit(solution)/shard_map/ppermute | solution.py:204
  13.8 16.1 %collective-permute-start.2 = (f32[392,128]{1,0:T(8,128)S(1)}, f32[392,128]{1,0:T(8,128)S(1)}, u32[]{:S(2)}, u32[]{:S(2)}) collective-permute-start(f32[392,128]{1,0:T(8,128)S(1)} %get-tuple-element.24), channel_id=1, source_target_pairs={{0,3},{1,2},{2,1},{3,0},{4,7},{5,6},{6,5},{7,4},{8,11},{9,10},{10,... | collective-permute-start | bytes 602120 | tf_op jit(solution)/shard_map/ppermute | solution.py:204
  19.1 20.4 %collective-permute-start.11 = (f32[392,128]{1,0:T(8,128)S(1)}, f32[392,128]{1,0:T(8,128)S(1)}, u32[]{:S(2)}, u32[]{:S(2)}) collective-permute-start(f32[392,128]{1,0:T(8,128)S(1)} %block_total.3), channel_id=1, source_target_pairs={{0,4},{4,8},{8,12},{12,16},{16,20},{20,24},{24,28},{1,5},{5,9},{9,... | collective-permute-start | bytes 602120 | tf_op jit(solution)/shard_map/ppermute | solution.py:229
  23.2 16.3 %collective-permute-start.12 = (f32[392,128]{1,0:T(8,128)S(1)}, f32[392,128]{1,0:T(8,128)S(1)}, u32[]{:S(2)}, u32[]{:S(2)}) collective-permute-start(f32[392,128]{1,0:T(8,128)S(1)} %block_total.3), channel_id=1, source_target_pairs={{0,8},{4,12},{8,16},{12,20},{16,24},{20,28},{1,9},{5,13},{9,17},{1... | collective-permute-start | bytes 602120 | tf_op jit(solution)/shard_map/ppermute | solution.py:229
  30.0 14.9 %collective-permute-start.3 = (f32[392,128]{1,0:T(8,128)S(1)}, f32[392,128]{1,0:T(8,128)S(1)}, u32[]{:S(2)}, u32[]{:S(2)}) collective-permute-start(f32[392,128]{1,0:T(8,128)S(1)} %block_total.2), channel_id=1, source_target_pairs={{0,4},{4,8},{8,12},{12,16},{16,20},{20,24},{24,28},{1,5},{5,9},{9,... | collective-permute-start | bytes 602120 | tf_op jit(solution)/shard_map/ppermute | solution.py:229
  33.9 11.0 %collective-permute-start.4 = (f32[392,128]{1,0:T(8,128)S(1)}, f32[392,128]{1,0:T(8,128)S(1)}, u32[]{:S(2)}, u32[]{:S(2)}) collective-permute-start(f32[392,128]{1,0:T(8,128)S(1)} %block_total.2), channel_id=1, source_target_pairs={{0,8},{4,12},{8,16},{12,20},{16,24},{20,28},{1,9},{5,13},{9,17},{1... | collective-permute-start | bytes 602120 | tf_op jit(solution)/shard_map/ppermute | solution.py:229
  39.5 25.2 %copy-start.4 = (bf16[128,2048]{1,0:T(8,128)(2,1)S(1)}, bf16[128,2048]{1,0:T(8,128)(2,1)}, u32[]{:S(2)}) copy-start(bf16[128,2048]{1,0:T(8,128)(2,1)} %q_ref.3) | copy-start | bytes 1572868
  39.8 8.1 %collective-permute-start.13 = (f32[392,128]{1,0:T(8,128)S(1)}, f32[392,128]{1,0:T(8,128)S(1)}, u32[]{:S(2)}, u32[]{:S(2)}) collective-permute-start(f32[392,128]{1,0:T(8,128)S(1)} %get-tuple-element.34), channel_id=1, source_target_pairs={{0,1},{1,0},{2,3},{3,2},{4,5},{5,4},{6,7},{7,6},{8,9},{9,8},{10,11... | collective-permute-start | bytes 602120 | tf_op jit(solution)/shard_map/ppermute | solution.py:204
  40.0 24.7 %copy-start.1 = (bf16[128,2048]{1,0:T(8,128)(2,1)S(1)}, bf16[128,2048]{1,0:T(8,128)(2,1)}, u32[]{:S(2)}) copy-start(bf16[128,2048]{1,0:T(8,128)(2,1)} %k_ref.7) | copy-start | bytes 1572868
  40.0 24.7 %copy-start.3 = (bf16[128,2048]{1,0:T(8,128)(2,1)S(1)}, bf16[128,2048]{1,0:T(8,128)(2,1)}, u32[]{:S(2)}) copy-start(bf16[128,2048]{1,0:T(8,128)(2,1)} %v_ref.7) | copy-start | bytes 1572868
  45.2 26.8 %collective-permute-start.5 = (f32[392,128]{1,0:T(8,128)S(1)}, f32[392,128]{1,0:T(8,128)S(1)}, u32[]{:S(2)}, u32[]{:S(2)}) collective-permute-start(f32[392,128]{1,0:T(8,128)S(1)} %get-tuple-element.26), channel_id=1, source_target_pairs={{0,1},{1,0},{2,3},{3,2},{4,5},{5,4},{6,7},{7,6},{8,9},{9,8},{10,11... | collective-permute-start | bytes 602120 | tf_op jit(solution)/shard_map/ppermute | solution.py:204
  45.3 26.8 %collective-permute-start.6 = (f32[392,128]{1,0:T(8,128)S(1)}, f32[392,128]{1,0:T(8,128)S(1)}, u32[]{:S(2)}, u32[]{:S(2)}) collective-permute-start(f32[392,128]{1,0:T(8,128)S(1)} %get-tuple-element.27), channel_id=1, source_target_pairs={{0,2},{1,3},{2,0},{3,1},{4,6},{5,7},{6,4},{7,5},{8,10},{9,11},{10,... | collective-permute-start | bytes 602120 | tf_op jit(solution)/shard_map/ppermute | solution.py:204
  45.7 26.3 %collective-permute-start.7 = (f32[392,128]{1,0:T(8,128)S(1)}, f32[392,128]{1,0:T(8,128)S(1)}, u32[]{:S(2)}, u32[]{:S(2)}) collective-permute-start(f32[392,128]{1,0:T(8,128)S(1)} %get-tuple-element.28), channel_id=1, source_target_pairs={{0,3},{1,2},{2,1},{3,0},{4,7},{5,6},{6,5},{7,4},{8,11},{9,10},{10,... | collective-permute-start | bytes 602120 | tf_op jit(solution)/shard_map/ppermute | solution.py:204
  47.9 13.1 %collective-permute-start.14 = (f32[392,128]{1,0:T(8,128)S(1)}, f32[392,128]{1,0:T(8,128)S(1)}, u32[]{:S(2)}, u32[]{:S(2)}) collective-permute-start(f32[392,128]{1,0:T(8,128)S(1)} %get-tuple-element.35), channel_id=1, source_target_pairs={{0,2},{1,3},{2,0},{3,1},{4,6},{5,7},{6,4},{7,5},{8,10},{9,11},{10,... | collective-permute-start | bytes 602120 | tf_op jit(solution)/shard_map/ppermute | solution.py:204
  47.9 16.8 %collective-permute-start.15 = (f32[392,128]{1,0:T(8,128)S(1)}, f32[392,128]{1,0:T(8,128)S(1)}, u32[]{:S(2)}, u32[]{:S(2)}) collective-permute-start(f32[392,128]{1,0:T(8,128)S(1)} %get-tuple-element.36), channel_id=1, source_target_pairs={{0,3},{1,2},{2,1},{3,0},{4,7},{5,6},{6,5},{7,4},{8,11},{9,10},{10,... | collective-permute-start | bytes 602120 | tf_op jit(solution)/shard_map/ppermute | solution.py:204
  49.4 15.3 %copy-start.5 = (f32[16]{0:T(128)S(1)}, f32[16]{0:T(128)}, u32[]{:S(2)}) copy-start(f32[16]{0:T(128)} %ridge_ref.3) | copy-start | bytes 196

commit v2 on v0

v2 whole, which is shorter than its diff:
```python
import functools

import jax
import jax.numpy as jnp
from jax import lax
from jax.experimental import pallas as pl
from jax.experimental.pallas import tpu as pltpu
from jax.sharding import Mesh
from jax.sharding import PartitionSpec as P

CG_ITERS = 3
DOC_SHARE = 4
EXTRA = 8


def split(x):
    high = x.astype(jnp.bfloat16)
    low = (x - high.astype(jnp.float32)).astype(jnp.bfloat16)
    return high, low


def dot(a, b):
    return lax.dot_general(a, b, (((1,), (0,)), ((), ())), preferred_element_type=jnp.float32)


def dot_rows(a, b):
    return lax.dot_general(a, b, (((0,), (0,)), ((), ())), preferred_element_type=jnp.float32)


def total(terms):
    return functools.reduce(lambda a, b: a + b, terms)


def triangle(width):
    row = lax.broadcasted_iota(jnp.int32, (width, width), 0)
    col = lax.broadcasted_iota(jnp.int32, (width, width), 1)
    return row <= col, row == col


def down(ids):
    count = ids.shape[1]
    return jnp.broadcast_to(ids, (count, count)).T[:, :1]


def last_weight(ids_ref, width):
    ids = ids_ref[...].astype(jnp.float32)
    newest = jnp.max(ids, 1, keepdims=True)
    weight = (down(ids) == newest).astype(jnp.float32)
    return ids, newest, jnp.broadcast_to(weight, (ids.shape[1], width))


def row_scale(wide):
    return lax.rsqrt(jnp.sum(wide * wide, -1, keepdims=True) + 1e-06)


def own_gram_kernel(width, pairs, me_ref, ids_ref, k_hbm, *refs):
    outs, (k_ref, sems) = refs[:-2], refs[-2:]
    span = pairs * 2 * width
    copies = []
    for slot in range(len(outs)):
        start = pl.multiple_of((me_ref[0] ^ slot) * span, span)
        copy = pltpu.make_async_copy(k_hbm.at[:, pl.ds(start, span)], k_ref.at[slot], sems.at[slot])
        copy.start()
        copies.append(copy)
    upper, diagonal = triangle(width)
    ids, newest, weight = last_weight(ids_ref, width)
    oldest = jnp.min(ids, 1, keepdims=True)
    marks = [jnp.broadcast_to(one + 1.0, (1, width)) for one in (oldest, newest)]
    filler = jnp.zeros((EXTRA - 3, width), jnp.float32)
    for slot, out in enumerate(outs):
        copies[slot].wait()
        for pair in range(pairs):
            grams = []
            for side in range(2):
                keys = k_ref[slot, :, pl.ds((pair * 2 + side) * width, width)]
                wide = keys.astype(jnp.float32)
                scale = row_scale(wide)
                high, low = split(weight * (scale * scale) * wide)
                grams.append(dot_rows(jnp.concatenate([keys, keys], 0), jnp.concatenate([high, low], 0)))
            top = pair * (width + EXTRA)
            out[pl.ds(top, width), :] = jnp.where(upper, grams[0], grams[1])
            second = jnp.sum(jnp.where(diagonal, grams[1], 0.0), 0, keepdims=True)
            out[pl.ds(top + width, EXTRA), :] = jnp.concatenate([second, *marks, filler], 0)


def own_cross_kernel(width, heads, me_ref, ids_ref, k_ref, v_ref, *outs):
    weight = last_weight(ids_ref, width)[2]
    for slot, out in enumerate(outs):
        for head in range(heads):
            lanes = pl.ds(pl.multiple_of(((me_ref[0] ^ slot) * heads + head) * width, width), width)
            keys = k_ref[:, lanes]
            scale = row_scale(keys.astype(jnp.float32))
            high, low = split(weight * scale * v_ref[:, lanes].astype(jnp.float32))
            out[pl.ds(head * width, width), :] = dot_rows(
                jnp.concatenate([keys, keys], 0), jnp.concatenate([high, low], 0)
            )


def marks_of(refs, width):
    first = [ref[pl.ds(width + 1, 1), :] for ref in refs]
    last = [ref[pl.ds(width + 2, 1), :] for ref in refs]
    return first, last


def total_kernel(width, pairs, with_marks, count, *refs):
    marked, slots, out = refs[:count], refs[-1 - count : -1], refs[-1]
    last = marks_of(marked, width)[1]
    newest = functools.reduce(jnp.maximum, last)
    out[...] = total([slot[...] * (one == newest).astype(jnp.float32) for slot, one in zip(slots, last)])
    if with_marks:
        for pair in range(pairs):
            out[pl.ds(pair * (width + EXTRA) + width + 1, 2), :] = jnp.concatenate([newest, newest], 0)


def prefix_kernel(width, count, steps, me_ref, *refs):
    outs, refs = refs[-count:], refs[:-count]
    marked, marked_carries = refs[:count], refs[count : count + steps]
    slots, carries = refs[-count - steps : len(refs) - steps], refs[len(refs) - steps :]
    first, last = marks_of(marked, width)
    oldest = functools.reduce(jnp.minimum, first)
    carry_last = marks_of(marked_carries, width)[1]
    carry = total([one[...] * (mark == oldest).astype(jnp.float32) for one, mark in zip(carries, carry_last)])
    me = me_ref[0]
    for target, out in enumerate(outs):
        terms = [carry * (first[target] == oldest).astype(jnp.float32)]
        for source in range(count):
            if source != target:
                before = jnp.where((me ^ source) < (me ^ target), 1.0, 0.0)
                terms.append(slots[source][...] * ((last[source] == first[target]).astype(jnp.float32) * before))
        out[...] = total(terms)


def solve_kernel(width, pairs, count, me_ref, ridge_ref, ids_ref, q_ref, k_ref, v_ref, *refs):
    slots, (x_ref, near_ref) = refs[:count], refs[count:]
    upper, diagonal = triangle(width)
    ids = ids_ref[...].astype(jnp.float32)
    column = down(ids)
    rows = ids.shape[1]
    carried = jnp.broadcast_to((column == jnp.min(ids, 1, keepdims=True)).astype(jnp.float32), (rows, width))
    row_at = lax.broadcasted_iota(jnp.int32, (rows, rows), 0)
    col_at = lax.broadcasted_iota(jnp.int32, (rows, rows), 1)
    within = jnp.where(row_at >= col_at, (column == ids).astype(jnp.float32), 0.0)

    def scores(vector, turned, mask):
        return split(dot(vector, turned) * mask)

    for slot, state in enumerate(slots):
        group = []
        for pair in range(pairs):
            top = pair * (width + EXTRA)
            packed = state[pl.ds(top, width), :]
            flipped = packed.T
            second = state[pl.ds(top + width, 1), :]
            grams = [
                jnp.where(upper, packed, flipped),
                jnp.where(diagonal, second, jnp.where(upper, flipped, packed)),
            ]
            for side in range(2):
                head = ((me_ref[0] ^ slot) * pairs + pair) * 2 + side
                lanes = pl.ds(pl.multiple_of(head * width, width), width)
                wide = q_ref[:, lanes].astype(jnp.float32)
                query = wide * row_scale(wide)
                keys = k_ref[:, lanes]
                turned = keys.astype(jnp.float32).T
                scale = lax.rsqrt(jnp.sum(turned * turned, 0, keepdims=True) + 1e-06)
                turned = turned.astype(jnp.bfloat16)
                high, low = split(grams[side])
                both = jnp.concatenate([high, turned], 1)
                group.append(
                    dict(
                        lanes=lanes,
                        both=jnp.concatenate([both, both], 0),
                        low=low,
                        turned=jnp.concatenate([turned, turned], 0),
                        keys=jnp.concatenate([keys, keys], 0),
                        once=within * scale,
                        twice=within * (scale * scale),
                        ridge=ridge_ref[head],
                        remain=query,
                        search=query,
                        square=jnp.sum(query * query, -1, keepdims=True),
                    )
                )
        for step in range(CG_ITERS):
            for h in group:
                high, low = split(h["search"])
                wide = dot(jnp.concatenate([high, low], 1), h["both"])
                h["state"] = wide[:, :width] + dot(high, h["low"])
                h["score"] = split(wide[:, width:] * h["twice"])
            for h in group:
                local = dot(jnp.concatenate(h["score"], 1), h["keys"])
                search = h["search"]
                applied = h["state"] * carried + local + h["ridge"] * search
                size = h["square"] / jnp.sum(search * applied, -1, keepdims=True)
                h["solved"] = size * search if step == 0 else h["solved"] + size * search
                if step < CG_ITERS - 1:
                    remain = h["remain"] - size * applied
                    square = jnp.sum(remain * remain, -1, keepdims=True)
                    h["search"] = remain + square / h["square"] * search
                    h["remain"], h["square"] = remain, square
        for h in group:
            high, low = split(h["solved"])
            h["score"] = split(dot(jnp.concatenate([high, low], 1), h["turned"]) * h["once"])
            x_ref[:, h["lanes"]] = h["solved"] * carried
        for h in group:
            values = v_ref[:, h["lanes"]]
            near_ref[:, h["lanes"]] = dot(jnp.concatenate(h["score"], 1), jnp.concatenate([values, values], 0))


def readout_kernel(width, heads, count, me_ref, x_ref, near_ref, *refs):
    slots, out = refs[:count], refs[count]
    for slot, state in enumerate(slots):
        for head in range(heads):
            lanes = pl.ds(pl.multiple_of(((me_ref[0] ^ slot) * heads + head) * width, width), width)
            high, low = split(x_ref[:, lanes])
            s_high, s_low = split(state[pl.ds(head * width, width), :])
            far = dot(jnp.concatenate([high, low], 1), jnp.concatenate([s_high, s_high], 0)) + dot(high, s_low)
            out[:, lanes] = near_ref[:, lanes] + far


VMEM = pl.BlockSpec(memory_space=pltpu.VMEM)
SMEM = pl.BlockSpec(memory_space=pltpu.SMEM)
ANY = pl.BlockSpec(memory_space=pl.ANY)
PARAMS = pltpu.CompilerParams(vmem_limit_bytes=40 * 1024 * 1024)


def call(kernel, name, flops, out_shape, in_specs, arguments, scratch=()):
    out_specs = [VMEM] * len(out_shape) if isinstance(out_shape, list) else VMEM
    return pl.pallas_call(
        kernel,
        out_shape=out_shape,
        in_specs=in_specs,
        out_specs=out_specs,
        scratch_shapes=scratch,
        compiler_params=PARAMS,
        cost_estimate=pl.CostEstimate(flops=flops, bytes_accessed=0, transcendentals=0),
        name=name,
    )(*arguments)


def on_device(queries, key_vectors, value_vectors, segment_ids, ridge_weight):
    row_count, columns = queries.shape
    head_count = ridge_weight.shape[0]
    width = columns // head_count
    outer, half, near = lax.axis_size("outer"), lax.axis_size("half"), lax.axis_size("near")
    blocks = outer * half
    heads = head_count // near
    pairs = heads // 2
    steps = min(-(-(row_count * near * blocks // DOC_SHARE - 1) // (row_count * near)), blocks - 1)
    me = lax.axis_index("near").astype(jnp.int32).reshape(1)
    ids = segment_ids.reshape(1, row_count)
    gram_shape = jax.ShapeDtypeStruct((pairs * (width + EXTRA), width), jnp.float32)
    cross_shape = jax.ShapeDtypeStruct((heads * width, width), jnp.float32)
    unit = 32 * head_count * width * width * row_count
    flat = jax.ShapeDtypeStruct((row_count, columns), jnp.float32)

    def exchange(slots):
        return [slots[0]] + [
            lax.ppermute(slots[j], "near", [(i, i ^ j) for i in range(near)]) for j in range(1, near)
        ]

    def onward(value):
        return [
            lax.ppermute(value, ("outer", "half"), [(i, i + step) for i in range(blocks - step)])
            for step in range(1, steps + 1)
        ]

    own_gram = call(
        functools.partial(own_gram_kernel, width, pairs),
        "own_gram",
        unit,
        [gram_shape] * near,
        [SMEM, VMEM, ANY],
        (me, ids, key_vectors),
        (pltpu.VMEM((near, row_count, heads * width), key_vectors.dtype), pltpu.SemaphoreType.DMA((near,))),
    )
    gram = exchange(own_gram)
    own_cross = call(
        functools.partial(own_cross_kernel, width, heads),
        "own_cross",
        unit,
        [cross_shape] * near,
        [SMEM, VMEM, VMEM, VMEM],
        (me, ids, key_vectors, value_vectors),
    )
    cross = exchange(own_cross)
    gram_carry = onward(
        call(functools.partial(total_kernel, width, pairs, True, near), "gram_total", unit // 4, gram_shape, [VMEM] * near, gram)
    )
    cross_carry = onward(
        call(
            functools.partial(total_kernel, width, pairs, False, near),
            "cross_total",
        unit // 4,
            cross_shape,
            [VMEM] * (2 * near),
            (*gram, *cross),
        )
    )
    gram_prefix = exchange(
        call(
            functools.partial(prefix_kernel, width, near, steps),
            "gram_prefix",
        unit // 4,
            [gram_shape] * near,
            [SMEM] + [VMEM] * (near + steps),
            (me, *gram, *gram_carry),
        )
    )
    cross_prefix = exchange(
        call(
            functools.partial(prefix_kernel, width, near, steps),
            "cross_prefix",
        unit // 4,
            [cross_shape] * near,
            [SMEM] + [VMEM] * (2 * (near + steps)),
            (me, *gram, *gram_carry, *cross, *cross_carry),
        )
    )
    solved, local = call(
        functools.partial(solve_kernel, width, pairs, near),
        "solve",
        8 * unit,
        [flat, flat],
        [SMEM, SMEM, VMEM, VMEM, VMEM, VMEM] + [VMEM] * near,
        (me, ridge_weight, ids, queries, key_vectors, value_vectors, *gram_prefix),
    )
    return call(
        functools.partial(readout_kernel, width, heads, near),
        "readout",
        2 * unit,
        flat,
        [SMEM, VMEM, VMEM] + [VMEM] * near,
        (me, solved, local, *cross_prefix),
    )


def solution(mesh):
    outer, inner = mesh.shape["outer"], mesh.shape["inner"]
    near = inner // 2
    finer = Mesh(mesh.devices.reshape(outer, 2, near), ("outer", "half", "near"))
    tokens = P(("outer", "half", "near"))
    return jax.shard_map(
        on_device, mesh=finer, in_specs=(tokens, tokens, tokens, tokens, P()), out_specs=tokens, check_vma=False
    )
```

time: 243 us -> 70.6 us (0.29)
  the two profiles are of different devices: /device:TPU:0 before, /device:TPU:1 now
where the time goes in v2:
time: 70.6 us; the launch traced here: 69.7 us
  starting transfers between devices  29.7 us (42%)
  waiting for transfers between devices  25.8 us (37%)
  Pallas kernels  12.4 us (18%)
  local copies, waits for them, and re-layouts  1.71 us (2%)
    ppermute x12, waiting for transfers between devices, exchange(): lax.ppermute(slots[j], 'near', [(i, i ^ j) for i in range(near)])  18 us
    ppermute x12, starting transfers between devices, exchange(): lax.ppermute(slots[j], 'near', [(i, i ^ j) for i in range(near)])  15.9 us
    ppermute x4, starting transfers between devices, onward(): lax.ppermute(value, ('outer', 'half'), [(i, i + step) for i in range(bloc...  13.8 us
    pallas_call x8, Pallas kernels, call(): pl.pallas_call(kernel, out_shape=out_shape, in_specs=in_specs, out_specs=...  12.4 us
    ppermute x4, waiting for transfers between devices, onward(): lax.ppermute(value, ('outer', 'half'), [(i, i + step) for i in range(bloc...  7.8 us
    unnamed x12, local copies, waits for them, and re-layouts  1.71 us
  transfers between devices with their start and end apart: 16, of which 6 were waited for; matrix products, arithmetic and copies ran while one was open for 0% of the time, Pallas kernels for 13%

profile of v2, /device:TPU:1, one launch (start us, length us, event | category | flops | bytes accessed | tf_op | source)
XLA Modules:
  0.0 69.7 jit_solution(9164050680298908762)
XLA Ops:
  0.0 0.0 copy-start.5
  0.0 0.7 copy-done.5
  0.7 0.0 copy-start.1
  0.7 1.0 %copy-done.1 = bf16[128,2048]{1,0:T(8,128)(2,1)S(1)} copy-done((bf16[128,2048]{1,0:T(8,128)(2,1)S(1)}, bf16[128,2048]{1,0:T(8,128)(2,1)}, u32[]{:S(2)}) %copy-start.1) | copy-done | bytes 524312
  1.7 0.0 copy-start.3
  1.7 1.7 %own_gram.1 = (f32[272,128]{1,0:T(8,128)S(1)}, f32[272,128]{1,0:T(8,128)S(1)}, f32[272,128]{1,0:T(8,128)S(1)}, f32[272,128]{1,0:T(8,128)S(1)}) custom-call(s32[1]{0:T(128)} %bitcast.me_ref, s32[1,128]{1,0:T(1,128)S(1)} %bitcast.2, bf16[128,2048]{1,0:T(8,128)(2,1)S(1)} %copy-done.1), custom_call_target="tpu_custom_call" | custom-call | flops 1073741824 | tf_op jit(solution)/shard_map/own_gram/pallas_call | solution.py:229
  3.4 2.1 %collective-permute-start = (f32[272,128]{1,0:T(8,128)S(1)}, f32[272,128]{1,0:T(8,128)S(1)}, u32[]{:S(2)}, u32[]{:S(2)}) collective-permute-start(f32[272,128]{1,0:T(8,128)S(1)} %get-tuple-element.24), channel_id=1, source_target_pairs={{0,1},{1,0},{2,3},{3,2},{4,5},{5,4},{6,7},{7,6},{8,9},{9,8},{10,11... | collective-permute-start | bytes 417800 | tf_op jit(solution)/shard_map/ppermute | solution.py:259
  5.5 0.0 copy-done.3
  5.5 0.8 %own_cross.1 = (f32[512,128]{1,0:T(8,128)S(1)}, f32[512,128]{1,0:T(8,128)S(1)}, f32[512,128]{1,0:T(8,128)S(1)}, f32[512,128]{1,0:T(8,128)S(1)}) custom-call(s32[1]{0:T(128)} %bitcast.me_ref, s32[1,128]{1,0:T(1,128)S(1)} %bitcast.3, bf16[128,2048]{1,0:T(8,128)(2,1)S(1)} %copy-done.1, bf16[128,2048]{1,0:T(8,128)(2,1)S(1)} %copy-done.3), custom_call_target="tpu_custom_call" | custom-call | flops 1073741824 | tf_op jit(solution)/shard_map/own_cross/pallas_call | solution.py:229
  6.4 0.1 collective-permute-start.8
  6.5 1.5 %collective-permute-start.9 = (f32[512,128]{1,0:T(8,128)S(1)}, f32[512,128]{1,0:T(8,128)S(1)}, u32[]{:S(2)}, u32[]{:S(2)}) collective-permute-start(f32[512,128]{1,0:T(8,128)S(1)} %get-tuple-element.35), channel_id=1, source_target_pairs={{0,2},{1,3},{2,0},{3,1},{4,6},{5,7},{6,4},{7,5},{8,10},{9,11},{10,... | collective-permute-start | bytes 786440 | tf_op jit(solution)/shard_map/ppermute | solution.py:259
  8.0 1.1 %collective-permute-start.10 = (f32[512,128]{1,0:T(8,128)S(1)}, f32[512,128]{1,0:T(8,128)S(1)}, u32[]{:S(2)}, u32[]{:S(2)}) collective-permute-start(f32[512,128]{1,0:T(8,128)S(1)} %get-tuple-element.36), channel_id=1, source_target_pairs={{0,3},{1,2},{2,1},{3,0},{4,7},{5,6},{6,5},{7,4},{8,11},{9,10},{10,... | collective-permute-start | bytes 786440 | tf_op jit(solution)/shard_map/ppermute | solution.py:259
  9.1 1.3 %collective-permute-start.1 = (f32[272,128]{1,0:T(8,128)S(1)}, f32[272,128]{1,0:T(8,128)S(1)}, u32[]{:S(2)}, u32[]{:S(2)}) collective-permute-start(f32[272,128]{1,0:T(8,128)S(1)} %get-tuple-element.25), channel_id=1, source_target_pairs={{0,2},{1,3},{2,0},{3,1},{4,6},{5,7},{6,4},{7,5},{8,10},{9,11},{10,... | collective-permute-start | bytes 417800 | tf_op jit(solution)/shard_map/ppermute | solution.py:259
  10.4 0.0 collective-permute-done.refs_1_
  10.4 0.7 collective-permute-start.2
  11.1 11.0 %collective-permute-done.1.refs_2_ = f32[272,128]{1,0:T(8,128)S(1)} collective-permute-done((f32[272,128]{1,0:T(8,128)S(1)}, f32[272,128]{1,0:T(8,128)S(1)}, u32[]{:S(2)}, u32[]{:S(2)}) %collective-permute-start.1) | collective-permute-done | bytes 139296 | tf_op jit(solution)/shard_map/ppermute | solution.py:259
  22.0 3.4 %collective-permute-done.2.refs_3_ = f32[272,128]{1,0:T(8,128)S(1)} collective-permute-done((f32[272,128]{1,0:T(8,128)S(1)}, f32[272,128]{1,0:T(8,128)S(1)}, u32[]{:S(2)}, u32[]{:S(2)}) %collective-permute-start.2) | collective-permute-done | bytes 139296 | tf_op jit(solution)/shard_map/ppermute | solution.py:259
  25.5 5.5 %collective-permute-start.4 = (f32[272,128]{1,0:T(8,128)S(1)}, f32[272,128]{1,0:T(8,128)S(1)}, u32[]{:S(2)}, u32[]{:S(2)}) collective-permute-start(f32[272,128]{1,0:T(8,128)S(1)} %gram_total.1), channel_id=1, source_target_pairs={{0,8},{4,12},{8,16},{12,20},{16,24},{20,28},{1,9},{5,13},{9,17},{1... | collective-permute-start | bytes 417800 | tf_op jit(solution)/shard_map/ppermute | solution.py:264
  31.0 4.2 %collective-permute-start.3 = (f32[272,128]{1,0:T(8,128)S(1)}, f32[272,128]{1,0:T(8,128)S(1)}, u32[]{:S(2)}, u32[]{:S(2)}) collective-permute-start(f32[272,128]{1,0:T(8,128)S(1)} %gram_total.1), channel_id=1, source_target_pairs={{0,4},{4,8},{8,12},{12,16},{16,20},{20,24},{24,28},{1,5},{5,9},{9,... | collective-permute-start | bytes 417800 | tf_op jit(solution)/shard_map/ppermute | solution.py:264
  35.2 0.0 collective-permute-done.8.refs_5_.refs_7_
  35.3 0.0 collective-permute-done.9.refs_6_.refs_8_
  35.3 0.0 collective-permute-done.10.refs_7_.refs_9_
  35.3 0.1 cross_total.1
  35.4 2.2 %collective-permute-start.12 = (f32[512,128]{1,0:T(8,128)S(1)}, f32[512,128]{1,0:T(8,128)S(1)}, u32[]{:S(2)}, u32[]{:S(2)}) collective-permute-start(f32[512,128]{1,0:T(8,128)S(1)} %cross_total.1), channel_id=1, source_target_pairs={{0,8},{4,12},{8,16},{12,20},{16,24},{20,28},{1,9},{5,13},{9,17},{1... | collective-permute-start | bytes 786440 | tf_op jit(solution)/shard_map/ppermute | solution.py:264
  37.6 1.9 %collective-permute-start.11 = (f32[512,128]{1,0:T(8,128)S(1)}, f32[512,128]{1,0:T(8,128)S(1)}, u32[]{:S(2)}, u32[]{:S(2)}) collective-permute-start(f32[512,128]{1,0:T(8,128)S(1)} %cross_total.1), channel_id=1, source_target_pairs={{0,4},{4,8},{8,12},{12,16},{16,20},{20,24},{24,28},{1,5},{5,9},{9,... | collective-permute-start | bytes 786440 | tf_op jit(solution)/shard_map/ppermute | solution.py:264
  39.5 0.0 collective-permute-done.4.refs_5_
  39.5 2.6 %collective-permute-done.3.refs_4_ = f32[272,128]{1,0:T(8,128)S(1)} collective-permute-done((f32[272,128]{1,0:T(8,128)S(1)}, f32[272,128]{1,0:T(8,128)S(1)}, u32[]{:S(2)}, u32[]{:S(2)}) %collective-permute-start.3) | collective-permute-done | bytes 139296 | tf_op jit(solution)/shard_map/ppermute | solution.py:264
  42.2 0.2 gram_prefix.1
  42.3 0.4 collective-permute-start.5
  42.7 5.1 %collective-permute-start.6 = (f32[272,128]{1,0:T(8,128)S(1)}, f32[272,128]{1,0:T(8,128)S(1)}, u32[]{:S(2)}, u32[]{:S(2)}) collective-permute-start(f32[272,128]{1,0:T(8,128)S(1)} %get-tuple-element.29), channel_id=1, source_target_pairs={{0,2},{1,3},{2,0},{3,1},{4,6},{5,7},{6,4},{7,5},{8,10},{9,11},{10,... | collective-permute-start | bytes 417800 | tf_op jit(solution)/shard_map/ppermute | solution.py:259
  47.8 0.0 copy-start
  47.8 0.0 copy-start.2
  47.8 0.9 %collective-permute-start.7 = (f32[272,128]{1,0:T(8,128)S(1)}, f32[272,128]{1,0:T(8,128)S(1)}, u32[]{:S(2)}, u32[]{:S(2)}) collective-permute-start(f32[272,128]{1,0:T(8,128)S(1)} %get-tuple-element.30), channel_id=1, source_target_pairs={{0,3},{1,2},{2,1},{3,0},{4,7},{5,6},{6,5},{7,4},{8,11},{9,10},{10,... | collective-permute-start | bytes 417800 | tf_op jit(solution)/shard_map/ppermute | solution.py:259
  48.7 0.0 collective-permute-done.12.refs_11_
  48.7 5.1 %collective-permute-done.11.refs_10_ = f32[512,128]{1,0:T(8,128)S(1)} collective-permute-done((f32[512,128]{1,0:T(8,128)S(1)}, f32[512,128]{1,0:T(8,128)S(1)}, u32[]{:S(2)}, u32[]{:S(2)}) %collective-permute-start.11) | collective-permute-done | bytes 262176 | tf_op jit(solution)/shard_map/ppermute | solution.py:264
  53.8 0.3 cross_prefix.1
  54.2 0.4 collective-permute-start.13
  54.5 0.0 collective-permute-start.14
  54.6 0.0 collective-permute-done.5.refs_1_
  54.6 0.0 copy-start.4
  54.6 2.3 %collective-permute-start.15 = (f32[512,128]{1,0:T(8,128)S(1)}, f32[512,128]{1,0:T(8,128)S(1)}, u32[]{:S(2)}, u32[]{:S(2)}) collective-permute-start(f32[512,128]{1,0:T(8,128)S(1)} %get-tuple-element.40), channel_id=1, source_target_pairs={{0,3},{1,2},{2,1},{3,0},{4,7},{5,6},{6,5},{7,4},{8,11},{9,10},{10,... | collective-permute-start | bytes 786440 | tf_op jit(solution)/shard_map/ppermute | solution.py:259
  56.9 0.0 collective-permute-done.6.refs_2_
  56.9 0.4 collective-permute-done.7.refs_3_
  57.3 0.0 copy-done
  57.3 0.0 copy-done.2
  57.3 0.0 copy-done.4
  57.3 7.5 %solve.1 = (f32[128,2048]{1,0:T(8,128)S(1)}, f32[128,2048]{1,0:T(8,128)S(1)}) custom-call(s32[1]{0:T(128)} %bitcast.me_ref, f32[16]{0:T(128)S(1)} %copy-done.4, s32[1,128]{1,0:T(1,128)S(1)} %bitcast.4, bf16[128,2048]{1,0:T(8,128)(2,1)S(1)} %copy-done, bf16[128,2048]{1,0:T(8,128)(2,1)S(1)} %copy-done.2, bf16[128,2048]{1,0:T(8,128)(2,1)S(1)} %copy-done.3, ...), custom_call_target="tpu_custom_call" | custom-call | flops 8589934592 | tf_op jit(solution)/shard_map/solve/pallas_call | solution.py:229
  64.8 0.0 collective-permute-done.13.refs_1_
  64.8 0.0 collective-permute-done.14.refs_2_
  64.8 3.2 %collective-permute-done.15.refs_3_ = f32[512,128]{1,0:T(8,128)S(1)} collective-permute-done((f32[512,128]{1,0:T(8,128)S(1)}, f32[512,128]{1,0:T(8,128)S(1)}, u32[]{:S(2)}, u32[]{:S(2)}) %collective-permute-start.15) | collective-permute-done | bytes 262176 | tf_op jit(solution)/shard_map/ppermute | solution.py:259
  68.0 1.7 %readout.1 = f32[128,2048]{1,0:T(8,128)} custom-call(s32[1]{0:T(128)} %bitcast.me_ref, f32[128,2048]{1,0:T(8,128)S(1)} %get-tuple-element.31.x_ref, f32[128,2048]{1,0:T(8,128)S(1)} %get-tuple-element.32.near_ref, f32[512,128]{1,0:T(8,128)S(1)} %get-tuple-element.37.refs_0_, f32[512,128]{1,0:T(8,128)S(1)} %collective-permute-done.13.refs_1_, ...), custom_call_target="tpu_custom_call" | custom-call | flops 2147483648 | tf_op jit(solution)/shard_map/readout/pallas_call | solution.py:229
  (1 shorter events, 0.0 us)
Async XLA Ops:
  0.0 0.7 copy-start.5
  0.7 1.0 %copy-start.1 = (bf16[128,2048]{1,0:T(8,128)(2,1)S(1)}, bf16[128,2048]{1,0:T(8,128)(2,1)}, u32[]{:S(2)}) copy-start(bf16[128,2048]{1,0:T(8,128)(2,1)} %k_ref.3) | copy-start | bytes 1572868
  1.7 3.8 %copy-start.3 = (bf16[128,2048]{1,0:T(8,128)(2,1)S(1)}, bf16[128,2048]{1,0:T(8,128)(2,1)}, u32[]{:S(2)}) copy-start(bf16[128,2048]{1,0:T(8,128)(2,1)} %v_ref.3) | copy-start | bytes 1572868
  3.4 7.0 %collective-permute-start = (f32[272,128]{1,0:T(8,128)S(1)}, f32[272,128]{1,0:T(8,128)S(1)}, u32[]{:S(2)}, u32[]{:S(2)}) collective-permute-start(f32[272,128]{1,0:T(8,128)S(1)} %get-tuple-element.24), channel_id=1, source_target_pairs={{0,1},{1,0},{2,3},{3,2},{4,5},{5,4},{6,7},{7,6},{8,9},{9,8},{10,11... | collective-permute-start | bytes 417800 | tf_op jit(solution)/shard_map/ppermute | solution.py:259
  6.4 28.9 %collective-permute-start.8 = (f32[512,128]{1,0:T(8,128)S(1)}, f32[512,128]{1,0:T(8,128)S(1)}, u32[]{:S(2)}, u32[]{:S(2)}) collective-permute-start(f32[512,128]{1,0:T(8,128)S(1)} %get-tuple-element.34), channel_id=1, source_target_pairs={{0,1},{1,0},{2,3},{3,2},{4,5},{5,4},{6,7},{7,6},{8,9},{9,8},{10,11... | collective-permute-start | bytes 786440 | tf_op jit(solution)/shard_map/ppermute | solution.py:259
  6.5 28.8 %collective-permute-start.9 = (f32[512,128]{1,0:T(8,128)S(1)}, f32[512,128]{1,0:T(8,128)S(1)}, u32[]{:S(2)}, u32[]{:S(2)}) collective-permute-start(f32[512,128]{1,0:T(8,128)S(1)} %get-tuple-element.35), channel_id=1, source_target_pairs={{0,2},{1,3},{2,0},{3,1},{4,6},{5,7},{6,4},{7,5},{8,10},{9,11},{10,... | collective-permute-start | bytes 786440 | tf_op jit(solution)/shard_map/ppermute | solution.py:259
  8.0 27.3 %collective-permute-start.10 = (f32[512,128]{1,0:T(8,128)S(1)}, f32[512,128]{1,0:T(8,128)S(1)}, u32[]{:S(2)}, u32[]{:S(2)}) collective-permute-start(f32[512,128]{1,0:T(8,128)S(1)} %get-tuple-element.36), channel_id=1, source_target_pairs={{0,3},{1,2},{2,1},{3,0},{4,7},{5,6},{6,5},{7,4},{8,11},{9,10},{10,... | collective-permute-start | bytes 786440 | tf_op jit(solution)/shard_map/ppermute | solution.py:259
  9.1 13.0 %collective-permute-start.1 = (f32[272,128]{1,0:T(8,128)S(1)}, f32[272,128]{1,0:T(8,128)S(1)}, u32[]{:S(2)}, u32[]{:S(2)}) collective-permute-start(f32[272,128]{1,0:T(8,128)S(1)} %get-tuple-element.25), channel_id=1, source_target_pairs={{0,2},{1,3},{2,0},{3,1},{4,6},{5,7},{6,4},{7,5},{8,10},{9,11},{10,... | collective-permute-start | bytes 417800 | tf_op jit(solution)/shard_map/ppermute | solution.py:259
  10.4 15.1 %collective-permute-start.2 = (f32[272,128]{1,0:T(8,128)S(1)}, f32[272,128]{1,0:T(8,128)S(1)}, u32[]{:S(2)}, u32[]{:S(2)}) collective-permute-start(f32[272,128]{1,0:T(8,128)S(1)} %get-tuple-element.26), channel_id=1, source_target_pairs={{0,3},{1,2},{2,1},{3,0},{4,7},{5,6},{6,5},{7,4},{8,11},{9,10},{10,... | collective-permute-start | bytes 417800 | tf_op jit(solution)/shard_map/ppermute | solution.py:259
  25.5 14.0 %collective-permute-start.4 = (f32[272,128]{1,0:T(8,128)S(1)}, f32[272,128]{1,0:T(8,128)S(1)}, u32[]{:S(2)}, u32[]{:S(2)}) collective-permute-start(f32[272,128]{1,0:T(8,128)S(1)} %gram_total.1), channel_id=1, source_target_pairs={{0,8},{4,12},{8,16},{12,20},{16,24},{20,28},{1,9},{5,13},{9,17},{1... | collective-permute-start | bytes 417800 | tf_op jit(solution)/shard_map/ppermute | solution.py:264
  31.0 11.1 %collective-permute-start.3 = (f32[272,128]{1,0:T(8,128)S(1)}, f32[272,128]{1,0:T(8,128)S(1)}, u32[]{:S(2)}, u32[]{:S(2)}) collective-permute-start(f32[272,128]{1,0:T(8,128)S(1)} %gram_total.1), channel_id=1, source_target_pairs={{0,4},{4,8},{8,12},{12,16},{16,20},{20,24},{24,28},{1,5},{5,9},{9,... | collective-permute-start | bytes 417800 | tf_op jit(solution)/shard_map/ppermute | solution.py:264
  35.4 13.3 %collective-permute-start.12 = (f32[512,128]{1,0:T(8,128)S(1)}, f32[512,128]{1,0:T(8,128)S(1)}, u32[]{:S(2)}, u32[]{:S(2)}) collective-permute-start(f32[512,128]{1,0:T(8,128)S(1)} %cross_total.1), channel_id=1, source_target_pairs={{0,8},{4,12},{8,16},{12,20},{16,24},{20,28},{1,9},{5,13},{9,17},{1... | collective-permute-start | bytes 786440 | tf_op jit(solution)/shard_map/ppermute | solution.py:264
  37.6 16.3 %collective-permute-start.11 = (f32[512,128]{1,0:T(8,128)S(1)}, f32[512,128]{1,0:T(8,128)S(1)}, u32[]{:S(2)}, u32[]{:S(2)}) collective-permute-start(f32[512,128]{1,0:T(8,128)S(1)} %cross_total.1), channel_id=1, source_target_pairs={{0,4},{4,8},{8,12},{12,16},{16,20},{20,24},{24,28},{1,5},{5,9},{9,... | collective-permute-start | bytes 786440 | tf_op jit(solution)/shard_map/ppermute | solution.py:264
  42.3 12.2 %collective-permute-start.5 = (f32[272,128]{1,0:T(8,128)S(1)}, f32[272,128]{1,0:T(8,128)S(1)}, u32[]{:S(2)}, u32[]{:S(2)}) collective-permute-start(f32[272,128]{1,0:T(8,128)S(1)} %get-tuple-element.28), channel_id=1, source_target_pairs={{0,1},{1,0},{2,3},{3,2},{4,5},{5,4},{6,7},{7,6},{8,9},{9,8},{10,11... | collective-permute-start | bytes 417800 | tf_op jit(solution)/shard_map/ppermute | solution.py:259
  42.7 14.2 %collective-permute-start.6 = (f32[272,128]{1,0:T(8,128)S(1)}, f32[272,128]{1,0:T(8,128)S(1)}, u32[]{:S(2)}, u32[]{:S(2)}) collective-permute-start(f32[272,128]{1,0:T(8,128)S(1)} %get-tuple-element.29), channel_id=1, source_target_pairs={{0,2},{1,3},{2,0},{3,1},{4,6},{5,7},{6,4},{7,5},{8,10},{9,11},{10,... | collective-permute-start | bytes 417800 | tf_op jit(solution)/shard_map/ppermute | solution.py:259
  47.8 9.4 %copy-start = (bf16[128,2048]{1,0:T(8,128)(2,1)S(1)}, bf16[128,2048]{1,0:T(8,128)(2,1)}, u32[]{:S(2)}) copy-start(bf16[128,2048]{1,0:T(8,128)(2,1)} %q_ref.1) | copy-start | bytes 1572868
  47.8 9.4 %copy-start.2 = (bf16[128,2048]{1,0:T(8,128)(2,1)S(1)}, bf16[128,2048]{1,0:T(8,128)(2,1)}, u32[]{:S(2)}) copy-start(bf16[128,2048]{1,0:T(8,128)(2,1)} %k_ref.3) | copy-start | bytes 1572868
  47.8 9.4 %collective-permute-start.7 = (f32[272,128]{1,0:T(8,128)S(1)}, f32[272,128]{1,0:T(8,128)S(1)}, u32[]{:S(2)}, u32[]{:S(2)}) collective-permute-start(f32[272,128]{1,0:T(8,128)S(1)} %get-tuple-element.30), channel_id=1, source_target_pairs={{0,3},{1,2},{2,1},{3,0},{4,7},{5,6},{6,5},{7,4},{8,11},{9,10},{10,... | collective-permute-start | bytes 417800 | tf_op jit(solution)/shard_map/ppermute | solution.py:259
  54.2 10.6 %collective-permute-start.13 = (f32[512,128]{1,0:T(8,128)S(1)}, f32[512,128]{1,0:T(8,128)S(1)}, u32[]{:S(2)}, u32[]{:S(2)}) collective-permute-start(f32[512,128]{1,0:T(8,128)S(1)} %get-tuple-element.38), channel_id=1, source_target_pairs={{0,1},{1,0},{2,3},{3,2},{4,5},{5,4},{6,7},{7,6},{8,9},{9,8},{10,11... | collective-permute-start | bytes 786440 | tf_op jit(solution)/shard_map/ppermute | solution.py:259
  54.5 10.2 %collective-permute-start.14 = (f32[512,128]{1,0:T(8,128)S(1)}, f32[512,128]{1,0:T(8,128)S(1)}, u32[]{:S(2)}, u32[]{:S(2)}) collective-permute-start(f32[512,128]{1,0:T(8,128)S(1)} %get-tuple-element.39), channel_id=1, source_target_pairs={{0,2},{1,3},{2,0},{3,1},{4,6},{5,7},{6,4},{7,5},{8,10},{9,11},{10,... | collective-permute-start | bytes 786440 | tf_op jit(solution)/shard_map/ppermute | solution.py:259
  54.6 2.7 %copy-start.4 = (f32[16]{0:T(128)S(1)}, f32[16]{0:T(128)}, u32[]{:S(2)}) copy-start(f32[16]{0:T(128)} %ridge_ref.1) | copy-start | bytes 196
  54.6 13.4 %collective-permute-start.15 = (f32[512,128]{1,0:T(8,128)S(1)}, f32[512,128]{1,0:T(8,128)S(1)}, u32[]{:S(2)}, u32[]{:S(2)}) collective-permute-start(f32[512,128]{1,0:T(8,128)S(1)} %get-tuple-element.40), channel_id=1, source_target_pairs={{0,3},{1,2},{2,1},{3,0},{4,7},{5,6},{6,5},{7,4},{8,11},{9,10},{10,... | collective-permute-start | bytes 786440 | tf_op jit(solution)/shard_map/ppermute | solution.py:259

commit v3 on v2

v3 whole, which is shorter than its diff:
```python
import functools

import jax
import jax.numpy as jnp
from jax import lax
from jax.experimental import pallas as pl
from jax.experimental.pallas import tpu as pltpu
from jax.sharding import Mesh
from jax.sharding import PartitionSpec as P

CG_ITERS = 3
DOC_SHARE = 4
EXTRA = 8


def split(x):
    high = x.astype(jnp.bfloat16)
    low = (x - high.astype(jnp.float32)).astype(jnp.bfloat16)
    return high, low


def dot(a, b):
    return lax.dot_general(a, b, (((1,), (0,)), ((), ())), preferred_element_type=jnp.float32)


def dot_rows(a, b):
    return lax.dot_general(a, b, (((0,), (0,)), ((), ())), preferred_element_type=jnp.float32)


def total(terms):
    return functools.reduce(lambda a, b: a + b, terms)


def triangle(width):
    row = lax.broadcasted_iota(jnp.int32, (width, width), 0)
    col = lax.broadcasted_iota(jnp.int32, (width, width), 1)
    return row <= col, row == col


def down(ids):
    count = ids.shape[1]
    return jnp.broadcast_to(ids, (count, count)).T[:, :1]


def last_weight(ids_ref, width):
    ids = ids_ref[...].astype(jnp.float32)
    newest = jnp.max(ids, 1, keepdims=True)
    weight = (down(ids) == newest).astype(jnp.float32)
    return ids, newest, jnp.broadcast_to(weight, (ids.shape[1], width))


def row_scale(wide):
    return lax.rsqrt(jnp.sum(wide * wide, -1, keepdims=True) + 1e-06)


def own_kernel(base, width, pairs, count, me_ref, ids_ref, k_ref, v_ref, *refs):
    outs = refs[-count:]
    upper, diagonal = triangle(width)
    ids, newest, weight = last_weight(ids_ref, width)
    oldest = jnp.min(ids, 1, keepdims=True)
    marks = [jnp.broadcast_to(one + 1.0, (1, width)) for one in (oldest, newest)]
    filler = jnp.zeros((EXTRA - 3, width), jnp.float32)
    for slot, out in enumerate(outs):
        for pair in range(pairs):
            top = pair * (3 * width + EXTRA)
            grams = []
            for side in range(2):
                head = base + ((me_ref[0] ^ slot) * pairs + pair) * 2 + side
                lanes = pl.ds(pl.multiple_of(head * width, width), width)
                keys = k_ref[:, lanes]
                wide = keys.astype(jnp.float32)
                scale = row_scale(wide)
                light = weight * scale
                k_high, k_low = split(light * scale * wide)
                v_high, v_low = split(light * v_ref[:, lanes].astype(jnp.float32))
                right = jnp.concatenate(
                    [jnp.concatenate([k_high, v_high], 1), jnp.concatenate([k_low, v_low], 1)], 0
                )
                both = dot_rows(jnp.concatenate([keys, keys], 0), right)
                grams.append(both[:, :width])
                out[pl.ds(top + (1 + side) * width + EXTRA, width), :] = both[:, width:]
            out[pl.ds(top, width), :] = jnp.where(upper, grams[0], grams[1])
            second = jnp.sum(jnp.where(diagonal, grams[1], 0.0), 0, keepdims=True)
            out[pl.ds(top + width, EXTRA), :] = jnp.concatenate([second, *marks, filler], 0)


def marks_of(refs, width):
    first = [ref[pl.ds(width + 1, 1), :] for ref in refs]
    last = [ref[pl.ds(width + 2, 1), :] for ref in refs]
    return first, last


def total_kernel(width, pairs, count, *refs):
    slots, out = refs[:count], refs[-1]
    last = marks_of(slots, width)[1]
    newest = functools.reduce(jnp.maximum, last)
    out[...] = total([slot[...] * (one == newest).astype(jnp.float32) for slot, one in zip(slots, last)])
    for pair in range(pairs):
        out[pl.ds(pair * (3 * width + EXTRA) + width + 1, 2), :] = jnp.concatenate([newest, newest], 0)


def prefix_kernel(width, count, me_ref, *refs):
    slots, carries, outs = refs[:count], refs[count:-count], refs[-count:]
    first, last = marks_of(slots, width)
    oldest = functools.reduce(jnp.minimum, first)
    carry_last = marks_of(carries, width)[1]
    carry = total([one[...] * (mark == oldest).astype(jnp.float32) for one, mark in zip(carries, carry_last)])
    me = me_ref[0]
    for target, out in enumerate(outs):
        terms = [carry * (first[target] == oldest).astype(jnp.float32)]
        for source in range(count):
            if source != target:
                before = jnp.where((me ^ source) < (me ^ target), 1.0, 0.0)
                terms.append(slots[source][...] * ((last[source] == first[target]).astype(jnp.float32) * before))
        out[...] = total(terms)


def solve_kernel(base, width, pairs, count, me_ref, ridge_ref, ids_ref, q_ref, k_ref, v_ref, *refs):
    slots, out = refs[:count], refs[-1]
    upper, diagonal = triangle(width)
    ids = ids_ref[...].astype(jnp.float32)
    column = down(ids)
    rows = ids.shape[1]
    carried = jnp.broadcast_to((column == jnp.min(ids, 1, keepdims=True)).astype(jnp.float32), (rows, width))
    row_at = lax.broadcasted_iota(jnp.int32, (rows, rows), 0)
    col_at = lax.broadcasted_iota(jnp.int32, (rows, rows), 1)
    within = jnp.where(row_at >= col_at, (column == ids).astype(jnp.float32), 0.0)

    group = []
    for slot, state in enumerate(slots):
        for pair in range(pairs):
            top = pair * (3 * width + EXTRA)
            packed = state[pl.ds(top, width), :]
            flipped = packed.T
            second = state[pl.ds(top + width, 1), :]
            grams = [
                jnp.where(upper, packed, flipped),
                jnp.where(diagonal, second, jnp.where(upper, flipped, packed)),
            ]
            for side in range(2):
                local = ((me_ref[0] ^ slot) * pairs + pair) * 2 + side
                head = base + local
                lanes = pl.ds(pl.multiple_of(head * width, width), width)
                wide = q_ref[:, lanes].astype(jnp.float32)
                query = wide * row_scale(wide)
                keys = k_ref[:, lanes]
                turned = keys.astype(jnp.float32).T
                scale = lax.rsqrt(jnp.sum(turned * turned, 0, keepdims=True) + 1e-06)
                turned = turned.astype(jnp.bfloat16)
                high, low = split(grams[side])
                both = jnp.concatenate([high, turned], 1)
                group.append(
                    dict(
                        lanes=lanes,
                        place=pl.ds(pl.multiple_of(local * width, width), width),
                        cross=state.at[pl.ds(top + EXTRA + (1 + side) * width, width)],
                        both=jnp.concatenate([both, both], 0),
                        low=low,
                        turned=turned,
                        keys=jnp.concatenate([keys, keys], 0),
                        once=within * scale,
                        twice=within * (scale * scale),
                        ridge=ridge_ref[head],
                        remain=query,
                        search=query,
                        square=jnp.sum(query * query, -1, keepdims=True),
                    )
                )
    for step in range(CG_ITERS):
        for h in group:
            high, low = split(h["search"])
            wide = dot(jnp.concatenate([high, low], 1), h["both"])
            h["state"] = wide[:, :width] + dot(high, h["low"])
            h["score"] = split(wide[:, width:] * h["twice"])
        for h in group:
            local = dot(jnp.concatenate(h["score"], 1), h["keys"])
            search = h["search"]
            applied = h["state"] * carried + local + h["ridge"] * search
            size = h["square"] / jnp.sum(search * applied, -1, keepdims=True)
            h["solved"] = size * search if step == 0 else h["solved"] + size * search
            if step < CG_ITERS - 1:
                remain = h["remain"] - size * applied
                square = jnp.sum(remain * remain, -1, keepdims=True)
                h["search"] = remain + square / h["square"] * search
                h["remain"], h["square"] = remain, square
    for h in group:
        high, low = split(h["solved"])
        c_high, c_low = split(h["cross"][...])
        both = jnp.concatenate([c_high, h["turned"]], 1)
        wide = dot(jnp.concatenate([high, low], 1), jnp.concatenate([both, both], 0))
        h["state"] = wide[:, :width] + dot(high, c_low)
        h["score"] = split(wide[:, width:] * h["once"])
    for h in group:
        values = v_ref[:, h["lanes"]]
        local = dot(jnp.concatenate(h["score"], 1), jnp.concatenate([values, values], 0))
        out[:, h["place"]] = h["state"] * carried + local


VMEM = pl.BlockSpec(memory_space=pltpu.VMEM)
SMEM = pl.BlockSpec(memory_space=pltpu.SMEM)
ANY = pl.BlockSpec(memory_space=pl.ANY)
PARAMS = pltpu.CompilerParams(vmem_limit_bytes=40 * 1024 * 1024)


def call(kernel, name, flops, out_shape, in_specs, arguments, **more):
    out_specs = [VMEM] * len(out_shape) if isinstance(out_shape, list) else VMEM
    return pl.pallas_call(
        kernel,
        out_shape=out_shape,
        in_specs=in_specs,
        compiler_params=PARAMS,
        cost_estimate=pl.CostEstimate(flops=flops, bytes_accessed=0, transcendentals=0),
        name=name,
        **{"out_specs": out_specs, **more},
    )(*arguments)


def on_device(queries, key_vectors, value_vectors, segment_ids, ridge_weight, *, pieces):
    row_count, columns = queries.shape
    head_count = ridge_weight.shape[0]
    width = columns // head_count
    outer, half, near = lax.axis_size("outer"), lax.axis_size("half"), lax.axis_size("near")
    blocks = outer * half
    pairs = head_count // (2 * near * pieces)
    steps = min(-(-(row_count * near * blocks // DOC_SHARE - 1) // (row_count * near)), blocks - 1)
    me = lax.axis_index("near").astype(jnp.int32).reshape(1)
    ids = segment_ids.reshape(1, row_count)
    shape = jax.ShapeDtypeStruct((pairs * (3 * width + EXTRA), width), jnp.float32)
    unit = 32 * pairs * 2 * near * width * width * row_count

    def exchange(slots):
        return [slots[0]] + [
            lax.ppermute(slots[j], "near", [(i, i ^ j) for i in range(near)]) for j in range(1, near)
        ]

    def onward(value):
        return [
            lax.ppermute(value, ("outer", "half"), [(i, i + step) for i in range(blocks - step)])
            for step in range(1, steps + 1)
        ]

    states = []
    for piece in range(pieces):
        own = call(
            functools.partial(own_kernel, piece * pairs * near * 2, width, pairs, near),
            "own_sums",
            unit,
            [shape] * near,
            [SMEM, VMEM, VMEM, VMEM],
            (me, ids, key_vectors, value_vectors),
        )
        slots = exchange(own)
        block_total = call(
            functools.partial(total_kernel, width, pairs, near), "block_total", unit // 4, shape, [VMEM] * near, slots
        )
        prefix = call(
            functools.partial(prefix_kernel, width, near),
            "prefixes",
            unit // 4,
            [shape] * near,
            [SMEM] + [VMEM] * (near + steps),
            (me, *slots, *onward(block_total)),
        )
        states.append(exchange(prefix))
    out = None
    for piece, state in enumerate(states):
        base = piece * pairs * near * 2
        span = pairs * near * 2 * width
        arguments = [me, ridge_weight, ids, queries, key_vectors, value_vectors, *state]
        in_specs = [SMEM, SMEM, VMEM, VMEM, VMEM, VMEM] + [VMEM] * near
        aliases = {}
        if out is not None:
            aliases = {len(arguments): 0}
            arguments.append(out)
            in_specs.append(ANY)
        out = call(
            functools.partial(solve_kernel, base, width, pairs, near),
            "solve",
            8 * unit,
            jax.ShapeDtypeStruct((row_count, columns), jnp.float32),
            in_specs,
            arguments,
            grid=(1,),
            out_specs=pl.BlockSpec((row_count, span), functools.partial(lambda p, i: (0, p), piece)),
            input_output_aliases=aliases,
        )
    return out


def solution(mesh):
    outer, inner = mesh.shape["outer"], mesh.shape["inner"]
    near = inner // 2
    finer = Mesh(mesh.devices.reshape(outer, 2, near), ("outer", "half", "near"))
    tokens = P(("outer", "half", "near"))

    def run(*arguments):
        pieces = max(1, min(2, arguments[-1].shape[0] // (2 * near)))
        return jax.shard_map(
            functools.partial(on_device, pieces=pieces),
            mesh=finer,
            in_specs=(tokens, tokens, tokens, tokens, P()),
            out_specs=tokens,
            check_vma=False,
        )(*arguments)

    return run
```

time: 70.6 us -> 63.3 us (0.90)
  waiting for transfers between devices: 25.8 us -> 14.4 us
  starting transfers between devices: 29.7 us -> 35 us
  Pallas kernels: 12.4 us -> 10.5 us
  local copies, waits for them, and re-layouts: 1.71 us -> 2.75 us
    ppermute x4, starting transfers between devices: 13.8 us -> 20.1 us  [onward(): lax.ppermute(value, ('outer', 'half'), [(i, i + step) for i in range(bloc...]
    ppermute x12, waiting for transfers between devices: 18 us -> 12 us  [exchange(): lax.ppermute(slots[j], 'near', [(i, i ^ j) for i in range(near)])]
    ppermute x4, waiting for transfers between devices: 7.8 us -> 2.32 us  [onward(): lax.ppermute(value, ('outer', 'half'), [(i, i + step) for i in range(bloc...]
    pallas_call x8, Pallas kernels: 12.4 us -> 10.5 us  [call(): pl.pallas_call(kernel, out_shape=out_shape, in_specs=in_specs, compiler_p...]
    unnamed x12 -> x14, local copies, waits for them, and re-layouts: 1.71 us -> 2.75 us
    ppermute x12, starting transfers between devices: 15.9 us -> 14.9 us  [exchange(): lax.ppermute(slots[j], 'near', [(i, i ^ j) for i in range(near)])]
  transfers between devices with their start and end apart: 16 -> 16, of which waited for: 6 -> 6; matrix products, arithmetic and copies ran while one was open for 0% -> 0% of each run, Pallas kernels for 13% -> 9%
where the time goes in v3:
time: 63.3 us; the launch traced here: 62.8 us
  starting transfers between devices  35 us (55%)
  waiting for transfers between devices  14.4 us (23%)
  Pallas kernels  10.5 us (17%)
  local copies, waits for them, and re-layouts  2.75 us (4%)
    ppermute x4, starting transfers between devices, onward(): lax.ppermute(value, ('outer', 'half'), [(i, i + step) for i in range(bloc...  20.1 us
    ppermute x12, starting transfers between devices, exchange(): lax.ppermute(slots[j], 'near', [(i, i ^ j) for i in range(near)])  14.9 us
    ppermute x12, waiting for transfers between devices, exchange(): lax.ppermute(slots[j], 'near', [(i, i ^ j) for i in range(near)])  12 us
    pallas_call x8, Pallas kernels, call(): pl.pallas_call(kernel, out_shape=out_shape, in_specs=in_specs, compiler_p...  10.5 us
    unnamed x14, local copies, waits for them, and re-layouts  2.75 us
    ppermute x4, waiting for transfers between devices, onward(): lax.ppermute(value, ('outer', 'half'), [(i, i + step) for i in range(bloc...  2.32 us
  transfers between devices with their start and end apart: 16, of which 6 were waited for; matrix products, arithmetic and copies ran while one was open for 0% of the time, Pallas kernels for 9%

profile of v3, /device:TPU:1, one launch (start us, length us, event | category | flops | bytes accessed | tf_op | source)
XLA Modules:
  0.0 62.8 jit_solution(17290531961734254882)
XLA Ops:
  0.0 0.0 copy-start.6
  0.0 0.7 %copy-done.6 = s32[128]{0:T(128)S(1)} copy-done((s32[128]{0:T(128)S(1)}, s32[128]{0:T(128)}, u32[]{:S(2)}) %copy-start.6) | copy-done | bytes 536
  0.7 0.0 copy-start.1
  0.7 1.0 %copy-done.1 = bf16[128,2048]{1,0:T(8,128)(2,1)S(1)} copy-done((bf16[128,2048]{1,0:T(8,128)(2,1)S(1)}, bf16[128,2048]{1,0:T(8,128)(2,1)}, u32[]{:S(2)}) %copy-start.1) | copy-done | bytes 524312
  1.7 0.0 copy-start.3
  1.7 1.0 %copy-done.3 = bf16[128,2048]{1,0:T(8,128)(2,1)S(1)} copy-done((bf16[128,2048]{1,0:T(8,128)(2,1)S(1)}, bf16[128,2048]{1,0:T(8,128)(2,1)}, u32[]{:S(2)}) %copy-start.3) | copy-done | bytes 524312
  2.7 0.7 %own_sums.3 = (f32[392,128]{1,0:T(8,128)S(1)}, f32[392,128]{1,0:T(8,128)S(1)}, f32[392,128]{1,0:T(8,128)S(1)}, f32[392,128]{1,0:T(8,128)S(1)}) custom-call(s32[1]{0:T(128)} %bitcast.me_ref, s32[1,128]{1,0:T(1,128)S(1)} %bitcast.2, bf16[128,2048]{1,0:T(8,128)(2,1)S(1)} %copy-done.1, bf16[128,2048]{1,0:T(8,128)(2,1)S(1)} %copy-done.3), custom_call_target="tpu_custom_call" | custom-call | flops 536870912 | tf_op jit(solution)/shard_map/own_sums/pallas_call | solution.py:207
  3.4 2.1 %collective-permute-start.8 = (f32[392,128]{1,0:T(8,128)S(1)}, f32[392,128]{1,0:T(8,128)S(1)}, u32[]{:S(2)}, u32[]{:S(2)}) collective-permute-start(f32[392,128]{1,0:T(8,128)S(1)} %get-tuple-element.30), channel_id=1, source_target_pairs={{0,1},{1,0},{2,3},{3,2},{4,5},{5,4},{6,7},{7,6},{8,9},{9,8},{10,11... | collective-permute-start | bytes 602120 | tf_op jit(solution)/shard_map/ppermute | solution.py:233
  5.5 1.3 %collective-permute-start.9 = (f32[392,128]{1,0:T(8,128)S(1)}, f32[392,128]{1,0:T(8,128)S(1)}, u32[]{:S(2)}, u32[]{:S(2)}) collective-permute-start(f32[392,128]{1,0:T(8,128)S(1)} %get-tuple-element.31), channel_id=1, source_target_pairs={{0,2},{1,3},{2,0},{3,1},{4,6},{5,7},{6,4},{7,5},{8,10},{9,11},{10,... | collective-permute-start | bytes 602120 | tf_op jit(solution)/shard_map/ppermute | solution.py:233
  6.8 0.0 collective-permute-start.10
  6.8 0.7 %own_sums.2 = (f32[392,128]{1,0:T(8,128)S(1)}, f32[392,128]{1,0:T(8,128)S(1)}, f32[392,128]{1,0:T(8,128)S(1)}, f32[392,128]{1,0:T(8,128)S(1)}) custom-call(s32[1]{0:T(128)} %bitcast.me_ref, s32[1,128]{1,0:T(1,128)S(1)} %bitcast.3, bf16[128,2048]{1,0:T(8,128)(2,1)S(1)} %copy-done.1, bf16[128,2048]{1,0:T(8,128)(2,1)S(1)} %copy-done.3), custom_call_target="tpu_custom_call" | custom-call | flops 536870912 | tf_op jit(solution)/shard_map/own_sums/pallas_call | solution.py:207
  7.5 1.4 %collective-permute-start = (f32[392,128]{1,0:T(8,128)S(1)}, f32[392,128]{1,0:T(8,128)S(1)}, u32[]{:S(2)}, u32[]{:S(2)}) collective-permute-start(f32[392,128]{1,0:T(8,128)S(1)} %get-tuple-element.22), channel_id=1, source_target_pairs={{0,1},{1,0},{2,3},{3,2},{4,5},{5,4},{6,7},{7,6},{8,9},{9,8},{10,11... | collective-permute-start | bytes 602120 | tf_op jit(solution)/shard_map/ppermute | solution.py:233
  8.9 1.3 %collective-permute-start.1 = (f32[392,128]{1,0:T(8,128)S(1)}, f32[392,128]{1,0:T(8,128)S(1)}, u32[]{:S(2)}, u32[]{:S(2)}) collective-permute-start(f32[392,128]{1,0:T(8,128)S(1)} %get-tuple-element.23), channel_id=1, source_target_pairs={{0,2},{1,3},{2,0},{3,1},{4,6},{5,7},{6,4},{7,5},{8,10},{9,11},{10,... | collective-permute-start | bytes 602120 | tf_op jit(solution)/shard_map/ppermute | solution.py:233
  10.2 0.0 collective-permute-done.8.refs_1_
  10.2 2.2 %collective-permute-start.2 = (f32[392,128]{1,0:T(8,128)S(1)}, f32[392,128]{1,0:T(8,128)S(1)}, u32[]{:S(2)}, u32[]{:S(2)}) collective-permute-start(f32[392,128]{1,0:T(8,128)S(1)} %get-tuple-element.24), channel_id=1, source_target_pairs={{0,3},{1,2},{2,1},{3,0},{4,7},{5,6},{6,5},{7,4},{8,11},{9,10},{10,... | collective-permute-start | bytes 602120 | tf_op jit(solution)/shard_map/ppermute | solution.py:233
  12.4 0.0 collective-permute-done.9.refs_2_
  12.4 3.1 %collective-permute-done.10.refs_3_ = f32[392,128]{1,0:T(8,128)S(1)} collective-permute-done((f32[392,128]{1,0:T(8,128)S(1)}, f32[392,128]{1,0:T(8,128)S(1)}, u32[]{:S(2)}, u32[]{:S(2)}) %collective-permute-start.10) | collective-permute-done | bytes 200736 | tf_op jit(solution)/shard_map/ppermute | solution.py:233
  15.5 0.1 block_total.3
  15.6 4.1 %collective-permute-start.11 = (f32[392,128]{1,0:T(8,128)S(1)}, f32[392,128]{1,0:T(8,128)S(1)}, u32[]{:S(2)}, u32[]{:S(2)}) collective-permute-start(f32[392,128]{1,0:T(8,128)S(1)} %block_total.3), channel_id=1, source_target_pairs={{0,4},{4,8},{8,12},{12,16},{16,20},{20,24},{24,28},{1,5},{5,9},{9,... | collective-permute-start | bytes 602120 | tf_op jit(solution)/shard_map/ppermute | solution.py:238
  19.7 6.6 %collective-permute-start.12 = (f32[392,128]{1,0:T(8,128)S(1)}, f32[392,128]{1,0:T(8,128)S(1)}, u32[]{:S(2)}, u32[]{:S(2)}) collective-permute-start(f32[392,128]{1,0:T(8,128)S(1)} %block_total.3), channel_id=1, source_target_pairs={{0,8},{4,12},{8,16},{12,20},{16,24},{20,28},{1,9},{5,13},{9,17},{1... | collective-permute-start | bytes 602120 | tf_op jit(solution)/shard_map/ppermute | solution.py:238
  26.3 0.0 collective-permute-done.refs_1_
  26.3 0.0 collective-permute-done.1.refs_2_
  26.3 0.0 collective-permute-done.2.refs_3_
  26.4 0.1 block_total.2
  26.4 4.0 %collective-permute-start.3 = (f32[392,128]{1,0:T(8,128)S(1)}, f32[392,128]{1,0:T(8,128)S(1)}, u32[]{:S(2)}, u32[]{:S(2)}) collective-permute-start(f32[392,128]{1,0:T(8,128)S(1)} %block_total.2), channel_id=1, source_target_pairs={{0,4},{4,8},{8,12},{12,16},{16,20},{20,24},{24,28},{1,5},{5,9},{9,... | collective-permute-start | bytes 602120 | tf_op jit(solution)/shard_map/ppermute | solution.py:238
  30.4 5.4 %collective-permute-start.4 = (f32[392,128]{1,0:T(8,128)S(1)}, f32[392,128]{1,0:T(8,128)S(1)}, u32[]{:S(2)}, u32[]{:S(2)}) collective-permute-start(f32[392,128]{1,0:T(8,128)S(1)} %block_total.2), channel_id=1, source_target_pairs={{0,8},{4,12},{8,16},{12,20},{16,24},{20,28},{1,9},{5,13},{9,17},{1... | collective-permute-start | bytes 602120 | tf_op jit(solution)/shard_map/ppermute | solution.py:238
  35.8 0.0 collective-permute-done.11.refs_4_
  35.9 0.0 collective-permute-done.12.refs_5_
  35.9 0.0 copy-start.4
  35.9 0.3 prefixes.3
  36.2 0.1 collective-permute-start.13
  36.2 3.4 %collective-permute-start.14 = (f32[392,128]{1,0:T(8,128)S(1)}, f32[392,128]{1,0:T(8,128)S(1)}, u32[]{:S(2)}, u32[]{:S(2)}) collective-permute-start(f32[392,128]{1,0:T(8,128)S(1)} %get-tuple-element.35), channel_id=1, source_target_pairs={{0,2},{1,3},{2,0},{3,1},{4,6},{5,7},{6,4},{7,5},{8,10},{9,11},{10,... | collective-permute-start | bytes 602120 | tf_op jit(solution)/shard_map/ppermute | solution.py:233
  39.6 0.0 copy-start
  39.6 0.0 copy-start.2
  39.6 0.0 collective-permute-start.15
  39.6 2.3 %collective-permute-done.3.refs_4_ = f32[392,128]{1,0:T(8,128)S(1)} collective-permute-done((f32[392,128]{1,0:T(8,128)S(1)}, f32[392,128]{1,0:T(8,128)S(1)}, u32[]{:S(2)}, u32[]{:S(2)}) %collective-permute-start.3) | collective-permute-done | bytes 200736 | tf_op jit(solution)/shard_map/ppermute | solution.py:238
  41.9 0.0 collective-permute-done.4.refs_5_
  41.9 0.3 prefixes.2
  42.2 0.1 collective-permute-start.5
  42.3 0.3 collective-permute-start.6
  42.6 0.0 collective-permute-done.13.refs_1_
  42.6 0.0 copy-start.5
  42.6 2.8 %collective-permute-start.7 = (f32[392,128]{1,0:T(8,128)S(1)}, f32[392,128]{1,0:T(8,128)S(1)}, u32[]{:S(2)}, u32[]{:S(2)}) collective-permute-start(f32[392,128]{1,0:T(8,128)S(1)} %get-tuple-element.28), channel_id=1, source_target_pairs={{0,3},{1,2},{2,1},{3,0},{4,7},{5,6},{6,5},{7,4},{8,11},{9,10},{10,... | collective-permute-start | bytes 602120 | tf_op jit(solution)/shard_map/ppermute | solution.py:233
  45.4 1.5 %collective-permute-done.14.refs_2_ = f32[392,128]{1,0:T(8,128)S(1)} collective-permute-done((f32[392,128]{1,0:T(8,128)S(1)}, f32[392,128]{1,0:T(8,128)S(1)}, u32[]{:S(2)}, u32[]{:S(2)}) %collective-permute-start.14) | collective-permute-done | bytes 200736 | tf_op jit(solution)/shard_map/ppermute | solution.py:233
  46.9 4.1 %collective-permute-done.15.refs_3_ = f32[392,128]{1,0:T(8,128)S(1)} collective-permute-done((f32[392,128]{1,0:T(8,128)S(1)}, f32[392,128]{1,0:T(8,128)S(1)}, u32[]{:S(2)}, u32[]{:S(2)}) %collective-permute-start.15) | collective-permute-done | bytes 200736 | tf_op jit(solution)/shard_map/ppermute | solution.py:233
  51.1 0.0 copy-done.4
  51.1 0.0 copy-done
  51.1 0.0 copy-done.2
  51.1 0.0 copy-done.5
  51.1 4.2 %solve.2.refs_4_ = f32[128,2048]{1,0:T(8,128)} custom-call(s32[1]{0:T(128)} %bitcast.me_ref, f32[16]{0:T(128)S(1)} %copy-done.5, s32[1,128]{1,0:T(1,128)S(1)} %bitcast.4, bf16[128,2048]{1,0:T(8,128)(2,1)S(1)} %copy-done, bf16[128,2048]{1,0:T(8,128)(2,1)S(1)} %copy-done.2, bf16[128,2048]{1,0:T(8,128)(2,1)S(1)} %copy-done.4, ...), custom_call_target="tpu_custom_call" | custom-call | flops 4294967296 | tf_op jit(solution)/shard_map/solve/pallas_call | solution.py:207
  55.3 0.0 collective-permute-done.5.refs_1_
  55.3 0.2 collective-permute-done.6.refs_2_
  55.5 3.0 %collective-permute-done.7.refs_3_ = f32[392,128]{1,0:T(8,128)S(1)} collective-permute-done((f32[392,128]{1,0:T(8,128)S(1)}, f32[392,128]{1,0:T(8,128)S(1)}, u32[]{:S(2)}, u32[]{:S(2)}) %collective-permute-start.7) | collective-permute-done | bytes 200736 | tf_op jit(solution)/shard_map/ppermute | solution.py:233
  58.6 4.2 %solve.3 = f32[128,2048]{1,0:T(8,128)} custom-call(s32[1]{0:T(128)} %bitcast.me_ref, f32[16]{0:T(128)S(1)} %copy-done.5, s32[1,128]{1,0:T(1,128)S(1)} %bitcast.5, bf16[128,2048]{1,0:T(8,128)(2,1)S(1)} %copy-done, bf16[128,2048]{1,0:T(8,128)(2,1)S(1)} %copy-done.2, bf16[128,2048]{1,0:T(8,128)(2,1)S(1)} %copy-done.4, ...), custom_call_target="tpu_custom_call", output_to_operand_aliasing={{}: (10, {})} | custom-call | flops 4294967296 | tf_op jit(solution)/shard_map/solve/pallas_call | solution.py:207
Async XLA Ops:
  0.0 0.7 %copy-start.6 = (s32[128]{0:T(128)S(1)}, s32[128]{0:T(128)}, u32[]{:S(2)}) copy-start(s32[128]{0:T(128)} %param.8) | copy-start | bytes 1540
  0.7 1.0 %copy-start.1 = (bf16[128,2048]{1,0:T(8,128)(2,1)S(1)}, bf16[128,2048]{1,0:T(8,128)(2,1)}, u32[]{:S(2)}) copy-start(bf16[128,2048]{1,0:T(8,128)(2,1)} %k_ref.7) | copy-start | bytes 1572868
  1.7 1.0 %copy-start.3 = (bf16[128,2048]{1,0:T(8,128)(2,1)S(1)}, bf16[128,2048]{1,0:T(8,128)(2,1)}, u32[]{:S(2)}) copy-start(bf16[128,2048]{1,0:T(8,128)(2,1)} %v_ref.7) | copy-start | bytes 1572868
  3.4 6.8 %collective-permute-start.8 = (f32[392,128]{1,0:T(8,128)S(1)}, f32[392,128]{1,0:T(8,128)S(1)}, u32[]{:S(2)}, u32[]{:S(2)}) collective-permute-start(f32[392,128]{1,0:T(8,128)S(1)} %get-tuple-element.30), channel_id=1, source_target_pairs={{0,1},{1,0},{2,3},{3,2},{4,5},{5,4},{6,7},{7,6},{8,9},{9,8},{10,11... | collective-permute-start | bytes 602120 | tf_op jit(solution)/shard_map/ppermute | solution.py:233
  5.5 6.9 %collective-permute-start.9 = (f32[392,128]{1,0:T(8,128)S(1)}, f32[392,128]{1,0:T(8,128)S(1)}, u32[]{:S(2)}, u32[]{:S(2)}) collective-permute-start(f32[392,128]{1,0:T(8,128)S(1)} %get-tuple-element.31), channel_id=1, source_target_pairs={{0,2},{1,3},{2,0},{3,1},{4,6},{5,7},{6,4},{7,5},{8,10},{9,11},{10,... | collective-permute-start | bytes 602120 | tf_op jit(solution)/shard_map/ppermute | solution.py:233
  6.8 8.7 %collective-permute-start.10 = (f32[392,128]{1,0:T(8,128)S(1)}, f32[392,128]{1,0:T(8,128)S(1)}, u32[]{:S(2)}, u32[]{:S(2)}) collective-permute-start(f32[392,128]{1,0:T(8,128)S(1)} %get-tuple-element.32), channel_id=1, source_target_pairs={{0,3},{1,2},{2,1},{3,0},{4,7},{5,6},{6,5},{7,4},{8,11},{9,10},{10,... | collective-permute-start | bytes 602120 | tf_op jit(solution)/shard_map/ppermute | solution.py:233
  7.5 18.8 %collective-permute-start = (f32[392,128]{1,0:T(8,128)S(1)}, f32[392,128]{1,0:T(8,128)S(1)}, u32[]{:S(2)}, u32[]{:S(2)}) collective-permute-start(f32[392,128]{1,0:T(8,128)S(1)} %get-tuple-element.22), channel_id=1, source_target_pairs={{0,1},{1,0},{2,3},{3,2},{4,5},{5,4},{6,7},{7,6},{8,9},{9,8},{10,11... | collective-permute-start | bytes 602120 | tf_op jit(solution)/shard_map/ppermute | solution.py:233
  8.9 17.4 %collective-permute-start.1 = (f32[392,128]{1,0:T(8,128)S(1)}, f32[392,128]{1,0:T(8,128)S(1)}, u32[]{:S(2)}, u32[]{:S(2)}) collective-permute-start(f32[392,128]{1,0:T(8,128)S(1)} %get-tuple-element.23), channel_id=1, source_target_pairs={{0,2},{1,3},{2,0},{3,1},{4,6},{5,7},{6,4},{7,5},{8,10},{9,11},{10,... | collective-permute-start | bytes 602120 | tf_op jit(solution)/shard_map/ppermute | solution.py:233
  10.2 16.1 %collective-permute-start.2 = (f32[392,128]{1,0:T(8,128)S(1)}, f32[392,128]{1,0:T(8,128)S(1)}, u32[]{:S(2)}, u32[]{:S(2)}) collective-permute-start(f32[392,128]{1,0:T(8,128)S(1)} %get-tuple-element.24), channel_id=1, source_target_pairs={{0,3},{1,2},{2,1},{3,0},{4,7},{5,6},{6,5},{7,4},{8,11},{9,10},{10,... | collective-permute-start | bytes 602120 | tf_op jit(solution)/shard_map/ppermute | solution.py:233
  15.6 20.2 %collective-permute-start.11 = (f32[392,128]{1,0:T(8,128)S(1)}, f32[392,128]{1,0:T(8,128)S(1)}, u32[]{:S(2)}, u32[]{:S(2)}) collective-permute-start(f32[392,128]{1,0:T(8,128)S(1)} %block_total.3), channel_id=1, source_target_pairs={{0,4},{4,8},{8,12},{12,16},{16,20},{20,24},{24,28},{1,5},{5,9},{9,... | collective-permute-start | bytes 602120 | tf_op jit(solution)/shard_map/ppermute | solution.py:238
  19.7 16.2 %collective-permute-start.12 = (f32[392,128]{1,0:T(8,128)S(1)}, f32[392,128]{1,0:T(8,128)S(1)}, u32[]{:S(2)}, u32[]{:S(2)}) collective-permute-start(f32[392,128]{1,0:T(8,128)S(1)} %block_total.3), channel_id=1, source_target_pairs={{0,8},{4,12},{8,16},{12,20},{16,24},{20,28},{1,9},{5,13},{9,17},{1... | collective-permute-start | bytes 602120 | tf_op jit(solution)/shard_map/ppermute | solution.py:238
  26.4 15.5 %collective-permute-start.3 = (f32[392,128]{1,0:T(8,128)S(1)}, f32[392,128]{1,0:T(8,128)S(1)}, u32[]{:S(2)}, u32[]{:S(2)}) collective-permute-start(f32[392,128]{1,0:T(8,128)S(1)} %block_total.2), channel_id=1, source_target_pairs={{0,4},{4,8},{8,12},{12,16},{16,20},{20,24},{24,28},{1,5},{5,9},{9,... | collective-permute-start | bytes 602120 | tf_op jit(solution)/shard_map/ppermute | solution.py:238
  30.4 11.5 %collective-permute-start.4 = (f32[392,128]{1,0:T(8,128)S(1)}, f32[392,128]{1,0:T(8,128)S(1)}, u32[]{:S(2)}, u32[]{:S(2)}) collective-permute-start(f32[392,128]{1,0:T(8,128)S(1)} %block_total.2), channel_id=1, source_target_pairs={{0,8},{4,12},{8,16},{12,20},{16,24},{20,28},{1,9},{5,13},{9,17},{1... | collective-permute-start | bytes 602120 | tf_op jit(solution)/shard_map/ppermute | solution.py:238
  35.9 15.2 %copy-start.4 = (bf16[128,2048]{1,0:T(8,128)(2,1)S(1)}, bf16[128,2048]{1,0:T(8,128)(2,1)}, u32[]{:S(2)}) copy-start(bf16[128,2048]{1,0:T(8,128)(2,1)} %v_ref.7) | copy-start | bytes 1572868
  36.2 6.5 %collective-permute-start.13 = (f32[392,128]{1,0:T(8,128)S(1)}, f32[392,128]{1,0:T(8,128)S(1)}, u32[]{:S(2)}, u32[]{:S(2)}) collective-permute-start(f32[392,128]{1,0:T(8,128)S(1)} %get-tuple-element.34), channel_id=1, source_target_pairs={{0,1},{1,0},{2,3},{3,2},{4,5},{5,4},{6,7},{7,6},{8,9},{9,8},{10,11... | collective-permute-start | bytes 602120 | tf_op jit(solution)/shard_map/ppermute | solution.py:233
  36.2 10.7 %collective-permute-start.14 = (f32[392,128]{1,0:T(8,128)S(1)}, f32[392,128]{1,0:T(8,128)S(1)}, u32[]{:S(2)}, u32[]{:S(2)}) collective-permute-start(f32[392,128]{1,0:T(8,128)S(1)} %get-tuple-element.35), channel_id=1, source_target_pairs={{0,2},{1,3},{2,0},{3,1},{4,6},{5,7},{6,4},{7,5},{8,10},{9,11},{10,... | collective-permute-start | bytes 602120 | tf_op jit(solution)/shard_map/ppermute | solution.py:233
  39.6 11.4 %copy-start = (bf16[128,2048]{1,0:T(8,128)(2,1)S(1)}, bf16[128,2048]{1,0:T(8,128)(2,1)}, u32[]{:S(2)}) copy-start(bf16[128,2048]{1,0:T(8,128)(2,1)} %q_ref.3) | copy-start | bytes 1572868
  39.6 11.4 %copy-start.2 = (bf16[128,2048]{1,0:T(8,128)(2,1)S(1)}, bf16[128,2048]{1,0:T(8,128)(2,1)}, u32[]{:S(2)}) copy-start(bf16[128,2048]{1,0:T(8,128)(2,1)} %k_ref.7) | copy-start | bytes 1572868
  39.6 11.4 %collective-permute-start.15 = (f32[392,128]{1,0:T(8,128)S(1)}, f32[392,128]{1,0:T(8,128)S(1)}, u32[]{:S(2)}, u32[]{:S(2)}) collective-permute-start(f32[392,128]{1,0:T(8,128)S(1)} %get-tuple-element.36), channel_id=1, source_target_pairs={{0,3},{1,2},{2,1},{3,0},{4,7},{5,6},{6,5},{7,4},{8,11},{9,10},{10,... | collective-permute-start | bytes 602120 | tf_op jit(solution)/shard_map/ppermute | solution.py:233
  42.2 13.1 %collective-permute-start.5 = (f32[392,128]{1,0:T(8,128)S(1)}, f32[392,128]{1,0:T(8,128)S(1)}, u32[]{:S(2)}, u32[]{:S(2)}) collective-permute-start(f32[392,128]{1,0:T(8,128)S(1)} %get-tuple-element.26), channel_id=1, source_target_pairs={{0,1},{1,0},{2,3},{3,2},{4,5},{5,4},{6,7},{7,6},{8,9},{9,8},{10,11... | collective-permute-start | bytes 602120 | tf_op jit(solution)/shard_map/ppermute | solution.py:233
  42.3 13.2 %collective-permute-start.6 = (f32[392,128]{1,0:T(8,128)S(1)}, f32[392,128]{1,0:T(8,128)S(1)}, u32[]{:S(2)}, u32[]{:S(2)}) collective-permute-start(f32[392,128]{1,0:T(8,128)S(1)} %get-tuple-element.27), channel_id=1, source_target_pairs={{0,2},{1,3},{2,0},{3,1},{4,6},{5,7},{6,4},{7,5},{8,10},{9,11},{10,... | collective-permute-start | bytes 602120 | tf_op jit(solution)/shard_map/ppermute | solution.py:233
  42.6 8.4 %copy-start.5 = (f32[16]{0:T(128)S(1)}, f32[16]{0:T(128)}, u32[]{:S(2)}) copy-start(f32[16]{0:T(128)} %ridge_ref.3) | copy-start | bytes 196
  42.6 15.9 %collective-permute-start.7 = (f32[392,128]{1,0:T(8,128)S(1)}, f32[392,128]{1,0:T(8,128)S(1)}, u32[]{:S(2)}, u32[]{:S(2)}) collective-permute-start(f32[392,128]{1,0:T(8,128)S(1)} %get-tuple-element.28), channel_id=1, source_target_pairs={{0,3},{1,2},{2,1},{3,0},{4,7},{5,6},{6,5},{7,4},{8,11},{9,10},{10,... | collective-permute-start | bytes 602120 | tf_op jit(solution)/shard_map/ppermute | solution.py:233

commit v4 on v3

--- a/solution.py
+++ b/solution.py
@@ -42,37 +42,48 @@
     return jnp.broadcast_to(ids, (count, count)).T[:, :1]
 
 
-def last_weight(ids_ref, width):
-    ids = ids_ref[...].astype(jnp.float32)
-    newest = jnp.max(ids, 1, keepdims=True)
-    weight = (down(ids) == newest).astype(jnp.float32)
-    return ids, newest, jnp.broadcast_to(weight, (ids.shape[1], width))
-
-
 def row_scale(wide):
     return lax.rsqrt(jnp.sum(wide * wide, -1, keepdims=True) + 1e-06)
 
 
 def own_kernel(base, width, pairs, count, me_ref, ids_ref, k_ref, v_ref, *refs):
-    outs = refs[-count:]
+    outs, scratch = refs[:count], refs[count:]
+    span = pairs * 2 * width
+    spans = [pl.ds(pl.multiple_of(base * width + (me_ref[0] ^ slot) * span, span), span) for slot in range(count)]
+    copies = []
+    if scratch:
+        ids_to, k_to, v_to, sems = scratch
+        moves = [(ids_ref, ids_to)]
+        for slot in range(count):
+            moves += [(k_ref.at[:, spans[slot]], k_to.at[slot]), (v_ref.at[:, spans[slot]], v_to.at[slot])]
+        copies = [pltpu.make_async_copy(*move, sems.at[number]) for number, move in enumerate(moves)]
+        for copy in copies:
+            copy.start()
+        ids_ref, k_parts, v_parts = ids_to, [k_to.at[slot] for slot in range(count)], [v_to.at[slot] for slot in range(count)]
+    else:
+        k_parts, v_parts = ([ref.at[:, one] for one in spans] for ref in (k_ref, v_ref))
     upper, diagonal = triangle(width)
-    ids, newest, weight = last_weight(ids_ref, width)
-    oldest = jnp.min(ids, 1, keepdims=True)
+    for copy in copies[:1]:
+        copy.wait()
+    ids = ids_ref[...].astype(jnp.float32)
+    oldest, newest = jnp.min(ids, 1, keepdims=True), jnp.max(ids, 1, keepdims=True)
+    weight = jnp.broadcast_to((down(ids) == newest).astype(jnp.float32), (ids.shape[1], width))
     marks = [jnp.broadcast_to(one + 1.0, (1, width)) for one in (oldest, newest)]
     filler = jnp.zeros((EXTRA - 3, width), jnp.float32)
     for slot, out in enumerate(outs):
+        for copy in copies[1 + 2 * slot : 3 + 2 * slot]:
+            copy.wait()
         for pair in range(pairs):
             top = pair * (3 * width + EXTRA)
             grams = []
             for side in range(2):
-                head = base + ((me_ref[0] ^ slot) * pairs + pair) * 2 + side
-                lanes = pl.ds(pl.multiple_of(head * width, width), width)
-                keys = k_ref[:, lanes]
+                lanes = pl.ds((pair * 2 + side) * width, width)
+                keys = k_parts[slot][:, lanes]
                 wide = keys.astype(jnp.float32)
                 scale = row_scale(wide)
                 light = weight * scale
                 k_high, k_low = split(light * scale * wide)
-                v_high, v_low = split(light * v_ref[:, lanes].astype(jnp.float32))
+                v_high, v_low = split(light * v_parts[slot][:, lanes].astype(jnp.float32))
                 right = jnp.concatenate(
                     [jnp.concatenate([k_high, v_high], 1), jnp.concatenate([k_low, v_low], 1)], 0
                 )
@@ -115,8 +126,8 @@
         out[...] = total(terms)
 
 
-def solve_kernel(base, width, pairs, count, me_ref, ridge_ref, ids_ref, q_ref, k_ref, v_ref, *refs):
-    slots, out = refs[:count], refs[-1]
+def solve_kernel(places, width, pairs, me_ref, ridge_ref, ids_ref, q_ref, k_ref, v_ref, *refs):
+    slots, (out_hbm, out, sems) = refs[: len(places)], refs[-3:]
     upper, diagonal = triangle(width)
     ids = ids_ref[...].astype(jnp.float32)
     column = down(ids)
@@ -127,7 +138,7 @@
     within = jnp.where(row_at >= col_at, (column == ids).astype(jnp.float32), 0.0)
 
     group = []
-    for slot, state in enumerate(slots):
+    for (base, slot), state in zip(places, slots):
         for pair in range(pairs):
             top = pair * (3 * width + EXTRA)
             packed = state[pl.ds(top, width), :]
@@ -138,8 +149,7 @@
                 jnp.where(diagonal, second, jnp.where(upper, flipped, packed)),
             ]
             for side in range(2):
-                local = ((me_ref[0] ^ slot) * pairs + pair) * 2 + side
-                head = base + local
+                head = base + ((me_ref[0] ^ slot) * pairs + pair) * 2 + side
                 lanes = pl.ds(pl.multiple_of(head * width, width), width)
                 wide = q_ref[:, lanes].astype(jnp.float32)
                 query = wide * row_scale(wide)
@@ -152,7 +162,6 @@
                 group.append(
                     dict(
                         lanes=lanes,
-                        place=pl.ds(pl.multiple_of(local * width, width), width),
                         cross=state.at[pl.ds(top + EXTRA + (1 + side) * width, width)],
                         both=jnp.concatenate([both, both], 0),
                         low=low,
@@ -190,15 +199,20 @@
         wide = dot(jnp.concatenate([high, low], 1), jnp.concatenate([both, both], 0))
         h["state"] = wide[:, :width] + dot(high, c_low)
         h["score"] = split(wide[:, width:] * h["once"])
-    for h in group:
+    copies = []
+    for number, h in enumerate(group):
         values = v_ref[:, h["lanes"]]
         local = dot(jnp.concatenate(h["score"], 1), jnp.concatenate([values, values], 0))
-        out[:, h["place"]] = h["state"] * carried + local
+        out[number] = h["state"] * carried + local
+        copies.append(pltpu.make_async_copy(out.at[number], out_hbm.at[:, h["lanes"]], sems.at[number]))
+        copies[-1].start()
+    for copy in copies:
+        copy.wait()
 
 
 VMEM = pl.BlockSpec(memory_space=pltpu.VMEM)
 SMEM = pl.BlockSpec(memory_space=pltpu.SMEM)
-ANY = pl.BlockSpec(memory_space=pl.ANY)
+HBM = pl.BlockSpec(memory_space=pltpu.HBM)
 PARAMS = pltpu.CompilerParams(vmem_limit_bytes=40 * 1024 * 1024)
 
 
@@ -235,19 +249,29 @@
 
     def onward(value):
         return [
-            lax.ppermute(value, ("outer", "half"), [(i, i + step) for i in range(blocks - step)])
+            lax.ppermute(value, ("outer", "half"), [(i, (i + step) % blocks) for i in range(blocks)])
             for step in range(1, steps + 1)
         ]
 
     states = []
+    tokens = (ids, key_vectors, value_vectors)
+    part = (near, row_count, 2 * pairs * width)
     for piece in range(pieces):
+        first = piece == 0
+        scratch = [
+            pltpu.VMEM(ids.shape, ids.dtype),
+            pltpu.VMEM(part, key_vectors.dtype),
+            pltpu.VMEM(part, value_vectors.dtype),
+            pltpu.SemaphoreType.DMA((2 * near + 1,)),
+        ]
         own = call(
             functools.partial(own_kernel, piece * pairs * near * 2, width, pairs, near),
             "own_sums",
             unit,
             [shape] * near,
-            [SMEM, VMEM, VMEM, VMEM],
-            (me, ids, key_vectors, value_vectors),
+            [SMEM] + [HBM if first else VMEM] * 3,
+            (me, *[pltpu.with_memory_space_constraint(one, pltpu.HBM) if first else one for one in tokens]),
+            scratch_shapes=scratch if first else [],
         )
         slots = exchange(own)
         block_total = call(
@@ -264,24 +288,24 @@
         states.append(exchange(prefix))
     out = None
     for piece, state in enumerate(states):
-        base = piece * pairs * near * 2
-        span = pairs * near * 2 * width
+        places = [(piece * pairs * near * 2, slot) for slot in range(near)]
         arguments = [me, ridge_weight, ids, queries, key_vectors, value_vectors, *state]
         in_specs = [SMEM, SMEM, VMEM, VMEM, VMEM, VMEM] + [VMEM] * near
         aliases = {}
         if out is not None:
             aliases = {len(arguments): 0}
             arguments.append(out)
-            in_specs.append(ANY)
+            in_specs.append(HBM)
+        count = 2 * pairs * near
         out = call(
-            functools.partial(solve_kernel, base, width, pairs, near),
+            functools.partial(solve_kernel, places, width, pairs),
             "solve",
             8 * unit,
             jax.ShapeDtypeStruct((row_count, columns), jnp.float32),
             in_specs,
             arguments,
-            grid=(1,),
-            out_specs=pl.BlockSpec((row_count, span), functools.partial(lambda p, i: (0, p), piece)),
+            out_specs=HBM,
+            scratch_shapes=[pltpu.VMEM((count, row_count, width), jnp.float32), pltpu.SemaphoreType.DMA((count,))],
             input_output_aliases=aliases,
         )
     return out

time: 63.3 us -> 60.9 us (0.962)
  starting transfers between devices: 35 us -> 27.2 us
  waiting for transfers between devices: 14.4 us -> 21.6 us
  local copies, waits for them, and re-layouts: 2.75 us -> 0.02 us
  Pallas kernels: 10.5 us -> 11.9 us
    ppermute x4, starting transfers between devices: 20.1 us -> 12.8 us  [onward(): lax.ppermute(value, ('outer', 'half'), [(i, (i + step) % blocks) for i in...]
    ppermute x12, waiting for transfers between devices: 12 us -> 17.4 us  [exchange(): lax.ppermute(slots[j], 'near', [(i, i ^ j) for i in range(near)])]
    unnamed x14 -> x10, local copies, waits for them, and re-layouts: 2.75 us -> 0.02 us
    ppermute x4, waiting for transfers between devices: 2.32 us -> 4.17 us  [onward(): lax.ppermute(value, ('outer', 'half'), [(i, (i + step) % blocks) for i in...]
    pallas_call x8, Pallas kernels: 10.5 us -> 11.9 us  [call(): pl.pallas_call(kernel, out_shape=out_shape, in_specs=in_specs, compiler_p...]
  transfers between devices with their start and end apart: 16 -> 16, of which waited for: 6 -> 7; matrix products, arithmetic and copies ran while one was open for 0% -> 0% of each run, Pallas kernels for 9% -> 9%
where the time goes in v4:
time: 60.9 us; the launch traced here: 60.7 us
  starting transfers between devices  27.2 us (45%)
  waiting for transfers between devices  21.6 us (35%)
  Pallas kernels  11.9 us (20%)
    ppermute x12, waiting for transfers between devices, exchange(): lax.ppermute(slots[j], 'near', [(i, i ^ j) for i in range(near)])  17.4 us
    ppermute x12, starting transfers between devices, exchange(): lax.ppermute(slots[j], 'near', [(i, i ^ j) for i in range(near)])  14.4 us
    ppermute x4, starting transfers between devices, onward(): lax.ppermute(value, ('outer', 'half'), [(i, (i + step) % blocks) for i in...  12.8 us
    pallas_call x8, Pallas kernels, call(): pl.pallas_call(kernel, out_shape=out_shape, in_specs=in_specs, compiler_p...  11.9 us
    ppermute x4, waiting for transfers between devices, onward(): lax.ppermute(value, ('outer', 'half'), [(i, (i + step) % blocks) for i in...  4.17 us
  transfers between devices with their start and end apart: 16, of which 7 were waited for; matrix products, arithmetic and copies ran while one was open for 0% of the time, Pallas kernels for 9%

profile of v4, /device:TPU:1, one launch (start us, length us, event | category | flops | bytes accessed | tf_op | source)
XLA Modules:
  0.0 60.7 jit_solution(5722668262647495202)
XLA Ops:
  0.0 0.0 copy-start.1
  0.0 0.0 copy-start.2
  0.0 2.2 %own_sums.3 = (f32[392,128]{1,0:T(8,128)S(1)}, f32[392,128]{1,0:T(8,128)S(1)}, f32[392,128]{1,0:T(8,128)S(1)}, f32[392,128]{1,0:T(8,128)S(1)}) custom-call(s32[1]{0:T(128)} %bitcast.me_ref, s32[1,128]{1,0:T(1,128)} %bitcast.2, bf16[128,2048]{1,0:T(8,128)(2,1)} %k_ref.7, bf16[128,2048]{1,0:T(8,128)(2,1)} %v_ref.7), custom_call_target="tpu_custom_call" | custom-call | flops 536870912 | tf_op jit(solution)/shard_map/own_sums/pallas_call | solution.py:221
  2.3 2.1 %collective-permute-start.8 = (f32[392,128]{1,0:T(8,128)S(1)}, f32[392,128]{1,0:T(8,128)S(1)}, u32[]{:S(2)}, u32[]{:S(2)}) collective-permute-start(f32[392,128]{1,0:T(8,128)S(1)} %get-tuple-element.30), channel_id=1, source_target_pairs={{0,1},{1,0},{2,3},{3,2},{4,5},{5,4},{6,7},{7,6},{8,9},{9,8},{10,11... | collective-permute-start | bytes 602120 | tf_op jit(solution)/shard_map/ppermute | solution.py:247
  4.4 0.0 copy-start.4
  4.4 1.3 %collective-permute-start.9 = (f32[392,128]{1,0:T(8,128)S(1)}, f32[392,128]{1,0:T(8,128)S(1)}, u32[]{:S(2)}, u32[]{:S(2)}) collective-permute-start(f32[392,128]{1,0:T(8,128)S(1)} %get-tuple-element.31), channel_id=1, source_target_pairs={{0,2},{1,3},{2,0},{3,1},{4,6},{5,7},{6,4},{7,5},{8,10},{9,11},{10,... | collective-permute-start | bytes 602120 | tf_op jit(solution)/shard_map/ppermute | solution.py:247
  5.7 0.0 collective-permute-start.10
  5.7 0.0 copy-done.1
  5.7 0.0 copy-done.2
  5.7 0.0 copy-done.4
  5.7 0.7 %own_sums.2 = (f32[392,128]{1,0:T(8,128)S(1)}, f32[392,128]{1,0:T(8,128)S(1)}, f32[392,128]{1,0:T(8,128)S(1)}, f32[392,128]{1,0:T(8,128)S(1)}) custom-call(s32[1]{0:T(128)} %bitcast.me_ref, s32[1,128]{1,0:T(1,128)S(1)} %bitcast.3, bf16[128,2048]{1,0:T(8,128)(2,1)S(1)} %copy-done.1, bf16[128,2048]{1,0:T(8,128)(2,1)S(1)} %copy-done.2), custom_call_target="tpu_custom_call" | custom-call | flops 536870912 | tf_op jit(solution)/shard_map/own_sums/pallas_call | solution.py:221
  6.3 1.4 %collective-permute-start = (f32[392,128]{1,0:T(8,128)S(1)}, f32[392,128]{1,0:T(8,128)S(1)}, u32[]{:S(2)}, u32[]{:S(2)}) collective-permute-start(f32[392,128]{1,0:T(8,128)S(1)} %get-tuple-element.22), channel_id=1, source_target_pairs={{0,1},{1,0},{2,3},{3,2},{4,5},{5,4},{6,7},{7,6},{8,9},{9,8},{10,11... | collective-permute-start | bytes 602120 | tf_op jit(solution)/shard_map/ppermute | solution.py:247
  7.8 1.3 %collective-permute-start.1 = (f32[392,128]{1,0:T(8,128)S(1)}, f32[392,128]{1,0:T(8,128)S(1)}, u32[]{:S(2)}, u32[]{:S(2)}) collective-permute-start(f32[392,128]{1,0:T(8,128)S(1)} %get-tuple-element.23), channel_id=1, source_target_pairs={{0,2},{1,3},{2,0},{3,1},{4,6},{5,7},{6,4},{7,5},{8,10},{9,11},{10,... | collective-permute-start | bytes 602120 | tf_op jit(solution)/shard_map/ppermute | solution.py:247
  9.0 0.0 collective-permute-done.8.refs_1_
  9.1 2.2 %collective-permute-start.2 = (f32[392,128]{1,0:T(8,128)S(1)}, f32[392,128]{1,0:T(8,128)S(1)}, u32[]{:S(2)}, u32[]{:S(2)}) collective-permute-start(f32[392,128]{1,0:T(8,128)S(1)} %get-tuple-element.24), channel_id=1, source_target_pairs={{0,3},{1,2},{2,1},{3,0},{4,7},{5,6},{6,5},{7,4},{8,11},{9,10},{10,... | collective-permute-start | bytes 602120 | tf_op jit(solution)/shard_map/ppermute | solution.py:247
  11.2 0.0 collective-permute-done.9.refs_2_
  11.2 3.1 %collective-permute-done.10.refs_3_ = f32[392,128]{1,0:T(8,128)S(1)} collective-permute-done((f32[392,128]{1,0:T(8,128)S(1)}, f32[392,128]{1,0:T(8,128)S(1)}, u32[]{:S(2)}, u32[]{:S(2)}) %collective-permute-start.10) | collective-permute-done | bytes 200736 | tf_op jit(solution)/shard_map/ppermute | solution.py:247
  14.4 0.1 block_total.3
  14.4 2.2 %collective-permute-start.11 = (f32[392,128]{1,0:T(8,128)S(1)}, f32[392,128]{1,0:T(8,128)S(1)}, u32[]{:S(2)}, u32[]{:S(2)}) collective-permute-start(f32[392,128]{1,0:T(8,128)S(1)} %block_total.3), channel_id=1, source_target_pairs={{0,4},{4,8},{8,12},{12,16},{16,20},{20,24},{24,28},{28,0},{1,5},{5... | collective-permute-start | bytes 602120 | tf_op jit(solution)/shard_map/ppermute | solution.py:252
  16.7 4.7 %collective-permute-start.12 = (f32[392,128]{1,0:T(8,128)S(1)}, f32[392,128]{1,0:T(8,128)S(1)}, u32[]{:S(2)}, u32[]{:S(2)}) collective-permute-start(f32[392,128]{1,0:T(8,128)S(1)} %block_total.3), channel_id=1, source_target_pairs={{0,8},{4,12},{8,16},{12,20},{16,24},{20,28},{24,0},{28,4},{1,9},{5... | collective-permute-start | bytes 602120 | tf_op jit(solution)/shard_map/ppermute | solution.py:252
  21.4 0.0 collective-permute-done.refs_1_
  21.4 0.0 collective-permute-done.1.refs_2_
  21.4 4.6 %collective-permute-done.2.refs_3_ = f32[392,128]{1,0:T(8,128)S(1)} collective-permute-done((f32[392,128]{1,0:T(8,128)S(1)}, f32[392,128]{1,0:T(8,128)S(1)}, u32[]{:S(2)}, u32[]{:S(2)}) %collective-permute-start.2) | collective-permute-done | bytes 200736 | tf_op jit(solution)/shard_map/ppermute | solution.py:247
  26.0 0.1 block_total.2
  26.1 2.6 %collective-permute-start.3 = (f32[392,128]{1,0:T(8,128)S(1)}, f32[392,128]{1,0:T(8,128)S(1)}, u32[]{:S(2)}, u32[]{:S(2)}) collective-permute-start(f32[392,128]{1,0:T(8,128)S(1)} %block_total.2), channel_id=1, source_target_pairs={{0,4},{4,8},{8,12},{12,16},{16,20},{20,24},{24,28},{28,0},{1,5},{5... | collective-permute-start | bytes 602120 | tf_op jit(solution)/shard_map/ppermute | solution.py:252
  28.7 3.3 %collective-permute-start.4 = (f32[392,128]{1,0:T(8,128)S(1)}, f32[392,128]{1,0:T(8,128)S(1)}, u32[]{:S(2)}, u32[]{:S(2)}) collective-permute-start(f32[392,128]{1,0:T(8,128)S(1)} %block_total.2), channel_id=1, source_target_pairs={{0,8},{4,12},{8,16},{12,20},{16,24},{20,28},{24,0},{28,4},{1,9},{5... | collective-permute-start | bytes 602120 | tf_op jit(solution)/shard_map/ppermute | solution.py:252
  32.0 0.0 collective-permute-done.11.refs_4_
  32.0 0.0 collective-permute-done.12.refs_5_
  32.0 0.3 prefixes.3
  32.3 0.1 collective-permute-start.13
  32.3 3.4 %collective-permute-start.14 = (f32[392,128]{1,0:T(8,128)S(1)}, f32[392,128]{1,0:T(8,128)S(1)}, u32[]{:S(2)}, u32[]{:S(2)}) collective-permute-start(f32[392,128]{1,0:T(8,128)S(1)} %get-tuple-element.35), channel_id=1, source_target_pairs={{0,2},{1,3},{2,0},{3,1},{4,6},{5,7},{6,4},{7,5},{8,10},{9,11},{10,... | collective-permute-start | bytes 602120 | tf_op jit(solution)/shard_map/ppermute | solution.py:247
  35.7 0.0 copy-start
  35.7 0.0 collective-permute-start.15
  35.7 4.2 %collective-permute-done.3.refs_4_ = f32[392,128]{1,0:T(8,128)S(1)} collective-permute-done((f32[392,128]{1,0:T(8,128)S(1)}, f32[392,128]{1,0:T(8,128)S(1)}, u32[]{:S(2)}, u32[]{:S(2)}) %collective-permute-start.3) | collective-permute-done | bytes 200736 | tf_op jit(solution)/shard_map/ppermute | solution.py:252
  39.9 0.0 collective-permute-done.4.refs_5_
  39.9 0.3 prefixes.2
  40.2 0.9 %collective-permute-start.5 = (f32[392,128]{1,0:T(8,128)S(1)}, f32[392,128]{1,0:T(8,128)S(1)}, u32[]{:S(2)}, u32[]{:S(2)}) collective-permute-start(f32[392,128]{1,0:T(8,128)S(1)} %get-tuple-element.26), channel_id=1, source_target_pairs={{0,1},{1,0},{2,3},{3,2},{4,5},{5,4},{6,7},{7,6},{8,9},{9,8},{10,11... | collective-permute-start | bytes 602120 | tf_op jit(solution)/shard_map/ppermute | solution.py:247
  41.1 0.0 collective-permute-start.6
  41.1 0.0 collective-permute-done.13.refs_1_
  41.1 0.0 copy-start.3
  41.1 1.8 %collective-permute-start.7 = (f32[392,128]{1,0:T(8,128)S(1)}, f32[392,128]{1,0:T(8,128)S(1)}, u32[]{:S(2)}, u32[]{:S(2)}) collective-permute-start(f32[392,128]{1,0:T(8,128)S(1)} %get-tuple-element.28), channel_id=1, source_target_pairs={{0,3},{1,2},{2,1},{3,0},{4,7},{5,6},{6,5},{7,4},{8,11},{9,10},{10,... | collective-permute-start | bytes 602120 | tf_op jit(solution)/shard_map/ppermute | solution.py:247
  42.9 1.8 %collective-permute-done.14.refs_2_ = f32[392,128]{1,0:T(8,128)S(1)} collective-permute-done((f32[392,128]{1,0:T(8,128)S(1)}, f32[392,128]{1,0:T(8,128)S(1)}, u32[]{:S(2)}, u32[]{:S(2)}) %collective-permute-start.14) | collective-permute-done | bytes 200736 | tf_op jit(solution)/shard_map/ppermute | solution.py:247
  44.7 4.1 %collective-permute-done.15.refs_3_ = f32[392,128]{1,0:T(8,128)S(1)} collective-permute-done((f32[392,128]{1,0:T(8,128)S(1)}, f32[392,128]{1,0:T(8,128)S(1)}, u32[]{:S(2)}, u32[]{:S(2)}) %collective-permute-start.15) | collective-permute-done | bytes 200736 | tf_op jit(solution)/shard_map/ppermute | solution.py:247
  48.8 0.0 copy-done
  48.8 0.0 copy-done.3
  48.8 4.1 %solve.2.refs_4_ = f32[128,2048]{1,0:T(8,128)} custom-call(s32[1]{0:T(128)} %bitcast.me_ref, f32[16]{0:T(128)S(1)} %copy-done.3, s32[1,128]{1,0:T(1,128)S(1)} %bitcast.4, bf16[128,2048]{1,0:T(8,128)(2,1)S(1)} %copy-done, bf16[128,2048]{1,0:T(8,128)(2,1)S(1)} %copy-done.1, bf16[128,2048]{1,0:T(8,128)(2,1)S(1)} %copy-done.2, ...), custom_call_target="tpu_custom_call" | custom-call | flops 4294967296 | tf_op jit(solution)/shard_map/solve/pallas_call | solution.py:221
  52.9 0.0 collective-permute-done.5.refs_1_
  52.9 0.4 collective-permute-done.6.refs_2_
  53.3 3.3 %collective-permute-done.7.refs_3_ = f32[392,128]{1,0:T(8,128)S(1)} collective-permute-done((f32[392,128]{1,0:T(8,128)S(1)}, f32[392,128]{1,0:T(8,128)S(1)}, u32[]{:S(2)}, u32[]{:S(2)}) %collective-permute-start.7) | collective-permute-done | bytes 200736 | tf_op jit(solution)/shard_map/ppermute | solution.py:247
  56.6 4.1 %solve.3 = f32[128,2048]{1,0:T(8,128)} custom-call(s32[1]{0:T(128)} %bitcast.me_ref, f32[16]{0:T(128)S(1)} %copy-done.3, s32[1,128]{1,0:T(1,128)S(1)} %bitcast.5, bf16[128,2048]{1,0:T(8,128)(2,1)S(1)} %copy-done, bf16[128,2048]{1,0:T(8,128)(2,1)S(1)} %copy-done.1, bf16[128,2048]{1,0:T(8,128)(2,1)S(1)} %copy-done.2, ...), custom_call_target="tpu_custom_call", output_to_operand_aliasing={{}: (10, {})} | custom-call | flops 4294967296 | tf_op jit(solution)/shard_map/solve/pallas_call | solution.py:221
Async XLA Ops:
  0.0 5.7 %copy-start.1 = (bf16[128,2048]{1,0:T(8,128)(2,1)S(1)}, bf16[128,2048]{1,0:T(8,128)(2,1)}, u32[]{:S(2)}) copy-start(bf16[128,2048]{1,0:T(8,128)(2,1)} %k_ref.7) | copy-start | bytes 1572868
  0.0 5.7 %copy-start.2 = (bf16[128,2048]{1,0:T(8,128)(2,1)S(1)}, bf16[128,2048]{1,0:T(8,128)(2,1)}, u32[]{:S(2)}) copy-start(bf16[128,2048]{1,0:T(8,128)(2,1)} %v_ref.7) | copy-start | bytes 1572868
  2.3 6.8 %collective-permute-start.8 = (f32[392,128]{1,0:T(8,128)S(1)}, f32[392,128]{1,0:T(8,128)S(1)}, u32[]{:S(2)}, u32[]{:S(2)}) collective-permute-start(f32[392,128]{1,0:T(8,128)S(1)} %get-tuple-element.30), channel_id=1, source_target_pairs={{0,1},{1,0},{2,3},{3,2},{4,5},{5,4},{6,7},{7,6},{8,9},{9,8},{10,11... | collective-permute-start | bytes 602120 | tf_op jit(solution)/shard_map/ppermute | solution.py:247
  4.4 1.3 %copy-start.4 = (s32[128]{0:T(128)S(1)}, s32[128]{0:T(128)}, u32[]{:S(2)}) copy-start(s32[128]{0:T(128)} %param.8) | copy-start | bytes 1540
  4.4 6.9 %collective-permute-start.9 = (f32[392,128]{1,0:T(8,128)S(1)}, f32[392,128]{1,0:T(8,128)S(1)}, u32[]{:S(2)}, u32[]{:S(2)}) collective-permute-start(f32[392,128]{1,0:T(8,128)S(1)} %get-tuple-element.31), channel_id=1, source_target_pairs={{0,2},{1,3},{2,0},{3,1},{4,6},{5,7},{6,4},{7,5},{8,10},{9,11},{10,... | collective-permute-start | bytes 602120 | tf_op jit(solution)/shard_map/ppermute | solution.py:247
  5.7 8.7 %collective-permute-start.10 = (f32[392,128]{1,0:T(8,128)S(1)}, f32[392,128]{1,0:T(8,128)S(1)}, u32[]{:S(2)}, u32[]{:S(2)}) collective-permute-start(f32[392,128]{1,0:T(8,128)S(1)} %get-tuple-element.32), channel_id=1, source_target_pairs={{0,3},{1,2},{2,1},{3,0},{4,7},{5,6},{6,5},{7,4},{8,11},{9,10},{10,... | collective-permute-start | bytes 602120 | tf_op jit(solution)/shard_map/ppermute | solution.py:247
  6.3 15.0 %collective-permute-start = (f32[392,128]{1,0:T(8,128)S(1)}, f32[392,128]{1,0:T(8,128)S(1)}, u32[]{:S(2)}, u32[]{:S(2)}) collective-permute-start(f32[392,128]{1,0:T(8,128)S(1)} %get-tuple-element.22), channel_id=1, source_target_pairs={{0,1},{1,0},{2,3},{3,2},{4,5},{5,4},{6,7},{7,6},{8,9},{9,8},{10,11... | collective-permute-start | bytes 602120 | tf_op jit(solution)/shard_map/ppermute | solution.py:247
  7.8 13.6 %collective-permute-start.1 = (f32[392,128]{1,0:T(8,128)S(1)}, f32[392,128]{1,0:T(8,128)S(1)}, u32[]{:S(2)}, u32[]{:S(2)}) collective-permute-start(f32[392,128]{1,0:T(8,128)S(1)} %get-tuple-element.23), channel_id=1, source_target_pairs={{0,2},{1,3},{2,0},{3,1},{4,6},{5,7},{6,4},{7,5},{8,10},{9,11},{10,... | collective-permute-start | bytes 602120 | tf_op jit(solution)/shard_map/ppermute | solution.py:247
  9.1 16.9 %collective-permute-start.2 = (f32[392,128]{1,0:T(8,128)S(1)}, f32[392,128]{1,0:T(8,128)S(1)}, u32[]{:S(2)}, u32[]{:S(2)}) collective-permute-start(f32[392,128]{1,0:T(8,128)S(1)} %get-tuple-element.24), channel_id=1, source_target_pairs={{0,3},{1,2},{2,1},{3,0},{4,7},{5,6},{6,5},{7,4},{8,11},{9,10},{10,... | collective-permute-start | bytes 602120 | tf_op jit(solution)/shard_map/ppermute | solution.py:247
  14.4 17.5 %collective-permute-start.11 = (f32[392,128]{1,0:T(8,128)S(1)}, f32[392,128]{1,0:T(8,128)S(1)}, u32[]{:S(2)}, u32[]{:S(2)}) collective-permute-start(f32[392,128]{1,0:T(8,128)S(1)} %block_total.3), channel_id=1, source_target_pairs={{0,4},{4,8},{8,12},{12,16},{16,20},{20,24},{24,28},{28,0},{1,5},{5... | collective-permute-start | bytes 602120 | tf_op jit(solution)/shard_map/ppermute | solution.py:252
  16.7 15.3 %collective-permute-start.12 = (f32[392,128]{1,0:T(8,128)S(1)}, f32[392,128]{1,0:T(8,128)S(1)}, u32[]{:S(2)}, u32[]{:S(2)}) collective-permute-start(f32[392,128]{1,0:T(8,128)S(1)} %block_total.3), channel_id=1, source_target_pairs={{0,8},{4,12},{8,16},{12,20},{16,24},{20,28},{24,0},{28,4},{1,9},{5... | collective-permute-start | bytes 602120 | tf_op jit(solution)/shard_map/ppermute | solution.py:252
  26.1 13.8 %collective-permute-start.3 = (f32[392,128]{1,0:T(8,128)S(1)}, f32[392,128]{1,0:T(8,128)S(1)}, u32[]{:S(2)}, u32[]{:S(2)}) collective-permute-start(f32[392,128]{1,0:T(8,128)S(1)} %block_total.2), channel_id=1, source_target_pairs={{0,4},{4,8},{8,12},{12,16},{16,20},{20,24},{24,28},{28,0},{1,5},{5... | collective-permute-start | bytes 602120 | tf_op jit(solution)/shard_map/ppermute | solution.py:252
  28.7 11.2 %collective-permute-start.4 = (f32[392,128]{1,0:T(8,128)S(1)}, f32[392,128]{1,0:T(8,128)S(1)}, u32[]{:S(2)}, u32[]{:S(2)}) collective-permute-start(f32[392,128]{1,0:T(8,128)S(1)} %block_total.2), channel_id=1, source_target_pairs={{0,8},{4,12},{8,16},{12,20},{16,24},{20,28},{24,0},{28,4},{1,9},{5... | collective-permute-start | bytes 602120 | tf_op jit(solution)/shard_map/ppermute | solution.py:252
  32.3 8.8 %collective-permute-start.13 = (f32[392,128]{1,0:T(8,128)S(1)}, f32[392,128]{1,0:T(8,128)S(1)}, u32[]{:S(2)}, u32[]{:S(2)}) collective-permute-start(f32[392,128]{1,0:T(8,128)S(1)} %get-tuple-element.34), channel_id=1, source_target_pairs={{0,1},{1,0},{2,3},{3,2},{4,5},{5,4},{6,7},{7,6},{8,9},{9,8},{10,11... | collective-permute-start | bytes 602120 | tf_op jit(solution)/shard_map/ppermute | solution.py:247
  32.3 12.3 %collective-permute-start.14 = (f32[392,128]{1,0:T(8,128)S(1)}, f32[392,128]{1,0:T(8,128)S(1)}, u32[]{:S(2)}, u32[]{:S(2)}) collective-permute-start(f32[392,128]{1,0:T(8,128)S(1)} %get-tuple-element.35), channel_id=1, source_target_pairs={{0,2},{1,3},{2,0},{3,1},{4,6},{5,7},{6,4},{7,5},{8,10},{9,11},{10,... | collective-permute-start | bytes 602120 | tf_op jit(solution)/shard_map/ppermute | solution.py:247
  35.7 13.1 %copy-start = (bf16[128,2048]{1,0:T(8,128)(2,1)S(1)}, bf16[128,2048]{1,0:T(8,128)(2,1)}, u32[]{:S(2)}) copy-start(bf16[128,2048]{1,0:T(8,128)(2,1)} %q_ref.3) | copy-start | bytes 1572868
  35.7 13.0 %collective-permute-start.15 = (f32[392,128]{1,0:T(8,128)S(1)}, f32[392,128]{1,0:T(8,128)S(1)}, u32[]{:S(2)}, u32[]{:S(2)}) collective-permute-start(f32[392,128]{1,0:T(8,128)S(1)} %get-tuple-element.36), channel_id=1, source_target_pairs={{0,3},{1,2},{2,1},{3,0},{4,7},{5,6},{6,5},{7,4},{8,11},{9,10},{10,... | collective-permute-start | bytes 602120 | tf_op jit(solution)/shard_map/ppermute | solution.py:247
  40.2 12.8 %collective-permute-start.5 = (f32[392,128]{1,0:T(8,128)S(1)}, f32[392,128]{1,0:T(8,128)S(1)}, u32[]{:S(2)}, u32[]{:S(2)}) collective-permute-start(f32[392,128]{1,0:T(8,128)S(1)} %get-tuple-element.26), channel_id=1, source_target_pairs={{0,1},{1,0},{2,3},{3,2},{4,5},{5,4},{6,7},{7,6},{8,9},{9,8},{10,11... | collective-permute-start | bytes 602120 | tf_op jit(solution)/shard_map/ppermute | solution.py:247
  41.1 12.2 %collective-permute-start.6 = (f32[392,128]{1,0:T(8,128)S(1)}, f32[392,128]{1,0:T(8,128)S(1)}, u32[]{:S(2)}, u32[]{:S(2)}) collective-permute-start(f32[392,128]{1,0:T(8,128)S(1)} %get-tuple-element.27), channel_id=1, source_target_pairs={{0,2},{1,3},{2,0},{3,1},{4,6},{5,7},{6,4},{7,5},{8,10},{9,11},{10,... | collective-permute-start | bytes 602120 | tf_op jit(solution)/shard_map/ppermute | solution.py:247
  41.1 7.7 %copy-start.3 = (f32[16]{0:T(128)S(1)}, f32[16]{0:T(128)}, u32[]{:S(2)}) copy-start(f32[16]{0:T(128)} %ridge_ref.3) | copy-start | bytes 196
  41.1 15.5 %collective-permute-start.7 = (f32[392,128]{1,0:T(8,128)S(1)}, f32[392,128]{1,0:T(8,128)S(1)}, u32[]{:S(2)}, u32[]{:S(2)}) collective-permute-start(f32[392,128]{1,0:T(8,128)S(1)} %get-tuple-element.28), channel_id=1, source_target_pairs={{0,3},{1,2},{2,1},{3,0},{4,7},{5,6},{6,5},{7,4},{8,11},{9,10},{10,... | collective-permute-start | bytes 602120 | tf_op jit(solution)/shard_map/ppermute | solution.py:247

commit v5 on v2

v5 whole, which is shorter than its diff:
```python
import functools

import jax
import jax.numpy as jnp
from jax import lax
from jax.experimental import pallas as pl
from jax.experimental.pallas import tpu as pltpu
from jax.sharding import Mesh
from jax.sharding import PartitionSpec as P

CG_ITERS = 3
DOC_SHARE = 4


def split(x):
    high = x.astype(jnp.bfloat16)
    low = (x - high.astype(jnp.float32)).astype(jnp.bfloat16)
    return high, low


def dot(a, b):
    return lax.dot_general(a, b, (((1,), (0,)), ((), ())), preferred_element_type=jnp.float32)


def dot_rows(a, b):
    return lax.dot_general(a, b, (((0,), (0,)), ((), ())), preferred_element_type=jnp.float32)


def total(terms):
    return functools.reduce(lambda a, b: a + b, terms)


def triangle(width):
    row = lax.broadcasted_iota(jnp.int32, (width, width), 0)
    col = lax.broadcasted_iota(jnp.int32, (width, width), 1)
    return row <= col, row == col


def down(ids):
    count = ids.shape[1]
    return jnp.broadcast_to(ids, (count, count)).T[:, :1]


def row_scale(wide):
    return lax.rsqrt(jnp.sum(wide * wide, -1, keepdims=True) + 1e-06)


def extra_of(packs):
    return -(-(packs + 2) // 8) * 8


def last_of(ids_ref, width):
    ids = ids_ref[...].astype(jnp.float32)
    oldest, newest = jnp.min(ids, 1, keepdims=True), jnp.max(ids, 1, keepdims=True)
    weight = jnp.broadcast_to((down(ids) == newest).astype(jnp.float32), (ids.shape[1], width))
    return oldest, newest, weight


def own_first_kernel(width, packs, early, count, ids_hbm, k_hbm, v_hbm, *refs):
    outs, (ids_ref, k_ref, v_ref, sems) = refs[:count], refs[count:]
    span = 2 * packs * width
    moves = [(ids_hbm, ids_ref)]
    for slot in range(count):
        start = pl.multiple_of((lax.axis_index("near") ^ slot) * span, span)
        moves.append((k_hbm.at[:, pl.ds(start, span)], k_ref.at[slot]))
        if early:
            moves.append((v_hbm.at[:, pl.ds(start, early * width)], v_ref.at[slot]))
    copies = [pltpu.make_async_copy(*move, sems.at[number]) for number, move in enumerate(moves)]
    for copy in copies:
        copy.start()
    upper, diagonal = triangle(width)
    for copy in copies:
        copy.wait()
    oldest, newest, weight = last_of(ids_ref, width)
    marks = [jnp.broadcast_to(one + 1.0, (1, width)) for one in (oldest, newest)]
    extra = extra_of(packs)
    filler = jnp.zeros((extra - packs - 2, width), jnp.float32)
    for slot, out in enumerate(outs):
        grams = []
        for head in range(2 * packs):
            lanes = pl.ds(head * width, width)
            keys = k_ref[slot, :, lanes]
            wide = keys.astype(jnp.float32)
            scale = row_scale(wide)
            light = weight * scale
            high, low = split(light * scale * wide)
            if head < early:
                v_high, v_low = split(light * v_ref[slot, :, lanes].astype(jnp.float32))
                high, low = jnp.concatenate([high, v_high], 1), jnp.concatenate([low, v_low], 1)
            both = dot_rows(jnp.concatenate([keys, keys], 0), jnp.concatenate([high, low], 0))
            grams.append(both[:, :width])
            if head < early:
                out[pl.ds((packs + head) * width + extra, width), :] = both[:, width:]
        seconds = []
        for pack in range(packs):
            one, two = grams[2 * pack : 2 * pack + 2]
            out[pl.ds(pack * width, width), :] = jnp.where(upper, one, two)
            seconds.append(jnp.sum(jnp.where(diagonal, two, 0.0), 0, keepdims=True))
        out[pl.ds(packs * width, extra), :] = jnp.concatenate([*seconds, *marks, filler], 0)


def own_rest_kernel(width, heads, early, ids_ref, k_ref, v_ref, *outs):
    weight = last_of(ids_ref, width)[2]
    for slot, out in enumerate(outs):
        for head in range(early, heads):
            at = (lax.axis_index("near") ^ slot) * heads + head
            lanes = pl.ds(pl.multiple_of(at * width, width), width)
            keys = k_ref[:, lanes]
            scale = row_scale(keys.astype(jnp.float32))
            high, low = split(weight * scale * v_ref[:, lanes].astype(jnp.float32))
            out[pl.ds((head - early) * width, width), :] = dot_rows(
                jnp.concatenate([keys, keys], 0), jnp.concatenate([high, low], 0)
            )


def marks_of(refs, at):
    return [ref[pl.ds(at, 1), :] for ref in refs], [ref[pl.ds(at + 1, 1), :] for ref in refs]


def flag(condition):
    return condition.astype(jnp.float32)


def total_kernel(at, count, *refs):
    marked, slots, out = refs[:count], refs[-1 - count : -1], refs[-1]
    last = marks_of(marked, at)[1]
    newest = functools.reduce(jnp.maximum, last)
    out[...] = total([slot[...] * flag(one == newest) for slot, one in zip(slots, last)])
    if len(refs) == count + 1:
        out[pl.ds(at, 2), :] = jnp.concatenate([newest, newest], 0)


def prefix_kernel(at, count, steps, *refs):
    outs, refs = refs[-count:], refs[:-count]
    marked, marked_carries = refs[:count], refs[count : count + steps]
    slots, carries = refs[-count - steps : -steps], refs[-steps:]
    first, last = marks_of(marked, at)
    oldest = functools.reduce(jnp.minimum, first)
    ends = marks_of(marked_carries, at)[1]
    carry = total([one[...] * flag(mark == oldest) for one, mark in zip(carries, ends)])
    me = lax.axis_index("near")
    for target, out in enumerate(outs):
        terms = [carry * flag(first[target] == oldest)]
        for source in range(count):
            if source != target:
                before = jnp.where((me ^ source) < (me ^ target), 1.0, 0.0)
                terms.append(slots[source][...] * (flag(last[source] == first[target]) * before))
        out[...] = total(terms)


def far_part(pair, high, cross):
    c_high, c_low = split(cross)
    return dot(pair, jnp.concatenate([c_high, c_high], 0)) + dot(high, c_low)


def solve_kernel(width, packs, early, together, ridge_ref, ids_ref, q_ref, k_ref, v_ref, *refs):
    slots, (x_ref, near_ref, out_hbm, out, sems) = refs[:-5], refs[-5:]
    upper, diagonal = triangle(width)
    ids = ids_ref[...].astype(jnp.float32)
    column = down(ids)
    rows = ids.shape[1]
    carried = jnp.broadcast_to(flag(column == jnp.min(ids, 1, keepdims=True)), (rows, width))
    row_at = lax.broadcasted_iota(jnp.int32, (rows, rows), 0)
    col_at = lax.broadcasted_iota(jnp.int32, (rows, rows), 1)
    within = jnp.where(row_at >= col_at, flag(column == ids), 0.0)
    copies = []
    for start in range(0, len(slots), together):
        group = []
        for slot, pack in [(j, p) for j in range(start, min(start + together, len(slots))) for p in range(packs)]:
            state = slots[slot]
            packed = state[pl.ds(pack * width, width), :]
            flipped = packed.T
            second = state[pl.ds(packs * width + pack, 1), :]
            grams = [
                jnp.where(upper, packed, flipped),
                jnp.where(diagonal, second, jnp.where(upper, flipped, packed)),
            ]
            for side in range(2):
                head = ((lax.axis_index("near") ^ slot) * packs + pack) * 2 + side
                lanes = pl.ds(pl.multiple_of(head * width, width), width)
                wide = q_ref[:, lanes].astype(jnp.float32)
                query = wide * row_scale(wide)
                keys = k_ref[:, lanes]
                turned = keys.astype(jnp.float32).T
                scale = lax.rsqrt(jnp.sum(turned * turned, 0, keepdims=True) + 1e-06)
                turned = turned.astype(jnp.bfloat16)
                high, low = split(grams[side])
                both = jnp.concatenate([high, turned], 1)
                group.append(
                    dict(
                        lanes=lanes,
                        cross=state.at[pl.ds((packs + 2 * pack + side) * width + extra_of(packs), width)]
                        if 2 * pack + side < early
                        else None,
                        both=jnp.concatenate([both, both], 0),
                        low=low,
                        turned=jnp.concatenate([turned, turned], 0),
                        keys=jnp.concatenate([keys, keys], 0),
                        once=within * scale,
                        twice=within * (scale * scale),
                        ridge=ridge_ref[head],
                        remain=query,
                        search=query,
                        square=jnp.sum(query * query, -1, keepdims=True),
                    )
                )
        for step in range(CG_ITERS):
            for h in group:
                high, low = split(h["search"])
                wide = dot(jnp.concatenate([high, low], 1), h["both"])
                h["state"] = wide[:, :width] + dot(high, h["low"])
                h["score"] = split(wide[:, width:] * h["twice"])
            for h in group:
                local = dot(jnp.concatenate(h["score"], 1), h["keys"])
                search = h["search"]
                applied = h["state"] * carried + local + h["ridge"] * search
                size = h["square"] / jnp.sum(search * applied, -1, keepdims=True)
                h["solved"] = size * search if step == 0 else h["solved"] + size * search
                if step < CG_ITERS - 1:
                    remain = h["remain"] - size * applied
                    square = jnp.sum(remain * remain, -1, keepdims=True)
                    h["search"] = remain + square / h["square"] * search
                    h["remain"], h["square"] = remain, square
        for h in group:
            high, low = split(h["solved"])
            pair = jnp.concatenate([high, low], 1)
            h["score"] = split(dot(pair, h["turned"]) * h["once"])
            if h["cross"] is None:
                x_ref[:, h["lanes"]] = h["solved"] * carried
            else:
                h["far"] = far_part(pair, high, h["cross"][...]) * carried
        for h in group:
            values = v_ref[:, h["lanes"]]
            local = dot(jnp.concatenate(h["score"], 1), jnp.concatenate([values, values], 0))
            if h["cross"] is None:
                near_ref[:, h["lanes"]] = local
            else:
                at = len(copies)
                out[at] = local + h["far"]
                copies.append(pltpu.make_async_copy(out.at[at], out_hbm.at[:, h["lanes"]], sems.at[at]))
                copies[-1].start()
    for copy in copies:
        copy.wait()


def readout_kernel(width, heads, early, count, x_ref, near_ref, *refs):
    slots, (out_hbm, out, sems) = refs[:count], refs[-3:]
    copies = []
    for slot, state in enumerate(slots):
        for head in range(early, heads):
            at = (lax.axis_index("near") ^ slot) * heads + head
            lanes = pl.ds(pl.multiple_of(at * width, width), width)
            high, low = split(x_ref[:, lanes])
            far = far_part(jnp.concatenate([high, low], 1), high, state[pl.ds((head - early) * width, width), :])
            number = len(copies)
            out[number] = near_ref[:, lanes] + far
            copies.append(pltpu.make_async_copy(out.at[number], out_hbm.at[:, lanes], sems.at[number]))
            copies[-1].start()
    for copy in copies:
        copy.wait()


VMEM = pl.BlockSpec(memory_space=pltpu.VMEM)
SMEM = pl.BlockSpec(memory_space=pltpu.SMEM)
HBM = pl.BlockSpec(memory_space=pltpu.HBM)
PARAMS = pltpu.CompilerParams(vmem_limit_bytes=40 * 1024 * 1024)


def call(kernel, name, flops, out_shape, in_specs, arguments, **more):
    out_specs = [VMEM] * len(out_shape) if isinstance(out_shape, list) else VMEM
    return pl.pallas_call(
        kernel,
        out_shape=out_shape,
        in_specs=in_specs,
        compiler_params=PARAMS,
        cost_estimate=pl.CostEstimate(flops=flops, bytes_accessed=0, transcendentals=0),
        name=name,
        **{"out_specs": out_specs, **more},
    )(*arguments)


def on_device(queries, key_vectors, value_vectors, segment_ids, ridge_weight):
    row_count, columns = queries.shape
    head_count = ridge_weight.shape[0]
    width = columns // head_count
    outer, half, near = lax.axis_size("outer"), lax.axis_size("half"), lax.axis_size("near")
    blocks = outer * half
    heads = head_count // near
    packs = heads // 2
    early = heads // 4
    steps = min(-(-(row_count * near * blocks // DOC_SHARE - 1) // (row_count * near)), blocks - 1)
    ids = segment_ids.reshape(1, row_count)
    mark_at = packs * width + packs
    first_shape = jax.ShapeDtypeStruct(((packs + early) * width + extra_of(packs), width), jnp.float32)
    rest_shape = jax.ShapeDtypeStruct(((heads - early) * width, width), jnp.float32)
    flat = jax.ShapeDtypeStruct((row_count, columns), jnp.float32)
    unit = 16 * head_count * width * width * row_count

    def exchange(slots):
        return [slots[0]] + [
            lax.ppermute(slots[j], "near", [(i, i ^ j) for i in range(near)]) for j in range(1, near)
        ]

    def onward(value):
        return [
            lax.ppermute(value, ("outer", "half"), [(i, (i + step) % blocks) for i in range(blocks)])
            for step in range(1, steps + 1)
        ]

    own_first = call(
        functools.partial(own_first_kernel, width, packs, early, near),
        "own_first",
        unit,
        [first_shape] * near,
        [HBM] * 3,
        [pltpu.with_memory_space_constraint(one, pltpu.HBM) for one in (ids, key_vectors, value_vectors)],
        scratch_shapes=[
            pltpu.VMEM(ids.shape, ids.dtype),
            pltpu.VMEM((near, row_count, heads * width), key_vectors.dtype),
            pltpu.VMEM((near, row_count, max(early, 1) * width), value_vectors.dtype),
            pltpu.SemaphoreType.DMA((2 * near + 1,)),
        ],
    )
    own_rest = call(
        functools.partial(own_rest_kernel, width, heads, early),
        "own_rest",
        unit,
        [rest_shape] * near,
        [VMEM] * 3,
        (ids, key_vectors, value_vectors),
    )
    marked, marked_carries, states = [], [], []
    for own, shape in ((own_first, first_shape), (own_rest, rest_shape)):
        slots = exchange(own)
        block_total = call(
            functools.partial(total_kernel, mark_at, near),
            "block_total",
            unit // 4,
            shape,
            [VMEM] * (len(marked) + near),
            (*marked, *slots),
        )
        carries = onward(block_total)
        prefix = call(
            functools.partial(prefix_kernel, mark_at, near, steps),
            "prefixes",
            unit // 4,
            [shape] * near,
            [VMEM] * (len(marked) + len(marked_carries) + near + steps),
            (*marked, *marked_carries, *slots, *carries),
        )
        states.append(exchange(prefix))
        marked, marked_carries = marked or slots, marked_carries or carries
    count = near * early
    solved, local, out = call(
        functools.partial(solve_kernel, width, packs, early, max(1, 8 // heads)),
        "solve",
        12 * unit,
        [flat] * 3,
        [SMEM] + [VMEM] * (4 + near),
        (ridge_weight, ids, queries, key_vectors, value_vectors, *states[0]),
        out_specs=[VMEM, VMEM, HBM],
        scratch_shapes=[
            pltpu.VMEM((max(count, 1), row_count, width), jnp.float32),
            pltpu.SemaphoreType.DMA((max(count, 1),)),
        ],
    )
    count = near * (heads - early)
    return call(
        functools.partial(readout_kernel, width, heads, early, near),
        "readout",
        2 * unit,
        flat,
        [VMEM] * (2 + near) + [HBM],
        (solved, local, *states[1], out),
        out_specs=HBM,
        scratch_shapes=[pltpu.VMEM((count, row_count, width), jnp.float32), pltpu.SemaphoreType.DMA((count,))],
        input_output_aliases={2 + near: 0},
    )


def solution(mesh):
    outer, inner = mesh.shape["outer"], mesh.shape["inner"]
    finer = Mesh(mesh.devices.reshape(outer, 2, inner // 2), ("outer", "half", "near"))
    tokens = P(("outer", "half", "near"))
    return jax.shard_map(
        on_device, mesh=finer, in_specs=(tokens, tokens, tokens, tokens, P()), out_specs=tokens, check_vma=False
    )
```

time: 70.6 us -> 57.1 us (0.81); the launches traced: 69.7 us -> 56.9 us
  waiting for transfers between devices: 25.8 us -> 15.5 us
  local copies, waits for them, and re-layouts: 1.71 us -> 0.02 us
  Pallas kernels: 12.4 us -> 11.2 us
    ppermute x12, waiting for transfers between devices: 18 us -> 10.2 us  [exchange(): lax.ppermute(slots[j], 'near', [(i, i ^ j) for i in range(near)])]
    ppermute x4, waiting for transfers between devices: 7.8 us -> 5.28 us  [onward(): lax.ppermute(value, ('outer', 'half'), [(i, (i + step) % blocks) for i in...]
    unnamed x12 -> x10, local copies, waits for them, and re-layouts: 1.71 us -> 0.02 us
    pallas_call x8, Pallas kernels: 12.4 us -> 11.2 us  [call(): pl.pallas_call(kernel, out_shape=out_shape, in_specs=in_specs, compiler_p...]
  transfers between devices with their start and end apart: 16 -> 16, of which waited for: 6 -> 7; matrix products, arithmetic and copies ran while one was open for 0% -> 0% of each run, Pallas kernels for 13% -> 14%
where the time goes in v5:
time: 57.1 us; the launch traced here: 56.9 us
  starting transfers between devices  30.1 us (53%)
  waiting for transfers between devices  15.5 us (27%)
  Pallas kernels  11.2 us (20%)
    ppermute x12, starting transfers between devices, exchange(): lax.ppermute(slots[j], 'near', [(i, i ^ j) for i in range(near)])  16.6 us
    ppermute x4, starting transfers between devices, onward(): lax.ppermute(value, ('outer', 'half'), [(i, (i + step) % blocks) for i in...  13.6 us
    pallas_call x8, Pallas kernels, call(): pl.pallas_call(kernel, out_shape=out_shape, in_specs=in_specs, compiler_p...  11.2 us
    ppermute x12, waiting for transfers between devices, exchange(): lax.ppermute(slots[j], 'near', [(i, i ^ j) for i in range(near)])  10.2 us
    ppermute x4, waiting for transfers between devices, onward(): lax.ppermute(value, ('outer', 'half'), [(i, (i + step) % blocks) for i in...  5.28 us
  transfers between devices with their start and end apart: 16, of which 7 were waited for; matrix products, arithmetic and copies ran while one was open for 0% of the time, Pallas kernels for 14%

profile of v5, /device:TPU:1, one launch (start us, length us, event | category | flops | bytes accessed | tf_op | source)
XLA Modules:
  0.0 56.9 jit_solution(12062936580323322313)
XLA Ops:
  0.0 0.0 copy-start.1
  0.0 0.0 copy-start.2
  0.0 2.2 %own_first.1 = (f32[392,128]{1,0:T(8,128)S(1)}, f32[392,128]{1,0:T(8,128)S(1)}, f32[392,128]{1,0:T(8,128)S(1)}, f32[392,128]{1,0:T(8,128)S(1)}) custom-call(s32[1,128]{1,0:T(1,128)} %bitcast.1, bf16[128,2048]{1,0:T(8,128)(2,1)} %k_ref.3, bf16[128,2048]{1,0:T(8,128)(2,1)} %v_ref.3), custom_call_target="tpu_custom_call" | custom-call | flops 536870912 | tf_op jit(solution)/shard_map/own_first/pallas_call | solution.py:271
  2.2 2.1 %collective-permute-start = (f32[392,128]{1,0:T(8,128)S(1)}, f32[392,128]{1,0:T(8,128)S(1)}, u32[]{:S(2)}, u32[]{:S(2)}) collective-permute-start(f32[392,128]{1,0:T(8,128)S(1)} %get-tuple-element.25), channel_id=1, source_target_pairs={{0,1},{1,0},{2,3},{3,2},{4,5},{5,4},{6,7},{7,6},{8,9},{9,8},{10,11... | collective-permute-start | bytes 602120 | tf_op jit(solution)/shard_map/ppermute | solution.py:301
  4.3 0.0 copy-start.4
  4.3 1.3 %collective-permute-start.1 = (f32[392,128]{1,0:T(8,128)S(1)}, f32[392,128]{1,0:T(8,128)S(1)}, u32[]{:S(2)}, u32[]{:S(2)}) collective-permute-start(f32[392,128]{1,0:T(8,128)S(1)} %get-tuple-element.26), channel_id=1, source_target_pairs={{0,2},{1,3},{2,0},{3,1},{4,6},{5,7},{6,4},{7,5},{8,10},{9,11},{10,... | collective-permute-start | bytes 602120 | tf_op jit(solution)/shard_map/ppermute | solution.py:301
  5.6 0.0 collective-permute-start.2
  5.6 0.0 copy-done.1
  5.6 0.0 copy-done.2
  5.6 0.0 copy-done.4
  5.6 0.7 %own_rest.1 = (f32[384,128]{1,0:T(8,128)S(1)}, f32[384,128]{1,0:T(8,128)S(1)}, f32[384,128]{1,0:T(8,128)S(1)}, f32[384,128]{1,0:T(8,128)S(1)}) custom-call(s32[1,128]{1,0:T(1,128)S(1)} %bitcast.2, bf16[128,2048]{1,0:T(8,128)(2,1)S(1)} %copy-done.1, bf16[128,2048]{1,0:T(8,128)(2,1)S(1)} %copy-done.2), custom_call_target="tpu_custom_call" | custom-call | flops 536870912 | tf_op jit(solution)/shard_map/own_rest/pallas_call | solution.py:271
  6.3 1.4 %collective-permute-start.8 = (f32[384,128]{1,0:T(8,128)S(1)}, f32[384,128]{1,0:T(8,128)S(1)}, u32[]{:S(2)}, u32[]{:S(2)}) collective-permute-start(f32[384,128]{1,0:T(8,128)S(1)} %get-tuple-element.35), channel_id=1, source_target_pairs={{0,1},{1,0},{2,3},{3,2},{4,5},{5,4},{6,7},{7,6},{8,9},{9,8},{10,11... | collective-permute-start | bytes 589832 | tf_op jit(solution)/shard_map/ppermute | solution.py:301
  7.7 1.3 %collective-permute-start.9 = (f32[384,128]{1,0:T(8,128)S(1)}, f32[384,128]{1,0:T(8,128)S(1)}, u32[]{:S(2)}, u32[]{:S(2)}) collective-permute-start(f32[384,128]{1,0:T(8,128)S(1)} %get-tuple-element.36), channel_id=1, source_target_pairs={{0,2},{1,3},{2,0},{3,1},{4,6},{5,7},{6,4},{7,5},{8,10},{9,11},{10,... | collective-permute-start | bytes 589832 | tf_op jit(solution)/shard_map/ppermute | solution.py:301
  9.0 0.0 collective-permute-done.refs_1_
  9.0 2.1 %collective-permute-start.10 = (f32[384,128]{1,0:T(8,128)S(1)}, f32[384,128]{1,0:T(8,128)S(1)}, u32[]{:S(2)}, u32[]{:S(2)}) collective-permute-start(f32[384,128]{1,0:T(8,128)S(1)} %get-tuple-element.37), channel_id=1, source_target_pairs={{0,3},{1,2},{2,1},{3,0},{4,7},{5,6},{6,5},{7,4},{8,11},{9,10},{10,... | collective-permute-start | bytes 589832 | tf_op jit(solution)/shard_map/ppermute | solution.py:301
  11.2 0.0 collective-permute-done.1.refs_2_
  11.2 3.1 %collective-permute-done.2.refs_3_ = f32[392,128]{1,0:T(8,128)S(1)} collective-permute-done((f32[392,128]{1,0:T(8,128)S(1)}, f32[392,128]{1,0:T(8,128)S(1)}, u32[]{:S(2)}, u32[]{:S(2)}) %collective-permute-start.2) | collective-permute-done | bytes 200736 | tf_op jit(solution)/shard_map/ppermute | solution.py:301
  14.3 0.1 block_total.2
  14.4 4.3 %collective-permute-start.4 = (f32[392,128]{1,0:T(8,128)S(1)}, f32[392,128]{1,0:T(8,128)S(1)}, u32[]{:S(2)}, u32[]{:S(2)}) collective-permute-start(f32[392,128]{1,0:T(8,128)S(1)} %block_total.2), channel_id=1, source_target_pairs={{0,8},{4,12},{8,16},{12,20},{16,24},{20,28},{24,0},{28,4},{1,9},{5... | collective-permute-start | bytes 602120 | tf_op jit(solution)/shard_map/ppermute | solution.py:306
  18.7 2.3 %collective-permute-start.3 = (f32[392,128]{1,0:T(8,128)S(1)}, f32[392,128]{1,0:T(8,128)S(1)}, u32[]{:S(2)}, u32[]{:S(2)}) collective-permute-start(f32[392,128]{1,0:T(8,128)S(1)} %block_total.2), channel_id=1, source_target_pairs={{0,4},{4,8},{8,12},{12,16},{16,20},{20,24},{24,28},{28,0},{1,5},{5... | collective-permute-start | bytes 602120 | tf_op jit(solution)/shard_map/ppermute | solution.py:306
  21.0 0.0 collective-permute-done.8.refs_5_.refs_7_
  21.0 0.0 collective-permute-done.9.refs_6_.refs_8_
  21.1 1.7 %collective-permute-done.10.refs_7_.refs_9_ = f32[384,128]{1,0:T(8,128)S(1)} collective-permute-done((f32[384,128]{1,0:T(8,128)S(1)}, f32[384,128]{1,0:T(8,128)S(1)}, u32[]{:S(2)}, u32[]{:S(2)}) %collective-permute-start.10) | collective-permute-done | bytes 196640 | tf_op jit(solution)/shard_map/ppermute | solution.py:301
  22.7 0.1 block_total.3
  22.8 6.8 %collective-permute-start.12 = (f32[384,128]{1,0:T(8,128)S(1)}, f32[384,128]{1,0:T(8,128)S(1)}, u32[]{:S(2)}, u32[]{:S(2)}) collective-permute-start(f32[384,128]{1,0:T(8,128)S(1)} %block_total.3), channel_id=1, source_target_pairs={{0,8},{4,12},{8,16},{12,20},{16,24},{20,28},{24,0},{28,4},{1,9},{5... | collective-permute-start | bytes 589832 | tf_op jit(solution)/shard_map/ppermute | solution.py:306
  29.6 0.1 collective-permute-start.11
  29.7 0.0 collective-permute-done.4.refs_5_
  29.7 1.3 %collective-permute-done.3.refs_4_ = f32[392,128]{1,0:T(8,128)S(1)} collective-permute-done((f32[392,128]{1,0:T(8,128)S(1)}, f32[392,128]{1,0:T(8,128)S(1)}, u32[]{:S(2)}, u32[]{:S(2)}) %collective-permute-start.3) | collective-permute-done | bytes 200736 | tf_op jit(solution)/shard_map/ppermute | solution.py:306
  30.9 0.3 prefixes.2
  31.2 1.0 %collective-permute-start.5 = (f32[392,128]{1,0:T(8,128)S(1)}, f32[392,128]{1,0:T(8,128)S(1)}, u32[]{:S(2)}, u32[]{:S(2)}) collective-permute-start(f32[392,128]{1,0:T(8,128)S(1)} %get-tuple-element.29), channel_id=1, source_target_pairs={{0,1},{1,0},{2,3},{3,2},{4,5},{5,4},{6,7},{7,6},{8,9},{9,8},{10,11... | collective-permute-start | bytes 602120 | tf_op jit(solution)/shard_map/ppermute | solution.py:301
  32.2 3.6 %collective-permute-start.6 = (f32[392,128]{1,0:T(8,128)S(1)}, f32[392,128]{1,0:T(8,128)S(1)}, u32[]{:S(2)}, u32[]{:S(2)}) collective-permute-start(f32[392,128]{1,0:T(8,128)S(1)} %get-tuple-element.30), channel_id=1, source_target_pairs={{0,2},{1,3},{2,0},{3,1},{4,6},{5,7},{6,4},{7,5},{8,10},{9,11},{10,... | collective-permute-start | bytes 602120 | tf_op jit(solution)/shard_map/ppermute | solution.py:301
  35.8 0.0 copy-start
  35.8 1.0 %collective-permute-start.7 = (f32[392,128]{1,0:T(8,128)S(1)}, f32[392,128]{1,0:T(8,128)S(1)}, u32[]{:S(2)}, u32[]{:S(2)}) collective-permute-start(f32[392,128]{1,0:T(8,128)S(1)} %get-tuple-element.31), channel_id=1, source_target_pairs={{0,3},{1,2},{2,1},{3,0},{4,7},{5,6},{6,5},{7,4},{8,11},{9,10},{10,... | collective-permute-start | bytes 602120 | tf_op jit(solution)/shard_map/ppermute | solution.py:301
  36.8 0.0 collective-permute-done.12.refs_11_
  36.8 4.0 %collective-permute-done.11.refs_10_ = f32[384,128]{1,0:T(8,128)S(1)} collective-permute-done((f32[384,128]{1,0:T(8,128)S(1)}, f32[384,128]{1,0:T(8,128)S(1)}, u32[]{:S(2)}, u32[]{:S(2)}) %collective-permute-start.11) | collective-permute-done | bytes 196640 | tf_op jit(solution)/shard_map/ppermute | solution.py:306
  40.9 0.2 prefixes.3
  41.1 1.2 %collective-permute-start.13 = (f32[384,128]{1,0:T(8,128)S(1)}, f32[384,128]{1,0:T(8,128)S(1)}, u32[]{:S(2)}, u32[]{:S(2)}) collective-permute-start(f32[384,128]{1,0:T(8,128)S(1)} %get-tuple-element.39), channel_id=1, source_target_pairs={{0,1},{1,0},{2,3},{3,2},{4,5},{5,4},{6,7},{7,6},{8,9},{9,8},{10,11... | collective-permute-start | bytes 589832 | tf_op jit(solution)/shard_map/ppermute | solution.py:301
  42.3 0.0 collective-permute-start.14
  42.3 0.0 collective-permute-done.5.refs_1_
  42.3 0.0 copy-start.3
  42.3 1.5 %collective-permute-start.15 = (f32[384,128]{1,0:T(8,128)S(1)}, f32[384,128]{1,0:T(8,128)S(1)}, u32[]{:S(2)}, u32[]{:S(2)}) collective-permute-start(f32[384,128]{1,0:T(8,128)S(1)} %get-tuple-element.41), channel_id=1, source_target_pairs={{0,3},{1,2},{2,1},{3,0},{4,7},{5,6},{6,5},{7,4},{8,11},{9,10},{10,... | collective-permute-start | bytes 589832 | tf_op jit(solution)/shard_map/ppermute | solution.py:301
  43.8 0.8 %collective-permute-done.6.refs_2_ = f32[392,128]{1,0:T(8,128)S(1)} collective-permute-done((f32[392,128]{1,0:T(8,128)S(1)}, f32[392,128]{1,0:T(8,128)S(1)}, u32[]{:S(2)}, u32[]{:S(2)}) %collective-permute-start.6) | collective-permute-done | bytes 200736 | tf_op jit(solution)/shard_map/ppermute | solution.py:301
  44.6 4.4 %collective-permute-done.7.refs_3_ = f32[392,128]{1,0:T(8,128)S(1)} collective-permute-done((f32[392,128]{1,0:T(8,128)S(1)}, f32[392,128]{1,0:T(8,128)S(1)}, u32[]{:S(2)}, u32[]{:S(2)}) %collective-permute-start.7) | collective-permute-done | bytes 200736 | tf_op jit(solution)/shard_map/ppermute | solution.py:301
  49.0 0.0 copy-done
  49.0 0.0 copy-done.3
  49.0 6.4 %solve.1 = (f32[128,2048]{1,0:T(8,128)S(1)}, f32[128,2048]{1,0:T(8,128)S(1)}, f32[128,2048]{1,0:T(8,128)}) custom-call(f32[16]{0:T(128)S(1)} %copy-done.3, s32[1,128]{1,0:T(1,128)S(1)} %bitcast.3, bf16[128,2048]{1,0:T(8,128)(2,1)S(1)} %copy-done, bf16[128,2048]{1,0:T(8,128)(2,1)S(1)} %copy-done.1, bf16[128,2048]{1,0:T(8,128)(2,1)S(1)} %copy-done.2, ...), custom_call_target="tpu_custom_call" | custom-call | flops 6442450944 | tf_op jit(solution)/shard_map/solve/pallas_call | solution.py:271
  55.4 0.0 collective-permute-done.13.refs_1_
  55.4 0.0 collective-permute-done.14.refs_2_
  55.4 0.2 collective-permute-done.15.refs_3_
  55.7 1.3 %readout.1 = f32[128,2048]{1,0:T(8,128)} custom-call(f32[128,2048]{1,0:T(8,128)S(1)} %get-tuple-element.32.x_ref, f32[128,2048]{1,0:T(8,128)S(1)} %get-tuple-element.33.near_ref, f32[384,128]{1,0:T(8,128)S(1)} %get-tuple-element.38.refs_0_, f32[384,128]{1,0:T(8,128)S(1)} %collective-permute-done.13.refs_1_, ...), custom_call_target="tpu_custom_call", output_to_operand_aliasing={{}: (6, {})} | custom-call | flops 1073741824 | tf_op jit(solution)/shard_map/readout/pallas_call | solution.py:271
Async XLA Ops:
  0.0 5.6 %copy-start.1 = (bf16[128,2048]{1,0:T(8,128)(2,1)S(1)}, bf16[128,2048]{1,0:T(8,128)(2,1)}, u32[]{:S(2)}) copy-start(bf16[128,2048]{1,0:T(8,128)(2,1)} %k_ref.3) | copy-start | bytes 1572868
  0.0 5.6 %copy-start.2 = (bf16[128,2048]{1,0:T(8,128)(2,1)S(1)}, bf16[128,2048]{1,0:T(8,128)(2,1)}, u32[]{:S(2)}) copy-start(bf16[128,2048]{1,0:T(8,128)(2,1)} %v_ref.3) | copy-start | bytes 1572868
  2.2 6.8 %collective-permute-start = (f32[392,128]{1,0:T(8,128)S(1)}, f32[392,128]{1,0:T(8,128)S(1)}, u32[]{:S(2)}, u32[]{:S(2)}) collective-permute-start(f32[392,128]{1,0:T(8,128)S(1)} %get-tuple-element.25), channel_id=1, source_target_pairs={{0,1},{1,0},{2,3},{3,2},{4,5},{5,4},{6,7},{7,6},{8,9},{9,8},{10,11... | collective-permute-start | bytes 602120 | tf_op jit(solution)/shard_map/ppermute | solution.py:301
  4.3 1.3 %copy-start.4 = (s32[128]{0:T(128)S(1)}, s32[128]{0:T(128)}, u32[]{:S(2)}) copy-start(s32[128]{0:T(128)} %param.8) | copy-start | bytes 1540
  4.3 6.9 %collective-permute-start.1 = (f32[392,128]{1,0:T(8,128)S(1)}, f32[392,128]{1,0:T(8,128)S(1)}, u32[]{:S(2)}, u32[]{:S(2)}) collective-permute-start(f32[392,128]{1,0:T(8,128)S(1)} %get-tuple-element.26), channel_id=1, source_target_pairs={{0,2},{1,3},{2,0},{3,1},{4,6},{5,7},{6,4},{7,5},{8,10},{9,11},{10,... | collective-permute-start | bytes 602120 | tf_op jit(solution)/shard_map/ppermute | solution.py:301
  5.6 8.7 %collective-permute-start.2 = (f32[392,128]{1,0:T(8,128)S(1)}, f32[392,128]{1,0:T(8,128)S(1)}, u32[]{:S(2)}, u32[]{:S(2)}) collective-permute-start(f32[392,128]{1,0:T(8,128)S(1)} %get-tuple-element.27), channel_id=1, source_target_pairs={{0,3},{1,2},{2,1},{3,0},{4,7},{5,6},{6,5},{7,4},{8,11},{9,10},{10,... | collective-permute-start | bytes 602120 | tf_op jit(solution)/shard_map/ppermute | solution.py:301
  6.3 14.7 %collective-permute-start.8 = (f32[384,128]{1,0:T(8,128)S(1)}, f32[384,128]{1,0:T(8,128)S(1)}, u32[]{:S(2)}, u32[]{:S(2)}) collective-permute-start(f32[384,128]{1,0:T(8,128)S(1)} %get-tuple-element.35), channel_id=1, source_target_pairs={{0,1},{1,0},{2,3},{3,2},{4,5},{5,4},{6,7},{7,6},{8,9},{9,8},{10,11... | collective-permute-start | bytes 589832 | tf_op jit(solution)/shard_map/ppermute | solution.py:301
  7.7 13.3 %collective-permute-start.9 = (f32[384,128]{1,0:T(8,128)S(1)}, f32[384,128]{1,0:T(8,128)S(1)}, u32[]{:S(2)}, u32[]{:S(2)}) collective-permute-start(f32[384,128]{1,0:T(8,128)S(1)} %get-tuple-element.36), channel_id=1, source_target_pairs={{0,2},{1,3},{2,0},{3,1},{4,6},{5,7},{6,4},{7,5},{8,10},{9,11},{10,... | collective-permute-start | bytes 589832 | tf_op jit(solution)/shard_map/ppermute | solution.py:301
  9.0 13.7 %collective-permute-start.10 = (f32[384,128]{1,0:T(8,128)S(1)}, f32[384,128]{1,0:T(8,128)S(1)}, u32[]{:S(2)}, u32[]{:S(2)}) collective-permute-start(f32[384,128]{1,0:T(8,128)S(1)} %get-tuple-element.37), channel_id=1, source_target_pairs={{0,3},{1,2},{2,1},{3,0},{4,7},{5,6},{6,5},{7,4},{8,11},{9,10},{10,... | collective-permute-start | bytes 589832 | tf_op jit(solution)/shard_map/ppermute | solution.py:301
  14.4 15.3 %collective-permute-start.4 = (f32[392,128]{1,0:T(8,128)S(1)}, f32[392,128]{1,0:T(8,128)S(1)}, u32[]{:S(2)}, u32[]{:S(2)}) collective-permute-start(f32[392,128]{1,0:T(8,128)S(1)} %block_total.2), channel_id=1, source_target_pairs={{0,8},{4,12},{8,16},{12,20},{16,24},{20,28},{24,0},{28,4},{1,9},{5... | collective-permute-start | bytes 602120 | tf_op jit(solution)/shard_map/ppermute | solution.py:306
  18.7 12.2 %collective-permute-start.3 = (f32[392,128]{1,0:T(8,128)S(1)}, f32[392,128]{1,0:T(8,128)S(1)}, u32[]{:S(2)}, u32[]{:S(2)}) collective-permute-start(f32[392,128]{1,0:T(8,128)S(1)} %block_total.2), channel_id=1, source_target_pairs={{0,4},{4,8},{8,12},{12,16},{16,20},{20,24},{24,28},{28,0},{1,5},{5... | collective-permute-start | bytes 602120 | tf_op jit(solution)/shard_map/ppermute | solution.py:306
  22.8 14.0 %collective-permute-start.12 = (f32[384,128]{1,0:T(8,128)S(1)}, f32[384,128]{1,0:T(8,128)S(1)}, u32[]{:S(2)}, u32[]{:S(2)}) collective-permute-start(f32[384,128]{1,0:T(8,128)S(1)} %block_total.3), channel_id=1, source_target_pairs={{0,8},{4,12},{8,16},{12,20},{16,24},{20,28},{24,0},{28,4},{1,9},{5... | collective-permute-start | bytes 589832 | tf_op jit(solution)/shard_map/ppermute | solution.py:306
  29.6 11.3 %collective-permute-start.11 = (f32[384,128]{1,0:T(8,128)S(1)}, f32[384,128]{1,0:T(8,128)S(1)}, u32[]{:S(2)}, u32[]{:S(2)}) collective-permute-start(f32[384,128]{1,0:T(8,128)S(1)} %block_total.3), channel_id=1, source_target_pairs={{0,4},{4,8},{8,12},{12,16},{16,20},{20,24},{24,28},{28,0},{1,5},{5... | collective-permute-start | bytes 589832 | tf_op jit(solution)/shard_map/ppermute | solution.py:306
  31.2 11.1 %collective-permute-start.5 = (f32[392,128]{1,0:T(8,128)S(1)}, f32[392,128]{1,0:T(8,128)S(1)}, u32[]{:S(2)}, u32[]{:S(2)}) collective-permute-start(f32[392,128]{1,0:T(8,128)S(1)} %get-tuple-element.29), channel_id=1, source_target_pairs={{0,1},{1,0},{2,3},{3,2},{4,5},{5,4},{6,7},{7,6},{8,9},{9,8},{10,11... | collective-permute-start | bytes 602120 | tf_op jit(solution)/shard_map/ppermute | solution.py:301
  32.2 12.4 %collective-permute-start.6 = (f32[392,128]{1,0:T(8,128)S(1)}, f32[392,128]{1,0:T(8,128)S(1)}, u32[]{:S(2)}, u32[]{:S(2)}) collective-permute-start(f32[392,128]{1,0:T(8,128)S(1)} %get-tuple-element.30), channel_id=1, source_target_pairs={{0,2},{1,3},{2,0},{3,1},{4,6},{5,7},{6,4},{7,5},{8,10},{9,11},{10,... | collective-permute-start | bytes 602120 | tf_op jit(solution)/shard_map/ppermute | solution.py:301
  35.8 13.2 %copy-start = (bf16[128,2048]{1,0:T(8,128)(2,1)S(1)}, bf16[128,2048]{1,0:T(8,128)(2,1)}, u32[]{:S(2)}) copy-start(bf16[128,2048]{1,0:T(8,128)(2,1)} %q_ref.1) | copy-start | bytes 1572868
  35.8 13.2 %collective-permute-start.7 = (f32[392,128]{1,0:T(8,128)S(1)}, f32[392,128]{1,0:T(8,128)S(1)}, u32[]{:S(2)}, u32[]{:S(2)}) collective-permute-start(f32[392,128]{1,0:T(8,128)S(1)} %get-tuple-element.31), channel_id=1, source_target_pairs={{0,3},{1,2},{2,1},{3,0},{4,7},{5,6},{6,5},{7,4},{8,11},{9,10},{10,... | collective-permute-start | bytes 602120 | tf_op jit(solution)/shard_map/ppermute | solution.py:301
  41.1 14.3 %collective-permute-start.13 = (f32[384,128]{1,0:T(8,128)S(1)}, f32[384,128]{1,0:T(8,128)S(1)}, u32[]{:S(2)}, u32[]{:S(2)}) collective-permute-start(f32[384,128]{1,0:T(8,128)S(1)} %get-tuple-element.39), channel_id=1, source_target_pairs={{0,1},{1,0},{2,3},{3,2},{4,5},{5,4},{6,7},{7,6},{8,9},{9,8},{10,11... | collective-permute-start | bytes 589832 | tf_op jit(solution)/shard_map/ppermute | solution.py:301
  42.3 13.1 %collective-permute-start.14 = (f32[384,128]{1,0:T(8,128)S(1)}, f32[384,128]{1,0:T(8,128)S(1)}, u32[]{:S(2)}, u32[]{:S(2)}) collective-permute-start(f32[384,128]{1,0:T(8,128)S(1)} %get-tuple-element.40), channel_id=1, source_target_pairs={{0,2},{1,3},{2,0},{3,1},{4,6},{5,7},{6,4},{7,5},{8,10},{9,11},{10,... | collective-permute-start | bytes 589832 | tf_op jit(solution)/shard_map/ppermute | solution.py:301
  42.3 6.6 %copy-start.3 = (f32[16]{0:T(128)S(1)}, f32[16]{0:T(128)}, u32[]{:S(2)}) copy-start(f32[16]{0:T(128)} %ridge_ref.1) | copy-start | bytes 196
  42.3 13.3 %collective-permute-start.15 = (f32[384,128]{1,0:T(8,128)S(1)}, f32[384,128]{1,0:T(8,128)S(1)}, u32[]{:S(2)}, u32[]{:S(2)}) collective-permute-start(f32[384,128]{1,0:T(8,128)S(1)} %get-tuple-element.41), channel_id=1, source_target_pairs={{0,3},{1,2},{2,1},{3,0},{4,7},{5,6},{6,5},{7,4},{8,11},{9,10},{10,... | collective-permute-start | bytes 589832 | tf_op jit(solution)/shard_map/ppermute | solution.py:301

commit v6 on v5

--- a/solution.py
+++ b/solution.py
@@ -56,12 +56,13 @@
     return oldest, newest, weight
 
 
-def own_first_kernel(width, packs, early, count, ids_hbm, k_hbm, v_hbm, *refs):
+def own_first_kernel(width, packs, early, masks, ids_hbm, k_hbm, v_hbm, *refs):
+    count = len(masks)
     outs, (ids_ref, k_ref, v_ref, sems) = refs[:count], refs[count:]
     span = 2 * packs * width
     moves = [(ids_hbm, ids_ref)]
     for slot in range(count):
-        start = pl.multiple_of((lax.axis_index("near") ^ slot) * span, span)
+        start = pl.multiple_of((lax.axis_index("near") ^ masks[slot]) * span, span)
         moves.append((k_hbm.at[:, pl.ds(start, span)], k_ref.at[slot]))
         if early:
             moves.append((v_hbm.at[:, pl.ds(start, early * width)], v_ref.at[slot]))
@@ -99,11 +100,11 @@
         out[pl.ds(packs * width, extra), :] = jnp.concatenate([*seconds, *marks, filler], 0)
 
 
-def own_rest_kernel(width, heads, early, ids_ref, k_ref, v_ref, *outs):
+def own_rest_kernel(width, heads, early, masks, ids_ref, k_ref, v_ref, *outs):
     weight = last_of(ids_ref, width)[2]
     for slot, out in enumerate(outs):
         for head in range(early, heads):
-            at = (lax.axis_index("near") ^ slot) * heads + head
+            at = (lax.axis_index("near") ^ masks[slot]) * heads + head
             lanes = pl.ds(pl.multiple_of(at * width, width), width)
             keys = k_ref[:, lanes]
             scale = row_scale(keys.astype(jnp.float32))
@@ -130,7 +131,8 @@
         out[pl.ds(at, 2), :] = jnp.concatenate([newest, newest], 0)
 
 
-def prefix_kernel(at, count, steps, *refs):
+def prefix_kernel(at, steps, masks, out_masks, *refs):
+    count = len(masks)
     outs, refs = refs[-count:], refs[:-count]
     marked, marked_carries = refs[:count], refs[count : count + steps]
     slots, carries = refs[-count - steps : -steps], refs[-steps:]
@@ -139,11 +141,12 @@
     ends = marks_of(marked_carries, at)[1]
     carry = total([one[...] * flag(mark == oldest) for one, mark in zip(carries, ends)])
     me = lax.axis_index("near")
-    for target, out in enumerate(outs):
+    for mask, out in zip(out_masks, outs):
+        target = masks.index(mask)
         terms = [carry * flag(first[target] == oldest)]
         for source in range(count):
             if source != target:
-                before = jnp.where((me ^ source) < (me ^ target), 1.0, 0.0)
+                before = jnp.where((me ^ masks[source]) < (me ^ mask), 1.0, 0.0)
                 terms.append(slots[source][...] * (flag(last[source] == first[target]) * before))
         out[...] = total(terms)
 
@@ -153,7 +156,7 @@
     return dot(pair, jnp.concatenate([c_high, c_high], 0)) + dot(high, c_low)
 
 
-def solve_kernel(width, packs, early, together, ridge_ref, ids_ref, q_ref, k_ref, v_ref, *refs):
+def solve_kernel(width, packs, early, together, masks, ridge_ref, ids_ref, q_ref, k_ref, v_ref, *refs):
     slots, (x_ref, near_ref, out_hbm, out, sems) = refs[:-5], refs[-5:]
     upper, diagonal = triangle(width)
     ids = ids_ref[...].astype(jnp.float32)
@@ -176,7 +179,7 @@
                 jnp.where(diagonal, second, jnp.where(upper, flipped, packed)),
             ]
             for side in range(2):
-                head = ((lax.axis_index("near") ^ slot) * packs + pack) * 2 + side
+                head = ((lax.axis_index("near") ^ masks[slot]) * packs + pack) * 2 + side
                 lanes = pl.ds(pl.multiple_of(head * width, width), width)
                 wide = q_ref[:, lanes].astype(jnp.float32)
                 query = wide * row_scale(wide)
@@ -243,12 +246,12 @@
         copy.wait()
 
 
-def readout_kernel(width, heads, early, count, x_ref, near_ref, *refs):
-    slots, (out_hbm, out, sems) = refs[:count], refs[-3:]
+def readout_kernel(width, heads, early, masks, x_ref, near_ref, *refs):
+    slots, (out_hbm, out, sems) = refs[: len(masks)], refs[-3:]
     copies = []
     for slot, state in enumerate(slots):
         for head in range(early, heads):
-            at = (lax.axis_index("near") ^ slot) * heads + head
+            at = (lax.axis_index("near") ^ masks[slot]) * heads + head
             lanes = pl.ds(pl.multiple_of(at * width, width), width)
             high, low = split(x_ref[:, lanes])
             far = far_part(jnp.concatenate([high, low], 1), high, state[pl.ds((head - early) * width, width), :])
@@ -296,9 +299,10 @@
     flat = jax.ShapeDtypeStruct((row_count, columns), jnp.float32)
     unit = 16 * head_count * width * width * row_count
 
-    def exchange(slots):
-        return [slots[0]] + [
-            lax.ppermute(slots[j], "near", [(i, i ^ j) for i in range(near)]) for j in range(1, near)
+    def exchange(slots, masks):
+        return [
+            lax.ppermute(slot, "near", [(i, i ^ mask) for i in range(near)]) if mask else slot
+            for slot, mask in zip(slots, masks)
         ]
 
     def onward(value):
@@ -307,8 +311,11 @@
             for step in range(1, steps + 1)
         ]
 
+    rising = list(range(near))
+    falling = rising[:1] + rising[:0:-1]
+    orders = falling, rising, falling, rising
     own_first = call(
-        functools.partial(own_first_kernel, width, packs, early, near),
+        functools.partial(own_first_kernel, width, packs, early, orders[0]),
         "own_first",
         unit,
         [first_shape] * near,
@@ -322,7 +329,7 @@
         ],
     )
     own_rest = call(
-        functools.partial(own_rest_kernel, width, heads, early),
+        functools.partial(own_rest_kernel, width, heads, early, orders[1]),
         "own_rest",
         unit,
         [rest_shape] * near,
@@ -330,8 +337,11 @@
         (ids, key_vectors, value_vectors),
     )
     marked, marked_carries, states = [], [], []
-    for own, shape in ((own_first, first_shape), (own_rest, rest_shape)):
-        slots = exchange(own)
+    for piece, (own, shape) in enumerate(((own_first, first_shape), (own_rest, rest_shape))):
+        masks, out_masks = orders[piece], orders[2 + piece]
+        slots = exchange(own, masks)
+        if marked:
+            marked = [marked[orders[0].index(mask)] for mask in masks]
         block_total = call(
             functools.partial(total_kernel, mark_at, near),
             "block_total",
@@ -342,18 +352,18 @@
         )
         carries = onward(block_total)
         prefix = call(
-            functools.partial(prefix_kernel, mark_at, near, steps),
+            functools.partial(prefix_kernel, mark_at, steps, masks, out_masks),
             "prefixes",
             unit // 4,
             [shape] * near,
             [VMEM] * (len(marked) + len(marked_carries) + near + steps),
             (*marked, *marked_carries, *slots, *carries),
         )
-        states.append(exchange(prefix))
+        states.append(exchange(prefix, out_masks))
         marked, marked_carries = marked or slots, marked_carries or carries
     count = near * early
     solved, local, out = call(
-        functools.partial(solve_kernel, width, packs, early, max(1, 8 // heads)),
+        functools.partial(solve_kernel, width, packs, early, max(1, 8 // heads), orders[2]),
         "solve",
         12 * unit,
         [flat] * 3,
@@ -367,7 +377,7 @@
     )
     count = near * (heads - early)
     return call(
-        functools.partial(readout_kernel, width, heads, early, near),
+        functools.partial(readout_kernel, width, heads, early, orders[3]),
         "readout",
         2 * unit,
         flat,

time: 57.1 us -> 56.4 us (0.988)
  starting transfers between devices: 30.1 us -> 21.3 us
  waiting for transfers between devices: 15.5 us -> 23 us
    ppermute x4, starting transfers between devices: 13.6 us -> 8.2 us  [onward(): lax.ppermute(value, ('outer', 'half'), [(i, (i + step) % blocks) for i in...]
    ppermute x12, waiting for transfers between devices: 10.2 us -> 15.1 us  [exchange(): lax.ppermute(slot, 'near', [(i, i ^ mask) for i in range(near)])]
    ppermute x12, starting transfers between devices: 16.6 us -> 13.1 us  [exchange(): lax.ppermute(slot, 'near', [(i, i ^ mask) for i in range(near)])]
    ppermute x4, waiting for transfers between devices: 5.28 us -> 7.91 us  [onward(): lax.ppermute(value, ('outer', 'half'), [(i, (i + step) % blocks) for i in...]
  transfers between devices with their start and end apart: 16 -> 16, of which waited for: 7 -> 9; matrix products, arithmetic and copies ran while one was open for 0% -> 0% of each run, Pallas kernels for 14% -> 14%
where the time goes in v6:
time: 56.4 us; the launch traced here: 55.9 us
  waiting for transfers between devices  23 us (41%)
  starting transfers between devices  21.3 us (38%)
  Pallas kernels  11.2 us (20%)
    ppermute x12, waiting for transfers between devices, exchange(): lax.ppermute(slot, 'near', [(i, i ^ mask) for i in range(near)])  15.1 us
    ppermute x12, starting transfers between devices, exchange(): lax.ppermute(slot, 'near', [(i, i ^ mask) for i in range(near)])  13.1 us
    pallas_call x8, Pallas kernels, call(): pl.pallas_call(kernel, out_shape=out_shape, in_specs=in_specs, compiler_p...  11.2 us
    ppermute x4, starting transfers between devices, onward(): lax.ppermute(value, ('outer', 'half'), [(i, (i + step) % blocks) for i in...  8.2 us
    ppermute x4, waiting for transfers between devices, onward(): lax.ppermute(value, ('outer', 'half'), [(i, (i + step) % blocks) for i in...  7.91 us
  transfers between devices with their start and end apart: 16, of which 9 were waited for; matrix products, arithmetic and copies ran while one was open for 0% of the time, Pallas kernels for 14%

profile of v6, /device:TPU:1, one launch (start us, length us, event | category | flops | bytes accessed | tf_op | source)
XLA Modules:
  0.0 55.9 jit_solution(13991937527967640990)
XLA Ops:
  0.0 0.0 copy-start.1
  0.0 0.0 copy-start.2
  0.0 2.2 %own_first.1 = (f32[392,128]{1,0:T(8,128)S(1)}, f32[392,128]{1,0:T(8,128)S(1)}, f32[392,128]{1,0:T(8,128)S(1)}, f32[392,128]{1,0:T(8,128)S(1)}) custom-call(s32[1,128]{1,0:T(1,128)} %bitcast.1, bf16[128,2048]{1,0:T(8,128)(2,1)} %k_ref.3, bf16[128,2048]{1,0:T(8,128)(2,1)} %v_ref.3), custom_call_target="tpu_custom_call" | custom-call | flops 536870912 | tf_op jit(solution)/shard_map/own_first/pallas_call | solution.py:274
  2.2 3.1 %collective-permute-start = (f32[392,128]{1,0:T(8,128)S(1)}, f32[392,128]{1,0:T(8,128)S(1)}, u32[]{:S(2)}, u32[]{:S(2)}) collective-permute-start(f32[392,128]{1,0:T(8,128)S(1)} %get-tuple-element.25), channel_id=1, source_target_pairs={{0,3},{1,2},{2,1},{3,0},{4,7},{5,6},{6,5},{7,4},{8,11},{9,10},{10,... | collective-permute-start | bytes 602120 | tf_op jit(solution)/shard_map/ppermute | solution.py:304
  5.3 0.0 copy-start.4
  5.3 0.2 collective-permute-start.1
  5.5 0.2 collective-permute-start.2
  5.7 0.0 copy-done.1
  5.7 0.0 copy-done.2
  5.7 0.3 copy-done.4
  6.0 0.7 %own_rest.1 = (f32[384,128]{1,0:T(8,128)S(1)}, f32[384,128]{1,0:T(8,128)S(1)}, f32[384,128]{1,0:T(8,128)S(1)}, f32[384,128]{1,0:T(8,128)S(1)}) custom-call(s32[1,128]{1,0:T(1,128)S(1)} %bitcast.2, bf16[128,2048]{1,0:T(8,128)(2,1)S(1)} %copy-done.1, bf16[128,2048]{1,0:T(8,128)(2,1)S(1)} %copy-done.2), custom_call_target="tpu_custom_call" | custom-call | flops 536870912 | tf_op jit(solution)/shard_map/own_rest/pallas_call | solution.py:274
  6.7 1.1 %collective-permute-start.8 = (f32[384,128]{1,0:T(8,128)S(1)}, f32[384,128]{1,0:T(8,128)S(1)}, u32[]{:S(2)}, u32[]{:S(2)}) collective-permute-start(f32[384,128]{1,0:T(8,128)S(1)} %get-tuple-element.35), channel_id=1, source_target_pairs={{0,1},{1,0},{2,3},{3,2},{4,5},{5,4},{6,7},{7,6},{8,9},{9,8},{10,11... | collective-permute-start | bytes 589832 | tf_op jit(solution)/shard_map/ppermute | solution.py:304
  7.7 1.3 %collective-permute-start.9 = (f32[384,128]{1,0:T(8,128)S(1)}, f32[384,128]{1,0:T(8,128)S(1)}, u32[]{:S(2)}, u32[]{:S(2)}) collective-permute-start(f32[384,128]{1,0:T(8,128)S(1)} %get-tuple-element.36), channel_id=1, source_target_pairs={{0,2},{1,3},{2,0},{3,1},{4,6},{5,7},{6,4},{7,5},{8,10},{9,11},{10,... | collective-permute-start | bytes 589832 | tf_op jit(solution)/shard_map/ppermute | solution.py:304
  9.0 1.0 %collective-permute-done.refs_1_.refs_3_ = f32[392,128]{1,0:T(8,128)S(1)} collective-permute-done((f32[392,128]{1,0:T(8,128)S(1)}, f32[392,128]{1,0:T(8,128)S(1)}, u32[]{:S(2)}, u32[]{:S(2)}) %collective-permute-start) | collective-permute-done | bytes 200736 | tf_op jit(solution)/shard_map/ppermute | solution.py:304
  10.1 2.0 %collective-permute-start.10 = (f32[384,128]{1,0:T(8,128)S(1)}, f32[384,128]{1,0:T(8,128)S(1)}, u32[]{:S(2)}, u32[]{:S(2)}) collective-permute-start(f32[384,128]{1,0:T(8,128)S(1)} %get-tuple-element.37), channel_id=1, source_target_pairs={{0,3},{1,2},{2,1},{3,0},{4,7},{5,6},{6,5},{7,4},{8,11},{9,10},{10,... | collective-permute-start | bytes 589832 | tf_op jit(solution)/shard_map/ppermute | solution.py:304
  12.1 2.1 %collective-permute-done.1.refs_2_ = f32[392,128]{1,0:T(8,128)S(1)} collective-permute-done((f32[392,128]{1,0:T(8,128)S(1)}, f32[392,128]{1,0:T(8,128)S(1)}, u32[]{:S(2)}, u32[]{:S(2)}) %collective-permute-start.1) | collective-permute-done | bytes 200736 | tf_op jit(solution)/shard_map/ppermute | solution.py:304
  14.2 0.8 %collective-permute-done.2.refs_3_.refs_1_ = f32[392,128]{1,0:T(8,128)S(1)} collective-permute-done((f32[392,128]{1,0:T(8,128)S(1)}, f32[392,128]{1,0:T(8,128)S(1)}, u32[]{:S(2)}, u32[]{:S(2)}) %collective-permute-start.2) | collective-permute-done | bytes 200736 | tf_op jit(solution)/shard_map/ppermute | solution.py:304
  15.1 0.1 block_total.2
  15.1 3.0 %collective-permute-start.4 = (f32[392,128]{1,0:T(8,128)S(1)}, f32[392,128]{1,0:T(8,128)S(1)}, u32[]{:S(2)}, u32[]{:S(2)}) collective-permute-start(f32[392,128]{1,0:T(8,128)S(1)} %block_total.2), channel_id=1, source_target_pairs={{0,8},{4,12},{8,16},{12,20},{16,24},{20,28},{24,0},{28,4},{1,9},{5... | collective-permute-start | bytes 602120 | tf_op jit(solution)/shard_map/ppermute | solution.py:310
  18.2 2.3 %collective-permute-start.3 = (f32[392,128]{1,0:T(8,128)S(1)}, f32[392,128]{1,0:T(8,128)S(1)}, u32[]{:S(2)}, u32[]{:S(2)}) collective-permute-start(f32[392,128]{1,0:T(8,128)S(1)} %block_total.2), channel_id=1, source_target_pairs={{0,4},{4,8},{8,12},{12,16},{16,20},{20,24},{24,28},{28,0},{1,5},{5... | collective-permute-start | bytes 602120 | tf_op jit(solution)/shard_map/ppermute | solution.py:310
  20.5 0.0 collective-permute-done.8.refs_5_.refs_7_
  20.5 0.0 collective-permute-done.9.refs_6_.refs_8_
  20.5 6.3 %collective-permute-done.10.refs_7_.refs_9_ = f32[384,128]{1,0:T(8,128)S(1)} collective-permute-done((f32[384,128]{1,0:T(8,128)S(1)}, f32[384,128]{1,0:T(8,128)S(1)}, u32[]{:S(2)}, u32[]{:S(2)}) %collective-permute-start.10) | collective-permute-done | bytes 196640 | tf_op jit(solution)/shard_map/ppermute | solution.py:304
  26.8 0.1 block_total.3
  26.8 2.9 %collective-permute-start.12 = (f32[384,128]{1,0:T(8,128)S(1)}, f32[384,128]{1,0:T(8,128)S(1)}, u32[]{:S(2)}, u32[]{:S(2)}) collective-permute-start(f32[384,128]{1,0:T(8,128)S(1)} %block_total.3), channel_id=1, source_target_pairs={{0,8},{4,12},{8,16},{12,20},{16,24},{20,28},{24,0},{28,4},{1,9},{5... | collective-permute-start | bytes 589832 | tf_op jit(solution)/shard_map/ppermute | solution.py:310
  29.7 0.0 collective-permute-start.11
  29.7 0.0 collective-permute-done.4.refs_5_
  29.7 0.4 collective-permute-done.3.refs_4_
  30.1 0.3 prefixes.2
  30.4 2.8 %collective-permute-start.5 = (f32[392,128]{1,0:T(8,128)S(1)}, f32[392,128]{1,0:T(8,128)S(1)}, u32[]{:S(2)}, u32[]{:S(2)}) collective-permute-start(f32[392,128]{1,0:T(8,128)S(1)} %get-tuple-element.29), channel_id=1, source_target_pairs={{0,3},{1,2},{2,1},{3,0},{4,7},{5,6},{6,5},{7,4},{8,11},{9,10},{10,... | collective-permute-start | bytes 602120 | tf_op jit(solution)/shard_map/ppermute | solution.py:304
  33.1 0.0 collective-permute-start.6
  33.1 0.0 copy-start
  33.1 0.4 collective-permute-start.7
  33.5 0.0 collective-permute-done.12.refs_11_
  33.5 7.5 %collective-permute-done.11.refs_10_ = f32[384,128]{1,0:T(8,128)S(1)} collective-permute-done((f32[384,128]{1,0:T(8,128)S(1)}, f32[384,128]{1,0:T(8,128)S(1)}, u32[]{:S(2)}, u32[]{:S(2)}) %collective-permute-start.11) | collective-permute-done | bytes 196640 | tf_op jit(solution)/shard_map/ppermute | solution.py:310
  41.0 0.2 prefixes.3
  41.3 0.6 %collective-permute-start.13 = (f32[384,128]{1,0:T(8,128)S(1)}, f32[384,128]{1,0:T(8,128)S(1)}, u32[]{:S(2)}, u32[]{:S(2)}) collective-permute-start(f32[384,128]{1,0:T(8,128)S(1)} %get-tuple-element.39), channel_id=1, source_target_pairs={{0,1},{1,0},{2,3},{3,2},{4,5},{5,4},{6,7},{7,6},{8,9},{9,8},{10,11... | collective-permute-start | bytes 589832 | tf_op jit(solution)/shard_map/ppermute | solution.py:304
  41.9 0.0 collective-permute-start.14
  41.9 0.7 %collective-permute-done.5.refs_1_ = f32[392,128]{1,0:T(8,128)S(1)} collective-permute-done((f32[392,128]{1,0:T(8,128)S(1)}, f32[392,128]{1,0:T(8,128)S(1)}, u32[]{:S(2)}, u32[]{:S(2)}) %collective-permute-start.5) | collective-permute-done | bytes 200736 | tf_op jit(solution)/shard_map/ppermute | solution.py:304
  42.6 0.0 copy-start.3
  42.6 1.4 %collective-permute-start.15 = (f32[384,128]{1,0:T(8,128)S(1)}, f32[384,128]{1,0:T(8,128)S(1)}, u32[]{:S(2)}, u32[]{:S(2)}) collective-permute-start(f32[384,128]{1,0:T(8,128)S(1)} %get-tuple-element.41), channel_id=1, source_target_pairs={{0,3},{1,2},{2,1},{3,0},{4,7},{5,6},{6,5},{7,4},{8,11},{9,10},{10,... | collective-permute-start | bytes 589832 | tf_op jit(solution)/shard_map/ppermute | solution.py:304
  44.0 1.9 %collective-permute-done.6.refs_2_ = f32[392,128]{1,0:T(8,128)S(1)} collective-permute-done((f32[392,128]{1,0:T(8,128)S(1)}, f32[392,128]{1,0:T(8,128)S(1)}, u32[]{:S(2)}, u32[]{:S(2)}) %collective-permute-start.6) | collective-permute-done | bytes 200736 | tf_op jit(solution)/shard_map/ppermute | solution.py:304
  45.8 0.0 collective-permute-done.7.refs_3_
  45.8 0.0 copy-done
  45.8 0.0 copy-done.3
  45.8 6.4 %solve.1 = (f32[128,2048]{1,0:T(8,128)S(1)}, f32[128,2048]{1,0:T(8,128)S(1)}, f32[128,2048]{1,0:T(8,128)}) custom-call(f32[16]{0:T(128)S(1)} %copy-done.3, s32[1,128]{1,0:T(1,128)S(1)} %bitcast.3, bf16[128,2048]{1,0:T(8,128)(2,1)S(1)} %copy-done, bf16[128,2048]{1,0:T(8,128)(2,1)S(1)} %copy-done.1, bf16[128,2048]{1,0:T(8,128)(2,1)S(1)} %copy-done.2, ...), custom_call_target="tpu_custom_call" | custom-call | flops 6442450944 | tf_op jit(solution)/shard_map/solve/pallas_call | solution.py:274
  52.3 0.0 collective-permute-done.13.refs_1_
  52.3 0.0 collective-permute-done.14.refs_2_
  52.3 2.3 %collective-permute-done.15.refs_3_ = f32[384,128]{1,0:T(8,128)S(1)} collective-permute-done((f32[384,128]{1,0:T(8,128)S(1)}, f32[384,128]{1,0:T(8,128)S(1)}, u32[]{:S(2)}, u32[]{:S(2)}) %collective-permute-start.15) | collective-permute-done | bytes 196640 | tf_op jit(solution)/shard_map/ppermute | solution.py:304
  54.6 1.3 %readout.1 = f32[128,2048]{1,0:T(8,128)} custom-call(f32[128,2048]{1,0:T(8,128)S(1)} %get-tuple-element.32.x_ref, f32[128,2048]{1,0:T(8,128)S(1)} %get-tuple-element.33.near_ref, f32[384,128]{1,0:T(8,128)S(1)} %get-tuple-element.38.refs_0_, f32[384,128]{1,0:T(8,128)S(1)} %collective-permute-done.13.refs_1_, ...), custom_call_target="tpu_custom_call", output_to_operand_aliasing={{}: (6, {})} | custom-call | flops 1073741824 | tf_op jit(solution)/shard_map/readout/pallas_call | solution.py:274
Async XLA Ops:
  0.0 5.7 %copy-start.1 = (bf16[128,2048]{1,0:T(8,128)(2,1)S(1)}, bf16[128,2048]{1,0:T(8,128)(2,1)}, u32[]{:S(2)}) copy-start(bf16[128,2048]{1,0:T(8,128)(2,1)} %k_ref.3) | copy-start | bytes 1572868
  0.0 5.7 %copy-start.2 = (bf16[128,2048]{1,0:T(8,128)(2,1)S(1)}, bf16[128,2048]{1,0:T(8,128)(2,1)}, u32[]{:S(2)}) copy-start(bf16[128,2048]{1,0:T(8,128)(2,1)} %v_ref.3) | copy-start | bytes 1572868
  2.2 7.9 %collective-permute-start = (f32[392,128]{1,0:T(8,128)S(1)}, f32[392,128]{1,0:T(8,128)S(1)}, u32[]{:S(2)}, u32[]{:S(2)}) collective-permute-start(f32[392,128]{1,0:T(8,128)S(1)} %get-tuple-element.25), channel_id=1, source_target_pairs={{0,3},{1,2},{2,1},{3,0},{4,7},{5,6},{6,5},{7,4},{8,11},{9,10},{10,... | collective-permute-start | bytes 602120 | tf_op jit(solution)/shard_map/ppermute | solution.py:304
  5.3 0.7 %copy-start.4 = (s32[128]{0:T(128)S(1)}, s32[128]{0:T(128)}, u32[]{:S(2)}) copy-start(s32[128]{0:T(128)} %param.8) | copy-start | bytes 1540
  5.3 8.9 %collective-permute-start.1 = (f32[392,128]{1,0:T(8,128)S(1)}, f32[392,128]{1,0:T(8,128)S(1)}, u32[]{:S(2)}, u32[]{:S(2)}) collective-permute-start(f32[392,128]{1,0:T(8,128)S(1)} %get-tuple-element.26), channel_id=1, source_target_pairs={{0,2},{1,3},{2,0},{3,1},{4,6},{5,7},{6,4},{7,5},{8,10},{9,11},{10,... | collective-permute-start | bytes 602120 | tf_op jit(solution)/shard_map/ppermute | solution.py:304
  5.5 9.6 %collective-permute-start.2 = (f32[392,128]{1,0:T(8,128)S(1)}, f32[392,128]{1,0:T(8,128)S(1)}, u32[]{:S(2)}, u32[]{:S(2)}) collective-permute-start(f32[392,128]{1,0:T(8,128)S(1)} %get-tuple-element.27), channel_id=1, source_target_pairs={{0,1},{1,0},{2,3},{3,2},{4,5},{5,4},{6,7},{7,6},{8,9},{9,8},{10,11... | collective-permute-start | bytes 602120 | tf_op jit(solution)/shard_map/ppermute | solution.py:304
  6.7 13.8 %collective-permute-start.8 = (f32[384,128]{1,0:T(8,128)S(1)}, f32[384,128]{1,0:T(8,128)S(1)}, u32[]{:S(2)}, u32[]{:S(2)}) collective-permute-start(f32[384,128]{1,0:T(8,128)S(1)} %get-tuple-element.35), channel_id=1, source_target_pairs={{0,1},{1,0},{2,3},{3,2},{4,5},{5,4},{6,7},{7,6},{8,9},{9,8},{10,11... | collective-permute-start | bytes 589832 | tf_op jit(solution)/shard_map/ppermute | solution.py:304
  7.7 12.8 %collective-permute-start.9 = (f32[384,128]{1,0:T(8,128)S(1)}, f32[384,128]{1,0:T(8,128)S(1)}, u32[]{:S(2)}, u32[]{:S(2)}) collective-permute-start(f32[384,128]{1,0:T(8,128)S(1)} %get-tuple-element.36), channel_id=1, source_target_pairs={{0,2},{1,3},{2,0},{3,1},{4,6},{5,7},{6,4},{7,5},{8,10},{9,11},{10,... | collective-permute-start | bytes 589832 | tf_op jit(solution)/shard_map/ppermute | solution.py:304
  10.1 16.7 %collective-permute-start.10 = (f32[384,128]{1,0:T(8,128)S(1)}, f32[384,128]{1,0:T(8,128)S(1)}, u32[]{:S(2)}, u32[]{:S(2)}) collective-permute-start(f32[384,128]{1,0:T(8,128)S(1)} %get-tuple-element.37), channel_id=1, source_target_pairs={{0,3},{1,2},{2,1},{3,0},{4,7},{5,6},{6,5},{7,4},{8,11},{9,10},{10,... | collective-permute-start | bytes 589832 | tf_op jit(solution)/shard_map/ppermute | solution.py:304
  15.1 14.5 %collective-permute-start.4 = (f32[392,128]{1,0:T(8,128)S(1)}, f32[392,128]{1,0:T(8,128)S(1)}, u32[]{:S(2)}, u32[]{:S(2)}) collective-permute-start(f32[392,128]{1,0:T(8,128)S(1)} %block_total.2), channel_id=1, source_target_pairs={{0,8},{4,12},{8,16},{12,20},{16,24},{20,28},{24,0},{28,4},{1,9},{5... | collective-permute-start | bytes 602120 | tf_op jit(solution)/shard_map/ppermute | solution.py:310
  18.2 11.9 %collective-permute-start.3 = (f32[392,128]{1,0:T(8,128)S(1)}, f32[392,128]{1,0:T(8,128)S(1)}, u32[]{:S(2)}, u32[]{:S(2)}) collective-permute-start(f32[392,128]{1,0:T(8,128)S(1)} %block_total.2), channel_id=1, source_target_pairs={{0,4},{4,8},{8,12},{12,16},{16,20},{20,24},{24,28},{28,0},{1,5},{5... | collective-permute-start | bytes 602120 | tf_op jit(solution)/shard_map/ppermute | solution.py:310
  26.8 6.7 %collective-permute-start.12 = (f32[384,128]{1,0:T(8,128)S(1)}, f32[384,128]{1,0:T(8,128)S(1)}, u32[]{:S(2)}, u32[]{:S(2)}) collective-permute-start(f32[384,128]{1,0:T(8,128)S(1)} %block_total.3), channel_id=1, source_target_pairs={{0,8},{4,12},{8,16},{12,20},{16,24},{20,28},{24,0},{28,4},{1,9},{5... | collective-permute-start | bytes 589832 | tf_op jit(solution)/shard_map/ppermute | solution.py:310
  29.7 11.4 %collective-permute-start.11 = (f32[384,128]{1,0:T(8,128)S(1)}, f32[384,128]{1,0:T(8,128)S(1)}, u32[]{:S(2)}, u32[]{:S(2)}) collective-permute-start(f32[384,128]{1,0:T(8,128)S(1)} %block_total.3), channel_id=1, source_target_pairs={{0,4},{4,8},{8,12},{12,16},{16,20},{20,24},{24,28},{28,0},{1,5},{5... | collective-permute-start | bytes 589832 | tf_op jit(solution)/shard_map/ppermute | solution.py:310
  30.4 12.2 %collective-permute-start.5 = (f32[392,128]{1,0:T(8,128)S(1)}, f32[392,128]{1,0:T(8,128)S(1)}, u32[]{:S(2)}, u32[]{:S(2)}) collective-permute-start(f32[392,128]{1,0:T(8,128)S(1)} %get-tuple-element.29), channel_id=1, source_target_pairs={{0,3},{1,2},{2,1},{3,0},{4,7},{5,6},{6,5},{7,4},{8,11},{9,10},{10,... | collective-permute-start | bytes 602120 | tf_op jit(solution)/shard_map/ppermute | solution.py:304
  33.1 12.7 %collective-permute-start.6 = (f32[392,128]{1,0:T(8,128)S(1)}, f32[392,128]{1,0:T(8,128)S(1)}, u32[]{:S(2)}, u32[]{:S(2)}) collective-permute-start(f32[392,128]{1,0:T(8,128)S(1)} %get-tuple-element.30), channel_id=1, source_target_pairs={{0,2},{1,3},{2,0},{3,1},{4,6},{5,7},{6,4},{7,5},{8,10},{9,11},{10,... | collective-permute-start | bytes 602120 | tf_op jit(solution)/shard_map/ppermute | solution.py:304
  33.1 12.7 %copy-start = (bf16[128,2048]{1,0:T(8,128)(2,1)S(1)}, bf16[128,2048]{1,0:T(8,128)(2,1)}, u32[]{:S(2)}) copy-start(bf16[128,2048]{1,0:T(8,128)(2,1)} %q_ref.1) | copy-start | bytes 1572868
  33.1 12.7 %collective-permute-start.7 = (f32[392,128]{1,0:T(8,128)S(1)}, f32[392,128]{1,0:T(8,128)S(1)}, u32[]{:S(2)}, u32[]{:S(2)}) collective-permute-start(f32[392,128]{1,0:T(8,128)S(1)} %get-tuple-element.31), channel_id=1, source_target_pairs={{0,1},{1,0},{2,3},{3,2},{4,5},{5,4},{6,7},{7,6},{8,9},{9,8},{10,11... | collective-permute-start | bytes 602120 | tf_op jit(solution)/shard_map/ppermute | solution.py:304
  41.3 11.0 %collective-permute-start.13 = (f32[384,128]{1,0:T(8,128)S(1)}, f32[384,128]{1,0:T(8,128)S(1)}, u32[]{:S(2)}, u32[]{:S(2)}) collective-permute-start(f32[384,128]{1,0:T(8,128)S(1)} %get-tuple-element.39), channel_id=1, source_target_pairs={{0,1},{1,0},{2,3},{3,2},{4,5},{5,4},{6,7},{7,6},{8,9},{9,8},{10,11... | collective-permute-start | bytes 589832 | tf_op jit(solution)/shard_map/ppermute | solution.py:304
  41.9 10.4 %collective-permute-start.14 = (f32[384,128]{1,0:T(8,128)S(1)}, f32[384,128]{1,0:T(8,128)S(1)}, u32[]{:S(2)}, u32[]{:S(2)}) collective-permute-start(f32[384,128]{1,0:T(8,128)S(1)} %get-tuple-element.40), channel_id=1, source_target_pairs={{0,2},{1,3},{2,0},{3,1},{4,6},{5,7},{6,4},{7,5},{8,10},{9,11},{10,... | collective-permute-start | bytes 589832 | tf_op jit(solution)/shard_map/ppermute | solution.py:304
  42.6 3.3 %copy-start.3 = (f32[16]{0:T(128)S(1)}, f32[16]{0:T(128)}, u32[]{:S(2)}) copy-start(f32[16]{0:T(128)} %ridge_ref.1) | copy-start | bytes 196
  42.6 12.0 %collective-permute-start.15 = (f32[384,128]{1,0:T(8,128)S(1)}, f32[384,128]{1,0:T(8,128)S(1)}, u32[]{:S(2)}, u32[]{:S(2)}) collective-permute-start(f32[384,128]{1,0:T(8,128)S(1)} %get-tuple-element.41), channel_id=1, source_target_pairs={{0,3},{1,2},{2,1},{3,0},{4,7},{5,6},{6,5},{7,4},{8,11},{9,10},{10,... | collective-permute-start | bytes 589832 | tf_op jit(solution)/shard_map/ppermute | solution.py:304

commit v7 on v6

--- a/solution.py
+++ b/solution.py
@@ -56,62 +56,72 @@
     return oldest, newest, weight
 
 
+def first_slot(width, packs, early, out, keys_of, values_of, last):
+    oldest, newest, weight = last
+    upper, diagonal = triangle(width)
+    extra = extra_of(packs)
+    marks = [jnp.broadcast_to(one + 1.0, (1, width)) for one in (oldest, newest)]
+    filler = jnp.zeros((extra - packs - 2, width), jnp.float32)
+    grams = []
+    for head in range(2 * packs):
+        keys = keys_of(head)
+        wide = keys.astype(jnp.float32)
+        scale = row_scale(wide)
+        light = weight * scale
+        high, low = split(light * scale * wide)
+        if head < early:
+            v_high, v_low = split(light * values_of(head).astype(jnp.float32))
+            high, low = jnp.concatenate([high, v_high], 1), jnp.concatenate([low, v_low], 1)
+        both = dot_rows(jnp.concatenate([keys, keys], 0), jnp.concatenate([high, low], 0))
+        grams.append(both[:, :width])
+        if head < early:
+            out[pl.ds((packs + head) * width + extra, width), :] = both[:, width:]
+    seconds = []
+    for pack in range(packs):
+        one, two = grams[2 * pack : 2 * pack + 2]
+        out[pl.ds(pack * width, width), :] = jnp.where(upper, one, two)
+        seconds.append(jnp.sum(jnp.where(diagonal, two, 0.0), 0, keepdims=True))
+    out[pl.ds(packs * width, extra), :] = jnp.concatenate([*seconds, *marks, filler], 0)
+
+
 def own_first_kernel(width, packs, early, masks, ids_hbm, k_hbm, v_hbm, *refs):
-    count = len(masks)
-    outs, (ids_ref, k_ref, v_ref, sems) = refs[:count], refs[count:]
+    outs, (ids_ref, k_ref, v_ref, sems) = refs[: len(masks)], refs[len(masks) :]
     span = 2 * packs * width
     moves = [(ids_hbm, ids_ref)]
-    for slot in range(count):
-        start = pl.multiple_of((lax.axis_index("near") ^ masks[slot]) * span, span)
+    for slot, mask in enumerate(masks):
+        start = pl.multiple_of((lax.axis_index("near") ^ mask) * span, span)
         moves.append((k_hbm.at[:, pl.ds(start, span)], k_ref.at[slot]))
         if early:
             moves.append((v_hbm.at[:, pl.ds(start, early * width)], v_ref.at[slot]))
     copies = [pltpu.make_async_copy(*move, sems.at[number]) for number, move in enumerate(moves)]
     for copy in copies:
         copy.start()
-    upper, diagonal = triangle(width)
     for copy in copies:
         copy.wait()
-    oldest, newest, weight = last_of(ids_ref, width)
-    marks = [jnp.broadcast_to(one + 1.0, (1, width)) for one in (oldest, newest)]
-    extra = extra_of(packs)
-    filler = jnp.zeros((extra - packs - 2, width), jnp.float32)
+    last = last_of(ids_ref, width)
     for slot, out in enumerate(outs):
-        grams = []
-        for head in range(2 * packs):
-            lanes = pl.ds(head * width, width)
-            keys = k_ref[slot, :, lanes]
-            wide = keys.astype(jnp.float32)
-            scale = row_scale(wide)
-            light = weight * scale
-            high, low = split(light * scale * wide)
-            if head < early:
-                v_high, v_low = split(light * v_ref[slot, :, lanes].astype(jnp.float32))
-                high, low = jnp.concatenate([high, v_high], 1), jnp.concatenate([low, v_low], 1)
-            both = dot_rows(jnp.concatenate([keys, keys], 0), jnp.concatenate([high, low], 0))
-            grams.append(both[:, :width])
-            if head < early:
-                out[pl.ds((packs + head) * width + extra, width), :] = both[:, width:]
-        seconds = []
-        for pack in range(packs):
-            one, two = grams[2 * pack : 2 * pack + 2]
-            out[pl.ds(pack * width, width), :] = jnp.where(upper, one, two)
-            seconds.append(jnp.sum(jnp.where(diagonal, two, 0.0), 0, keepdims=True))
-        out[pl.ds(packs * width, extra), :] = jnp.concatenate([*seconds, *marks, filler], 0)
-
-
-def own_rest_kernel(width, heads, early, masks, ids_ref, k_ref, v_ref, *outs):
-    weight = last_of(ids_ref, width)[2]
-    for slot, out in enumerate(outs):
-        for head in range(early, heads):
-            at = (lax.axis_index("near") ^ masks[slot]) * heads + head
-            lanes = pl.ds(pl.multiple_of(at * width, width), width)
+        keys_of, values_of = (lambda head, ref=ref: ref[slot, :, pl.ds(head * width, width)] for ref in (k_ref, v_ref))
+        first_slot(width, packs, early, out, keys_of, values_of, last)
+
+
+def own_rest_kernel(width, packs, early, masks, ids_ref, k_ref, v_ref, *outs):
+    last = last_of(ids_ref, width)
+
+    def lanes_of(mask, head):
+        at = (lax.axis_index("near") ^ mask) * 2 * packs + head
+        return pl.ds(pl.multiple_of(at * width, width), width)
+
+    for mask, out in zip(masks, outs):
+        for head in range(early, 2 * packs):
+            lanes = lanes_of(mask, head)
             keys = k_ref[:, lanes]
             scale = row_scale(keys.astype(jnp.float32))
-            high, low = split(weight * scale * v_ref[:, lanes].astype(jnp.float32))
+            high, low = split(last[2] * scale * v_ref[:, lanes].astype(jnp.float32))
             out[pl.ds((head - early) * width, width), :] = dot_rows(
                 jnp.concatenate([keys, keys], 0), jnp.concatenate([high, low], 0)
             )
+    keys_of, values_of = (lambda head, ref=ref: ref[:, lanes_of(0, head)] for ref in (k_ref, v_ref))
+    first_slot(width, packs, early, outs[-1], keys_of, values_of, last)
 
 
 def marks_of(refs, at):
@@ -314,28 +324,29 @@
     rising = list(range(near))
     falling = rising[:1] + rising[:0:-1]
     orders = falling, rising, falling, rising
-    own_first = call(
-        functools.partial(own_first_kernel, width, packs, early, orders[0]),
+    own_away = call(
+        functools.partial(own_first_kernel, width, packs, early, orders[0][1:]),
         "own_first",
         unit,
-        [first_shape] * near,
+        [first_shape] * (near - 1),
         [HBM] * 3,
         [pltpu.with_memory_space_constraint(one, pltpu.HBM) for one in (ids, key_vectors, value_vectors)],
         scratch_shapes=[
             pltpu.VMEM(ids.shape, ids.dtype),
-            pltpu.VMEM((near, row_count, heads * width), key_vectors.dtype),
-            pltpu.VMEM((near, row_count, max(early, 1) * width), value_vectors.dtype),
-            pltpu.SemaphoreType.DMA((2 * near + 1,)),
+            pltpu.VMEM((near - 1, row_count, heads * width), key_vectors.dtype),
+            pltpu.VMEM((near - 1, row_count, max(early, 1) * width), value_vectors.dtype),
+            pltpu.SemaphoreType.DMA((2 * near - 1,)),
         ],
     )
-    own_rest = call(
-        functools.partial(own_rest_kernel, width, heads, early, orders[1]),
+    *own_rest, own_here = call(
+        functools.partial(own_rest_kernel, width, packs, early, orders[1]),
         "own_rest",
         unit,
-        [rest_shape] * near,
+        [rest_shape] * near + [first_shape],
         [VMEM] * 3,
         (ids, key_vectors, value_vectors),
     )
+    own_first = [own_here, *own_away]
     marked, marked_carries, states = [], [], []
     for piece, (own, shape) in enumerate(((own_first, first_shape), (own_rest, rest_shape))):
         masks, out_masks = orders[piece], orders[2 + piece]
@@ -375,18 +386,20 @@
             pltpu.SemaphoreType.DMA((max(count, 1),)),
         ],
     )
-    count = near * (heads - early)
-    return call(
-        functools.partial(readout_kernel, width, heads, early, orders[3]),
-        "readout",
-        2 * unit,
-        flat,
-        [VMEM] * (2 + near) + [HBM],
-        (solved, local, *states[1], out),
-        out_specs=HBM,
-        scratch_shapes=[pltpu.VMEM((count, row_count, width), jnp.float32), pltpu.SemaphoreType.DMA((count,))],
-        input_output_aliases={2 + near: 0},
-    )
+    for slots in (range(near // 2), range(near // 2, near)):
+        count = len(slots) * (heads - early)
+        out = call(
+            functools.partial(readout_kernel, width, heads, early, [orders[3][slot] for slot in slots]),
+            "readout",
+            2 * unit * len(slots) // near,
+            flat,
+            [VMEM] * (2 + len(slots)) + [HBM],
+            (solved, local, *[states[1][slot] for slot in slots], out),
+            out_specs=HBM,
+            scratch_shapes=[pltpu.VMEM((count, row_count, width), jnp.float32), pltpu.SemaphoreType.DMA((count,))],
+            input_output_aliases={2 + len(slots): 0},
+        )
+    return out
 
 
 def solution(mesh):

time: 56.4 us -> 55.4 us (0.982)
  waiting for transfers between devices: 23 us -> 20.8 us
  Pallas kernels: 11.2 us -> 12 us
  starting transfers between devices: 21.3 us -> 22 us
    ppermute x12, waiting for transfers between devices: 15.1 us -> 12.9 us  [exchange(): lax.ppermute(slot, 'near', [(i, i ^ mask) for i in range(near)])]
    pallas_call x8 -> x9, Pallas kernels: 11.2 us -> 12 us  [call(): pl.pallas_call(kernel, out_shape=out_shape, in_specs=in_specs, compiler_p...]
    ppermute x12, starting transfers between devices: 13.1 us -> 13.7 us  [exchange(): lax.ppermute(slot, 'near', [(i, i ^ mask) for i in range(near)])]
  transfers between devices with their start and end apart: 16 -> 16, of which waited for: 9 -> 8; matrix products, arithmetic and copies ran while one was open for 0% -> 0% of each run, Pallas kernels for 14% -> 16%
where the time goes in v7:
time: 55.4 us; the launch traced here: 55.1 us
  starting transfers between devices  22 us (40%)
  waiting for transfers between devices  20.8 us (38%)
  Pallas kernels  12 us (22%)
    ppermute x12, starting transfers between devices, exchange(): lax.ppermute(slot, 'near', [(i, i ^ mask) for i in range(near)])  13.7 us
    ppermute x12, waiting for transfers between devices, exchange(): lax.ppermute(slot, 'near', [(i, i ^ mask) for i in range(near)])  12.9 us
    pallas_call x9, Pallas kernels, call(): pl.pallas_call(kernel, out_shape=out_shape, in_specs=in_specs, compiler_p...  12 us
    ppermute x4, starting transfers between devices, onward(): lax.ppermute(value, ('outer', 'half'), [(i, (i + step) % blocks) for i in...  8.21 us
    ppermute x4, waiting for transfers between devices, onward(): lax.ppermute(value, ('outer', 'half'), [(i, (i + step) % blocks) for i in...  7.9 us
  transfers between devices with their start and end apart: 16, of which 8 were waited for; matrix products, arithmetic and copies ran while one was open for 0% of the time, Pallas kernels for 16%

profile of v7, /device:TPU:1, one launch (start us, length us, event | category | flops | bytes accessed | tf_op | source)
XLA Modules:
  0.0 55.1 jit_solution(14225557153255950215)
XLA Ops:
  0.0 0.0 copy-start.1
  0.0 0.0 copy-start.2
  0.0 1.9 %own_first.1 = (f32[392,128]{1,0:T(8,128)S(1)}, f32[392,128]{1,0:T(8,128)S(1)}, f32[392,128]{1,0:T(8,128)S(1)}) custom-call(s32[1,128]{1,0:T(1,128)} %bitcast.1, bf16[128,2048]{1,0:T(8,128)(2,1)} %k_ref.3, bf16[128,2048]{1,0:T(8,128)(2,1)} %v_ref.3), custom_call_target="tpu_custom_call" | custom-call | flops 536870912 | tf_op jit(solution)/shard_map/own_first/pallas_call | solution.py:284
  2.0 3.1 %collective-permute-start = (f32[392,128]{1,0:T(8,128)S(1)}, f32[392,128]{1,0:T(8,128)S(1)}, u32[]{:S(2)}, u32[]{:S(2)}) collective-permute-start(f32[392,128]{1,0:T(8,128)S(1)} %get-tuple-element.25), channel_id=1, source_target_pairs={{0,3},{1,2},{2,1},{3,0},{4,7},{5,6},{6,5},{7,4},{8,11},{9,10},{10,... | collective-permute-start | bytes 602120 | tf_op jit(solution)/shard_map/ppermute | solution.py:314
  5.1 0.0 copy-start.4
  5.1 0.2 collective-permute-start.1
  5.2 0.2 collective-permute-start.2
  5.4 0.0 copy-done.1
  5.4 0.0 copy-done.2
  5.5 0.3 copy-done.4
  5.7 0.9 %own_rest.1 = (f32[384,128]{1,0:T(8,128)S(1)}, f32[384,128]{1,0:T(8,128)S(1)}, f32[384,128]{1,0:T(8,128)S(1)}, f32[384,128]{1,0:T(8,128)S(1)}, f32[392,128]{1,0:T(8,128)S(1)}) custom-call(s32[1,128]{1,0:T(1,128)S(1)} %bitcast.2, bf16[128,2048]{1,0:T(8,128)(2,1)S(1)} %copy-done.1, bf16[128,2048]{1,0:T(8,128)(2,1)S(1)} %copy-done.2), custom_call_target="tpu_custom_call" | custom-call | flops 536870912 | tf_op jit(solution)/shard_map/own_rest/pallas_call | solution.py:284
  6.6 1.1 %collective-permute-start.8 = (f32[384,128]{1,0:T(8,128)S(1)}, f32[384,128]{1,0:T(8,128)S(1)}, u32[]{:S(2)}, u32[]{:S(2)}) collective-permute-start(f32[384,128]{1,0:T(8,128)S(1)} %get-tuple-element.35), channel_id=1, source_target_pairs={{0,1},{1,0},{2,3},{3,2},{4,5},{5,4},{6,7},{7,6},{8,9},{9,8},{10,11... | collective-permute-start | bytes 589832 | tf_op jit(solution)/shard_map/ppermute | solution.py:314
  7.7 1.3 %collective-permute-start.9 = (f32[384,128]{1,0:T(8,128)S(1)}, f32[384,128]{1,0:T(8,128)S(1)}, u32[]{:S(2)}, u32[]{:S(2)}) collective-permute-start(f32[384,128]{1,0:T(8,128)S(1)} %get-tuple-element.36), channel_id=1, source_target_pairs={{0,2},{1,3},{2,0},{3,1},{4,6},{5,7},{6,4},{7,5},{8,10},{9,11},{10,... | collective-permute-start | bytes 589832 | tf_op jit(solution)/shard_map/ppermute | solution.py:314
  9.0 0.8 %collective-permute-done.refs_1_.refs_3_ = f32[392,128]{1,0:T(8,128)S(1)} collective-permute-done((f32[392,128]{1,0:T(8,128)S(1)}, f32[392,128]{1,0:T(8,128)S(1)}, u32[]{:S(2)}, u32[]{:S(2)}) %collective-permute-start) | collective-permute-done | bytes 200736 | tf_op jit(solution)/shard_map/ppermute | solution.py:314
  9.8 2.0 %collective-permute-start.10 = (f32[384,128]{1,0:T(8,128)S(1)}, f32[384,128]{1,0:T(8,128)S(1)}, u32[]{:S(2)}, u32[]{:S(2)}) collective-permute-start(f32[384,128]{1,0:T(8,128)S(1)} %get-tuple-element.37), channel_id=1, source_target_pairs={{0,3},{1,2},{2,1},{3,0},{4,7},{5,6},{6,5},{7,4},{8,11},{9,10},{10,... | collective-permute-start | bytes 589832 | tf_op jit(solution)/shard_map/ppermute | solution.py:314
  11.9 2.1 %collective-permute-done.1.refs_2_ = f32[392,128]{1,0:T(8,128)S(1)} collective-permute-done((f32[392,128]{1,0:T(8,128)S(1)}, f32[392,128]{1,0:T(8,128)S(1)}, u32[]{:S(2)}, u32[]{:S(2)}) %collective-permute-start.1) | collective-permute-done | bytes 200736 | tf_op jit(solution)/shard_map/ppermute | solution.py:314
  14.0 0.8 %collective-permute-done.2.refs_3_.refs_1_ = f32[392,128]{1,0:T(8,128)S(1)} collective-permute-done((f32[392,128]{1,0:T(8,128)S(1)}, f32[392,128]{1,0:T(8,128)S(1)}, u32[]{:S(2)}, u32[]{:S(2)}) %collective-permute-start.2) | collective-permute-done | bytes 200736 | tf_op jit(solution)/shard_map/ppermute | solution.py:314
  14.8 0.1 block_total.2
  14.9 3.0 %collective-permute-start.4 = (f32[392,128]{1,0:T(8,128)S(1)}, f32[392,128]{1,0:T(8,128)S(1)}, u32[]{:S(2)}, u32[]{:S(2)}) collective-permute-start(f32[392,128]{1,0:T(8,128)S(1)} %block_total.2), channel_id=1, source_target_pairs={{0,8},{4,12},{8,16},{12,20},{16,24},{20,28},{24,0},{28,4},{1,9},{5... | collective-permute-start | bytes 602120 | tf_op jit(solution)/shard_map/ppermute | solution.py:320
  17.9 2.3 %collective-permute-start.3 = (f32[392,128]{1,0:T(8,128)S(1)}, f32[392,128]{1,0:T(8,128)S(1)}, u32[]{:S(2)}, u32[]{:S(2)}) collective-permute-start(f32[392,128]{1,0:T(8,128)S(1)} %block_total.2), channel_id=1, source_target_pairs={{0,4},{4,8},{8,12},{12,16},{16,20},{20,24},{24,28},{28,0},{1,5},{5... | collective-permute-start | bytes 602120 | tf_op jit(solution)/shard_map/ppermute | solution.py:320
  20.2 0.0 collective-permute-done.8.refs_5_.refs_7_
  20.2 0.0 collective-permute-done.9.refs_6_.refs_8_
  20.2 6.3 %collective-permute-done.10.refs_7_.refs_9_ = f32[384,128]{1,0:T(8,128)S(1)} collective-permute-done((f32[384,128]{1,0:T(8,128)S(1)}, f32[384,128]{1,0:T(8,128)S(1)}, u32[]{:S(2)}, u32[]{:S(2)}) %collective-permute-start.10) | collective-permute-done | bytes 196640 | tf_op jit(solution)/shard_map/ppermute | solution.py:314
  26.5 0.1 block_total.3
  26.6 2.8 %collective-permute-start.12 = (f32[384,128]{1,0:T(8,128)S(1)}, f32[384,128]{1,0:T(8,128)S(1)}, u32[]{:S(2)}, u32[]{:S(2)}) collective-permute-start(f32[384,128]{1,0:T(8,128)S(1)} %block_total.3), channel_id=1, source_target_pairs={{0,8},{4,12},{8,16},{12,20},{16,24},{20,28},{24,0},{28,4},{1,9},{5... | collective-permute-start | bytes 589832 | tf_op jit(solution)/shard_map/ppermute | solution.py:320
  29.4 0.0 collective-permute-start.11
  29.5 0.0 collective-permute-done.4.refs_5_
  29.5 0.4 collective-permute-done.3.refs_4_
  29.8 0.3 prefixes.2
  30.1 2.8 %collective-permute-start.5 = (f32[392,128]{1,0:T(8,128)S(1)}, f32[392,128]{1,0:T(8,128)S(1)}, u32[]{:S(2)}, u32[]{:S(2)}) collective-permute-start(f32[392,128]{1,0:T(8,128)S(1)} %get-tuple-element.29), channel_id=1, source_target_pairs={{0,3},{1,2},{2,1},{3,0},{4,7},{5,6},{6,5},{7,4},{8,11},{9,10},{10,... | collective-permute-start | bytes 602120 | tf_op jit(solution)/shard_map/ppermute | solution.py:314
  32.9 0.0 collective-permute-start.6
  32.9 0.0 copy-start
  32.9 0.4 collective-permute-start.7
  33.3 0.0 collective-permute-done.12.refs_11_
  33.3 7.5 %collective-permute-done.11.refs_10_ = f32[384,128]{1,0:T(8,128)S(1)} collective-permute-done((f32[384,128]{1,0:T(8,128)S(1)}, f32[384,128]{1,0:T(8,128)S(1)}, u32[]{:S(2)}, u32[]{:S(2)}) %collective-permute-start.11) | collective-permute-done | bytes 196640 | tf_op jit(solution)/shard_map/ppermute | solution.py:320
  40.8 0.3 prefixes.3
  41.1 0.1 collective-permute-start.13
  41.1 1.7 %collective-permute-start.14 = (f32[384,128]{1,0:T(8,128)S(1)}, f32[384,128]{1,0:T(8,128)S(1)}, u32[]{:S(2)}, u32[]{:S(2)}) collective-permute-start(f32[384,128]{1,0:T(8,128)S(1)} %get-tuple-element.39), channel_id=1, source_target_pairs={{0,3},{1,2},{2,1},{3,0},{4,7},{5,6},{6,5},{7,4},{8,11},{9,10},{10,... | collective-permute-start | bytes 589832 | tf_op jit(solution)/shard_map/ppermute | solution.py:314
  42.9 0.0 collective-permute-done.5.refs_1_
  42.9 0.0 copy-start.3
  42.9 0.9 %collective-permute-start.15 = (f32[384,128]{1,0:T(8,128)S(1)}, f32[384,128]{1,0:T(8,128)S(1)}, u32[]{:S(2)}, u32[]{:S(2)}) collective-permute-start(f32[384,128]{1,0:T(8,128)S(1)} %get-tuple-element.41), channel_id=1, source_target_pairs={{0,1},{1,0},{2,3},{3,2},{4,5},{5,4},{6,7},{7,6},{8,9},{9,8},{10,11... | collective-permute-start | bytes 589832 | tf_op jit(solution)/shard_map/ppermute | solution.py:314
  43.8 2.4 %collective-permute-done.6.refs_2_ = f32[392,128]{1,0:T(8,128)S(1)} collective-permute-done((f32[392,128]{1,0:T(8,128)S(1)}, f32[392,128]{1,0:T(8,128)S(1)}, u32[]{:S(2)}, u32[]{:S(2)}) %collective-permute-start.6) | collective-permute-done | bytes 200736 | tf_op jit(solution)/shard_map/ppermute | solution.py:314
  46.2 0.0 collective-permute-done.7.refs_3_
  46.2 0.0 copy-done
  46.2 0.0 copy-done.3
  46.2 6.4 %solve.1 = (f32[128,2048]{1,0:T(8,128)S(1)}, f32[128,2048]{1,0:T(8,128)S(1)}, f32[128,2048]{1,0:T(8,128)}) custom-call(f32[16]{0:T(128)S(1)} %copy-done.3, s32[1,128]{1,0:T(1,128)S(1)} %bitcast.3, bf16[128,2048]{1,0:T(8,128)(2,1)S(1)} %copy-done, bf16[128,2048]{1,0:T(8,128)(2,1)S(1)} %copy-done.1, bf16[128,2048]{1,0:T(8,128)(2,1)S(1)} %copy-done.2, ...), custom_call_target="tpu_custom_call" | custom-call | flops 6442450944 | tf_op jit(solution)/shard_map/solve/pallas_call | solution.py:284
  52.7 0.0 collective-permute-done.15.refs_1_
  52.7 1.0 %readout.2.refs_2_ = f32[128,2048]{1,0:T(8,128)} custom-call(f32[128,2048]{1,0:T(8,128)S(1)} %get-tuple-element.32.x_ref, f32[128,2048]{1,0:T(8,128)S(1)} %get-tuple-element.33.near_ref, f32[384,128]{1,0:T(8,128)S(1)} %get-tuple-element.40.refs_0_, f32[384,128]{1,0:T(8,128)S(1)} %collective-permute-done.15.refs_1_, ...), custom_call_target="tpu_custom_call", output_to_operand_aliasing={{}: (4, {})} | custom-call | flops 536870912 | tf_op jit(solution)/shard_map/readout/pallas_call | solution.py:284
  53.7 0.0 collective-permute-done.13.refs_0_
  53.7 0.4 collective-permute-done.14.refs_1_
  54.1 1.0 %readout.3 = f32[128,2048]{1,0:T(8,128)} custom-call(f32[128,2048]{1,0:T(8,128)S(1)} %get-tuple-element.32.x_ref, f32[128,2048]{1,0:T(8,128)S(1)} %get-tuple-element.33.near_ref, f32[384,128]{1,0:T(8,128)S(1)} %collective-permute-done.13.refs_0_, f32[384,128]{1,0:T(8,128)S(1)} %collective-permute-done.14.refs_1_, ...), custom_call_target="tpu_custom_call", output_to_operand_aliasing={{}: (4, {})} | custom-call | flops 536870912 | tf_op jit(solution)/shard_map/readout/pallas_call | solution.py:284
Async XLA Ops:
  0.0 5.4 %copy-start.1 = (bf16[128,2048]{1,0:T(8,128)(2,1)S(1)}, bf16[128,2048]{1,0:T(8,128)(2,1)}, u32[]{:S(2)}) copy-start(bf16[128,2048]{1,0:T(8,128)(2,1)} %k_ref.3) | copy-start | bytes 1572868
  0.0 5.4 %copy-start.2 = (bf16[128,2048]{1,0:T(8,128)(2,1)S(1)}, bf16[128,2048]{1,0:T(8,128)(2,1)}, u32[]{:S(2)}) copy-start(bf16[128,2048]{1,0:T(8,128)(2,1)} %v_ref.3) | copy-start | bytes 1572868
  2.0 7.9 %collective-permute-start = (f32[392,128]{1,0:T(8,128)S(1)}, f32[392,128]{1,0:T(8,128)S(1)}, u32[]{:S(2)}, u32[]{:S(2)}) collective-permute-start(f32[392,128]{1,0:T(8,128)S(1)} %get-tuple-element.25), channel_id=1, source_target_pairs={{0,3},{1,2},{2,1},{3,0},{4,7},{5,6},{6,5},{7,4},{8,11},{9,10},{10,... | collective-permute-start | bytes 602120 | tf_op jit(solution)/shard_map/ppermute | solution.py:314
  5.1 0.7 %copy-start.4 = (s32[128]{0:T(128)S(1)}, s32[128]{0:T(128)}, u32[]{:S(2)}) copy-start(s32[128]{0:T(128)} %param.8) | copy-start | bytes 1540
  5.1 8.9 %collective-permute-start.1 = (f32[392,128]{1,0:T(8,128)S(1)}, f32[392,128]{1,0:T(8,128)S(1)}, u32[]{:S(2)}, u32[]{:S(2)}) collective-permute-start(f32[392,128]{1,0:T(8,128)S(1)} %get-tuple-element.26), channel_id=1, source_target_pairs={{0,2},{1,3},{2,0},{3,1},{4,6},{5,7},{6,4},{7,5},{8,10},{9,11},{10,... | collective-permute-start | bytes 602120 | tf_op jit(solution)/shard_map/ppermute | solution.py:314
  5.2 9.6 %collective-permute-start.2 = (f32[392,128]{1,0:T(8,128)S(1)}, f32[392,128]{1,0:T(8,128)S(1)}, u32[]{:S(2)}, u32[]{:S(2)}) collective-permute-start(f32[392,128]{1,0:T(8,128)S(1)} %get-tuple-element.27), channel_id=1, source_target_pairs={{0,1},{1,0},{2,3},{3,2},{4,5},{5,4},{6,7},{7,6},{8,9},{9,8},{10,11... | collective-permute-start | bytes 602120 | tf_op jit(solution)/shard_map/ppermute | solution.py:314
  6.6 13.6 %collective-permute-start.8 = (f32[384,128]{1,0:T(8,128)S(1)}, f32[384,128]{1,0:T(8,128)S(1)}, u32[]{:S(2)}, u32[]{:S(2)}) collective-permute-start(f32[384,128]{1,0:T(8,128)S(1)} %get-tuple-element.35), channel_id=1, source_target_pairs={{0,1},{1,0},{2,3},{3,2},{4,5},{5,4},{6,7},{7,6},{8,9},{9,8},{10,11... | collective-permute-start | bytes 589832 | tf_op jit(solution)/shard_map/ppermute | solution.py:314
  7.7 12.6 %collective-permute-start.9 = (f32[384,128]{1,0:T(8,128)S(1)}, f32[384,128]{1,0:T(8,128)S(1)}, u32[]{:S(2)}, u32[]{:S(2)}) collective-permute-start(f32[384,128]{1,0:T(8,128)S(1)} %get-tuple-element.36), channel_id=1, source_target_pairs={{0,2},{1,3},{2,0},{3,1},{4,6},{5,7},{6,4},{7,5},{8,10},{9,11},{10,... | collective-permute-start | bytes 589832 | tf_op jit(solution)/shard_map/ppermute | solution.py:314
  9.8 16.7 %collective-permute-start.10 = (f32[384,128]{1,0:T(8,128)S(1)}, f32[384,128]{1,0:T(8,128)S(1)}, u32[]{:S(2)}, u32[]{:S(2)}) collective-permute-start(f32[384,128]{1,0:T(8,128)S(1)} %get-tuple-element.37), channel_id=1, source_target_pairs={{0,3},{1,2},{2,1},{3,0},{4,7},{5,6},{6,5},{7,4},{8,11},{9,10},{10,... | collective-permute-start | bytes 589832 | tf_op jit(solution)/shard_map/ppermute | solution.py:314
  14.9 14.6 %collective-permute-start.4 = (f32[392,128]{1,0:T(8,128)S(1)}, f32[392,128]{1,0:T(8,128)S(1)}, u32[]{:S(2)}, u32[]{:S(2)}) collective-permute-start(f32[392,128]{1,0:T(8,128)S(1)} %block_total.2), channel_id=1, source_target_pairs={{0,8},{4,12},{8,16},{12,20},{16,24},{20,28},{24,0},{28,4},{1,9},{5... | collective-permute-start | bytes 602120 | tf_op jit(solution)/shard_map/ppermute | solution.py:320
  17.9 11.9 %collective-permute-start.3 = (f32[392,128]{1,0:T(8,128)S(1)}, f32[392,128]{1,0:T(8,128)S(1)}, u32[]{:S(2)}, u32[]{:S(2)}) collective-permute-start(f32[392,128]{1,0:T(8,128)S(1)} %block_total.2), channel_id=1, source_target_pairs={{0,4},{4,8},{8,12},{12,16},{16,20},{20,24},{24,28},{28,0},{1,5},{5... | collective-permute-start | bytes 602120 | tf_op jit(solution)/shard_map/ppermute | solution.py:320
  26.6 6.7 %collective-permute-start.12 = (f32[384,128]{1,0:T(8,128)S(1)}, f32[384,128]{1,0:T(8,128)S(1)}, u32[]{:S(2)}, u32[]{:S(2)}) collective-permute-start(f32[384,128]{1,0:T(8,128)S(1)} %block_total.3), channel_id=1, source_target_pairs={{0,8},{4,12},{8,16},{12,20},{16,24},{20,28},{24,0},{28,4},{1,9},{5... | collective-permute-start | bytes 589832 | tf_op jit(solution)/shard_map/ppermute | solution.py:320
  29.4 11.4 %collective-permute-start.11 = (f32[384,128]{1,0:T(8,128)S(1)}, f32[384,128]{1,0:T(8,128)S(1)}, u32[]{:S(2)}, u32[]{:S(2)}) collective-permute-start(f32[384,128]{1,0:T(8,128)S(1)} %block_total.3), channel_id=1, source_target_pairs={{0,4},{4,8},{8,12},{12,16},{16,20},{20,24},{24,28},{28,0},{1,5},{5... | collective-permute-start | bytes 589832 | tf_op jit(solution)/shard_map/ppermute | solution.py:320
  30.1 12.8 %collective-permute-start.5 = (f32[392,128]{1,0:T(8,128)S(1)}, f32[392,128]{1,0:T(8,128)S(1)}, u32[]{:S(2)}, u32[]{:S(2)}) collective-permute-start(f32[392,128]{1,0:T(8,128)S(1)} %get-tuple-element.29), channel_id=1, source_target_pairs={{0,3},{1,2},{2,1},{3,0},{4,7},{5,6},{6,5},{7,4},{8,11},{9,10},{10,... | collective-permute-start | bytes 602120 | tf_op jit(solution)/shard_map/ppermute | solution.py:314
  32.9 13.3 %collective-permute-start.6 = (f32[392,128]{1,0:T(8,128)S(1)}, f32[392,128]{1,0:T(8,128)S(1)}, u32[]{:S(2)}, u32[]{:S(2)}) collective-permute-start(f32[392,128]{1,0:T(8,128)S(1)} %get-tuple-element.30), channel_id=1, source_target_pairs={{0,2},{1,3},{2,0},{3,1},{4,6},{5,7},{6,4},{7,5},{8,10},{9,11},{10,... | collective-permute-start | bytes 602120 | tf_op jit(solution)/shard_map/ppermute | solution.py:314
  32.9 13.3 %copy-start = (bf16[128,2048]{1,0:T(8,128)(2,1)S(1)}, bf16[128,2048]{1,0:T(8,128)(2,1)}, u32[]{:S(2)}) copy-start(bf16[128,2048]{1,0:T(8,128)(2,1)} %q_ref.1) | copy-start | bytes 1572868
  32.9 13.3 %collective-permute-start.7 = (f32[392,128]{1,0:T(8,128)S(1)}, f32[392,128]{1,0:T(8,128)S(1)}, u32[]{:S(2)}, u32[]{:S(2)}) collective-permute-start(f32[392,128]{1,0:T(8,128)S(1)} %get-tuple-element.31), channel_id=1, source_target_pairs={{0,1},{1,0},{2,3},{3,2},{4,5},{5,4},{6,7},{7,6},{8,9},{9,8},{10,11... | collective-permute-start | bytes 602120 | tf_op jit(solution)/shard_map/ppermute | solution.py:314
  41.1 12.6 %collective-permute-start.13 = (f32[384,128]{1,0:T(8,128)S(1)}, f32[384,128]{1,0:T(8,128)S(1)}, u32[]{:S(2)}, u32[]{:S(2)}) collective-permute-start(f32[384,128]{1,0:T(8,128)S(1)} %get-tuple-element.38), channel_id=1, source_target_pairs={{0,2},{1,3},{2,0},{3,1},{4,6},{5,7},{6,4},{7,5},{8,10},{9,11},{10,... | collective-permute-start | bytes 589832 | tf_op jit(solution)/shard_map/ppermute | solution.py:314
  41.1 12.9 %collective-permute-start.14 = (f32[384,128]{1,0:T(8,128)S(1)}, f32[384,128]{1,0:T(8,128)S(1)}, u32[]{:S(2)}, u32[]{:S(2)}) collective-permute-start(f32[384,128]{1,0:T(8,128)S(1)} %get-tuple-element.39), channel_id=1, source_target_pairs={{0,3},{1,2},{2,1},{3,0},{4,7},{5,6},{6,5},{7,4},{8,11},{9,10},{10,... | collective-permute-start | bytes 589832 | tf_op jit(solution)/shard_map/ppermute | solution.py:314
  42.9 3.3 %copy-start.3 = (f32[16]{0:T(128)S(1)}, f32[16]{0:T(128)}, u32[]{:S(2)}) copy-start(f32[16]{0:T(128)} %ridge_ref.1) | copy-start | bytes 196
  42.9 9.8 %collective-permute-start.15 = (f32[384,128]{1,0:T(8,128)S(1)}, f32[384,128]{1,0:T(8,128)S(1)}, u32[]{:S(2)}, u32[]{:S(2)}) collective-permute-start(f32[384,128]{1,0:T(8,128)S(1)} %get-tuple-element.41), channel_id=1, source_target_pairs={{0,1},{1,0},{2,3},{3,2},{4,5},{5,4},{6,7},{7,6},{8,9},{9,8},{10,11... | collective-permute-start | bytes 589832 | tf_op jit(solution)/shard_map/ppermute | solution.py:314

commit v8 on v7

--- a/solution.py
+++ b/solution.py
@@ -104,7 +104,7 @@
         first_slot(width, packs, early, out, keys_of, values_of, last)
 
 
-def own_rest_kernel(width, packs, early, masks, ids_ref, k_ref, v_ref, *outs):
+def own_rest_kernel(width, packs, early, later, masks, ids_ref, k_ref, v_ref, *outs):
     last = last_of(ids_ref, width)
 
     def lanes_of(mask, head):
@@ -120,8 +120,9 @@
             out[pl.ds((head - early) * width, width), :] = dot_rows(
                 jnp.concatenate([keys, keys], 0), jnp.concatenate([high, low], 0)
             )
-    keys_of, values_of = (lambda head, ref=ref: ref[:, lanes_of(0, head)] for ref in (k_ref, v_ref))
-    first_slot(width, packs, early, outs[-1], keys_of, values_of, last)
+    for mask, out in zip(later, outs[len(masks) :]):
+        keys_of, values_of = (lambda head, r=ref, m=mask: r[:, lanes_of(m, head)] for ref in (k_ref, v_ref))
+        first_slot(width, packs, early, out, keys_of, values_of, last)
 
 
 def marks_of(refs, at):
@@ -173,6 +174,7 @@
     column = down(ids)
     rows = ids.shape[1]
     carried = jnp.broadcast_to(flag(column == jnp.min(ids, 1, keepdims=True)), (rows, width))
+    carried_pair = jnp.concatenate([carried, carried], 1).astype(jnp.bfloat16)
     row_at = lax.broadcasted_iota(jnp.int32, (rows, rows), 0)
     col_at = lax.broadcasted_iota(jnp.int32, (rows, rows), 1)
     within = jnp.where(row_at >= col_at, flag(column == ids), 0.0)
@@ -202,6 +204,7 @@
                 group.append(
                     dict(
                         lanes=lanes,
+                        twin=pl.ds(pl.multiple_of(head * 2 * width, 2 * width), 2 * width),
                         cross=state.at[pl.ds((packs + 2 * pack + side) * width + extra_of(packs), width)]
                         if 2 * pack + side < early
                         else None,
@@ -239,7 +242,7 @@
             pair = jnp.concatenate([high, low], 1)
             h["score"] = split(dot(pair, h["turned"]) * h["once"])
             if h["cross"] is None:
-                x_ref[:, h["lanes"]] = h["solved"] * carried
+                x_ref[:, h["twin"]] = pair * carried_pair
             else:
                 h["far"] = far_part(pair, high, h["cross"][...]) * carried
         for h in group:
@@ -263,8 +266,8 @@
         for head in range(early, heads):
             at = (lax.axis_index("near") ^ masks[slot]) * heads + head
             lanes = pl.ds(pl.multiple_of(at * width, width), width)
-            high, low = split(x_ref[:, lanes])
-            far = far_part(jnp.concatenate([high, low], 1), high, state[pl.ds((head - early) * width, width), :])
+            pair = x_ref[:, pl.ds(pl.multiple_of(at * 2 * width, 2 * width), 2 * width)]
+            far = far_part(pair, pair[:, :width], state[pl.ds((head - early) * width, width), :])
             number = len(copies)
             out[number] = near_ref[:, lanes] + far
             copies.append(pltpu.make_async_copy(out.at[number], out_hbm.at[:, lanes], sems.at[number]))
@@ -324,29 +327,31 @@
     rising = list(range(near))
     falling = rising[:1] + rising[:0:-1]
     orders = falling, rising, falling, rising
-    own_away = call(
-        functools.partial(own_first_kernel, width, packs, early, orders[0][1:]),
+    soon, later = orders[0][1 : 1 + near // 2], orders[0][1 + near // 2 :] + [0]
+    own_soon = call(
+        functools.partial(own_first_kernel, width, packs, early, soon),
         "own_first",
         unit,
-        [first_shape] * (near - 1),
+        [first_shape] * len(soon),
         [HBM] * 3,
         [pltpu.with_memory_space_constraint(one, pltpu.HBM) for one in (ids, key_vectors, value_vectors)],
         scratch_shapes=[
             pltpu.VMEM(ids.shape, ids.dtype),
-            pltpu.VMEM((near - 1, row_count, heads * width), key_vectors.dtype),
-            pltpu.VMEM((near - 1, row_count, max(early, 1) * width), value_vectors.dtype),
-            pltpu.SemaphoreType.DMA((2 * near - 1,)),
+            pltpu.VMEM((len(soon), row_count, heads * width), key_vectors.dtype),
+            pltpu.VMEM((len(soon), row_count, max(early, 1) * width), value_vectors.dtype),
+            pltpu.SemaphoreType.DMA((2 * len(soon) + 1,)),
         ],
     )
-    *own_rest, own_here = call(
-        functools.partial(own_rest_kernel, width, packs, early, orders[1]),
+    own_more = call(
+        functools.partial(own_rest_kernel, width, packs, early, later, orders[1]),
         "own_rest",
         unit,
-        [rest_shape] * near + [first_shape],
+        [rest_shape] * near + [first_shape] * len(later),
         [VMEM] * 3,
         (ids, key_vectors, value_vectors),
     )
-    own_first = [own_here, *own_away]
+    own_rest, own_later = own_more[:near], own_more[near:]
+    own_first = [own_later[-1], *own_soon, *own_later[:-1]]
     marked, marked_carries, states = [], [], []
     for piece, (own, shape) in enumerate(((own_first, first_shape), (own_rest, rest_shape))):
         masks, out_masks = orders[piece], orders[2 + piece]
@@ -377,7 +382,7 @@
         functools.partial(solve_kernel, width, packs, early, max(1, 8 // heads), orders[2]),
         "solve",
         12 * unit,
-        [flat] * 3,
+        [jax.ShapeDtypeStruct((row_count, 2 * columns), jnp.bfloat16), flat, flat],
         [SMEM] + [VMEM] * (4 + near),
         (ridge_weight, ids, queries, key_vectors, value_vectors, *states[0]),
         out_specs=[VMEM, VMEM, HBM],

time: 55.4 us -> 55.2 us (level)
  starting transfers between devices: 22 us -> 22.7 us
  waiting for transfers between devices: 20.8 us -> 20.2 us
    ppermute x12, waiting for transfers between devices: 12.9 us -> 12.3 us  [exchange(): lax.ppermute(slot, 'near', [(i, i ^ mask) for i in range(near)])]
  transfers between devices with their start and end apart: 16 -> 16, of which waited for: 8 -> 8; matrix products, arithmetic and copies ran while one was open for 0% -> 0% of each run, Pallas kernels for 16% -> 17%
where the time goes in v8:
time: 55.2 us; the launch traced here: 54.9 us
  starting transfers between devices  22.7 us (41%)
  waiting for transfers between devices  20.2 us (37%)
  Pallas kernels  11.9 us (22%)
    ppermute x12, starting transfers between devices, exchange(): lax.ppermute(slot, 'near', [(i, i ^ mask) for i in range(near)])  14.1 us
    ppermute x12, waiting for transfers between devices, exchange(): lax.ppermute(slot, 'near', [(i, i ^ mask) for i in range(near)])  12.3 us
    pallas_call x9, Pallas kernels, call(): pl.pallas_call(kernel, out_shape=out_shape, in_specs=in_specs, compiler_p...  11.9 us
    ppermute x4, starting transfers between devices, onward(): lax.ppermute(value, ('outer', 'half'), [(i, (i + step) % blocks) for i in...  8.61 us
    ppermute x4, waiting for transfers between devices, onward(): lax.ppermute(value, ('outer', 'half'), [(i, (i + step) % blocks) for i in...  7.9 us
  transfers between devices with their start and end apart: 16, of which 8 were waited for; matrix products, arithmetic and copies ran while one was open for 0% of the time, Pallas kernels for 17%

profile of v8, /device:TPU:1, one launch (start us, length us, event | category | flops | bytes accessed | tf_op | source)
XLA Modules:
  0.0 54.9 jit_solution(283878941516529857)
XLA Ops:
  0.0 0.0 copy-start.1
  0.0 0.0 copy-start.2
  0.0 1.8 %own_first.1 = (f32[392,128]{1,0:T(8,128)S(1)}, f32[392,128]{1,0:T(8,128)S(1)}) custom-call(s32[1,128]{1,0:T(1,128)} %bitcast.1, bf16[128,2048]{1,0:T(8,128)(2,1)} %k_ref.3, bf16[128,2048]{1,0:T(8,128)(2,1)} %v_ref.3), custom_call_target="tpu_custom_call" | custom-call | flops 536870912 | tf_op jit(solution)/shard_map/own_first/pallas_call | solution.py:287
  1.8 0.0 copy-start.4
  1.8 3.1 %collective-permute-start = (f32[392,128]{1,0:T(8,128)S(1)}, f32[392,128]{1,0:T(8,128)S(1)}, u32[]{:S(2)}, u32[]{:S(2)}) collective-permute-start(f32[392,128]{1,0:T(8,128)S(1)} %get-tuple-element.25), channel_id=1, source_target_pairs={{0,3},{1,2},{2,1},{3,0},{4,7},{5,6},{6,5},{7,4},{8,11},{9,10},{10,... | collective-permute-start | bytes 602120 | tf_op jit(solution)/shard_map/ppermute | solution.py:317
  4.9 0.2 collective-permute-start.1
  5.1 0.0 copy-done.1
  5.1 0.0 copy-done.2
  5.1 0.0 copy-done.4
  5.1 1.0 %own_rest.1 = (f32[384,128]{1,0:T(8,128)S(1)}, f32[384,128]{1,0:T(8,128)S(1)}, f32[384,128]{1,0:T(8,128)S(1)}, f32[384,128]{1,0:T(8,128)S(1)}, f32[392,128]{1,0:T(8,128)S(1)}, /*index=5*/f32[392,128]{1,0:T(8,128)S(1)}) custom-call(s32[1,128]{1,0:T(1,128)S(1)} %bitcast.2, bf16[128,2048]{1,0:T(8,128)(2,1)S(1)} %copy-done.1, bf16[128,2048]{1,0:T(8,128)(2,1)S(1)} %copy-done.2), custom_call_target="tpu_custom_call" | custom-call | flops 536870912 | tf_op jit(solution)/shard_map/own_rest/pallas_call | solution.py:287
  6.1 0.3 collective-permute-start.2
  6.4 1.3 %collective-permute-start.8 = (f32[384,128]{1,0:T(8,128)S(1)}, f32[384,128]{1,0:T(8,128)S(1)}, u32[]{:S(2)}, u32[]{:S(2)}) collective-permute-start(f32[384,128]{1,0:T(8,128)S(1)} %get-tuple-element.35), channel_id=1, source_target_pairs={{0,1},{1,0},{2,3},{3,2},{4,5},{5,4},{6,7},{7,6},{8,9},{9,8},{10,11... | collective-permute-start | bytes 589832 | tf_op jit(solution)/shard_map/ppermute | solution.py:317
  7.6 1.3 %collective-permute-start.9 = (f32[384,128]{1,0:T(8,128)S(1)}, f32[384,128]{1,0:T(8,128)S(1)}, u32[]{:S(2)}, u32[]{:S(2)}) collective-permute-start(f32[384,128]{1,0:T(8,128)S(1)} %get-tuple-element.36), channel_id=1, source_target_pairs={{0,2},{1,3},{2,0},{3,1},{4,6},{5,7},{6,4},{7,5},{8,10},{9,11},{10,... | collective-permute-start | bytes 589832 | tf_op jit(solution)/shard_map/ppermute | solution.py:317
  8.9 0.7 %collective-permute-done.refs_1_.refs_3_ = f32[392,128]{1,0:T(8,128)S(1)} collective-permute-done((f32[392,128]{1,0:T(8,128)S(1)}, f32[392,128]{1,0:T(8,128)S(1)}, u32[]{:S(2)}, u32[]{:S(2)}) %collective-permute-start) | collective-permute-done | bytes 200736 | tf_op jit(solution)/shard_map/ppermute | solution.py:317
  9.6 2.0 %collective-permute-start.10 = (f32[384,128]{1,0:T(8,128)S(1)}, f32[384,128]{1,0:T(8,128)S(1)}, u32[]{:S(2)}, u32[]{:S(2)}) collective-permute-start(f32[384,128]{1,0:T(8,128)S(1)} %get-tuple-element.37), channel_id=1, source_target_pairs={{0,3},{1,2},{2,1},{3,0},{4,7},{5,6},{6,5},{7,4},{8,11},{9,10},{10,... | collective-permute-start | bytes 589832 | tf_op jit(solution)/shard_map/ppermute | solution.py:317
  11.7 2.1 %collective-permute-done.1.refs_2_ = f32[392,128]{1,0:T(8,128)S(1)} collective-permute-done((f32[392,128]{1,0:T(8,128)S(1)}, f32[392,128]{1,0:T(8,128)S(1)}, u32[]{:S(2)}, u32[]{:S(2)}) %collective-permute-start.1) | collective-permute-done | bytes 200736 | tf_op jit(solution)/shard_map/ppermute | solution.py:317
  13.8 0.4 collective-permute-done.2.refs_3_.refs_1_
  14.2 0.1 block_total.2
  14.3 3.4 %collective-permute-start.4 = (f32[392,128]{1,0:T(8,128)S(1)}, f32[392,128]{1,0:T(8,128)S(1)}, u32[]{:S(2)}, u32[]{:S(2)}) collective-permute-start(f32[392,128]{1,0:T(8,128)S(1)} %block_total.2), channel_id=1, source_target_pairs={{0,8},{4,12},{8,16},{12,20},{16,24},{20,28},{24,0},{28,4},{1,9},{5... | collective-permute-start | bytes 602120 | tf_op jit(solution)/shard_map/ppermute | solution.py:323
  17.7 2.3 %collective-permute-start.3 = (f32[392,128]{1,0:T(8,128)S(1)}, f32[392,128]{1,0:T(8,128)S(1)}, u32[]{:S(2)}, u32[]{:S(2)}) collective-permute-start(f32[392,128]{1,0:T(8,128)S(1)} %block_total.2), channel_id=1, source_target_pairs={{0,4},{4,8},{8,12},{12,16},{16,20},{20,24},{24,28},{28,0},{1,5},{5... | collective-permute-start | bytes 602120 | tf_op jit(solution)/shard_map/ppermute | solution.py:323
  20.0 0.0 collective-permute-done.8.refs_5_.refs_7_
  20.0 0.0 collective-permute-done.9.refs_6_.refs_8_
  20.0 6.3 %collective-permute-done.10.refs_7_.refs_9_ = f32[384,128]{1,0:T(8,128)S(1)} collective-permute-done((f32[384,128]{1,0:T(8,128)S(1)}, f32[384,128]{1,0:T(8,128)S(1)}, u32[]{:S(2)}, u32[]{:S(2)}) %collective-permute-start.10) | collective-permute-done | bytes 196640 | tf_op jit(solution)/shard_map/ppermute | solution.py:317
  26.3 0.1 block_total.3
  26.4 2.9 %collective-permute-start.12 = (f32[384,128]{1,0:T(8,128)S(1)}, f32[384,128]{1,0:T(8,128)S(1)}, u32[]{:S(2)}, u32[]{:S(2)}) collective-permute-start(f32[384,128]{1,0:T(8,128)S(1)} %block_total.3), channel_id=1, source_target_pairs={{0,8},{4,12},{8,16},{12,20},{16,24},{20,28},{24,0},{28,4},{1,9},{5... | collective-permute-start | bytes 589832 | tf_op jit(solution)/shard_map/ppermute | solution.py:323
  29.3 0.0 collective-permute-start.11
  29.3 0.0 collective-permute-done.4.refs_5_
  29.3 0.3 collective-permute-done.3.refs_4_
  29.6 0.3 prefixes.2
  29.9 2.8 %collective-permute-start.5 = (f32[392,128]{1,0:T(8,128)S(1)}, f32[392,128]{1,0:T(8,128)S(1)}, u32[]{:S(2)}, u32[]{:S(2)}) collective-permute-start(f32[392,128]{1,0:T(8,128)S(1)} %get-tuple-element.29), channel_id=1, source_target_pairs={{0,3},{1,2},{2,1},{3,0},{4,7},{5,6},{6,5},{7,4},{8,11},{9,10},{10,... | collective-permute-start | bytes 602120 | tf_op jit(solution)/shard_map/ppermute | solution.py:317
  32.7 0.0 collective-permute-start.6
  32.7 0.0 copy-start
  32.7 0.4 collective-permute-start.7
  33.1 0.0 collective-permute-done.12.refs_11_
  33.1 7.6 %collective-permute-done.11.refs_10_ = f32[384,128]{1,0:T(8,128)S(1)} collective-permute-done((f32[384,128]{1,0:T(8,128)S(1)}, f32[384,128]{1,0:T(8,128)S(1)}, u32[]{:S(2)}, u32[]{:S(2)}) %collective-permute-start.11) | collective-permute-done | bytes 196640 | tf_op jit(solution)/shard_map/ppermute | solution.py:323
  40.6 0.2 prefixes.3
  40.9 0.1 collective-permute-start.13
  41.0 1.7 %collective-permute-start.14 = (f32[384,128]{1,0:T(8,128)S(1)}, f32[384,128]{1,0:T(8,128)S(1)}, u32[]{:S(2)}, u32[]{:S(2)}) collective-permute-start(f32[384,128]{1,0:T(8,128)S(1)} %get-tuple-element.39), channel_id=1, source_target_pairs={{0,3},{1,2},{2,1},{3,0},{4,7},{5,6},{6,5},{7,4},{8,11},{9,10},{10,... | collective-permute-start | bytes 589832 | tf_op jit(solution)/shard_map/ppermute | solution.py:317
  42.7 0.0 collective-permute-done.5.refs_1_
  42.7 0.0 copy-start.3
  42.7 0.9 %collective-permute-start.15 = (f32[384,128]{1,0:T(8,128)S(1)}, f32[384,128]{1,0:T(8,128)S(1)}, u32[]{:S(2)}, u32[]{:S(2)}) collective-permute-start(f32[384,128]{1,0:T(8,128)S(1)} %get-tuple-element.41), channel_id=1, source_target_pairs={{0,1},{1,0},{2,3},{3,2},{4,5},{5,4},{6,7},{7,6},{8,9},{9,8},{10,11... | collective-permute-start | bytes 589832 | tf_op jit(solution)/shard_map/ppermute | solution.py:317
  43.6 2.4 %collective-permute-done.6.refs_2_ = f32[392,128]{1,0:T(8,128)S(1)} collective-permute-done((f32[392,128]{1,0:T(8,128)S(1)}, f32[392,128]{1,0:T(8,128)S(1)}, u32[]{:S(2)}, u32[]{:S(2)}) %collective-permute-start.6) | collective-permute-done | bytes 200736 | tf_op jit(solution)/shard_map/ppermute | solution.py:317
  46.0 0.0 collective-permute-done.7.refs_3_
  46.0 0.0 copy-done
  46.0 0.0 copy-done.3
  46.0 6.5 %solve.1 = (bf16[128,4096]{1,0:T(8,128)(2,1)S(1)}, f32[128,2048]{1,0:T(8,128)S(1)}, f32[128,2048]{1,0:T(8,128)}) custom-call(f32[16]{0:T(128)S(1)} %copy-done.3, s32[1,128]{1,0:T(1,128)S(1)} %bitcast.3, bf16[128,2048]{1,0:T(8,128)(2,1)S(1)} %copy-done, bf16[128,2048]{1,0:T(8,128)(2,1)S(1)} %copy-done.1, bf16[128,2048]{1,0:T(8,128)(2,1)S(1)} %copy-done.2, ...), custom_call_target="tpu_custom_call" | custom-call | flops 6442450944 | tf_op jit(solution)/shard_map/solve/pallas_call | solution.py:287
  52.5 0.0 collective-permute-done.15.refs_1_
  52.5 1.0 %readout.2.refs_2_ = f32[128,2048]{1,0:T(8,128)} custom-call(bf16[128,4096]{1,0:T(8,128)(2,1)S(1)} %get-tuple-element.32.x_ref, f32[128,2048]{1,0:T(8,128)S(1)} %get-tuple-element.33.near_ref, f32[384,128]{1,0:T(8,128)S(1)} %get-tuple-element.40.refs_0_, f32[384,128]{1,0:T(8,128)S(1)} %collective-permute-done.15.refs_1_, ...), custom_call_target="tpu_custom_call", output_to_operand_aliasing={{}: (4, {})} | custom-call | flops 536870912 | tf_op jit(solution)/shard_map/readout/pallas_call | solution.py:287
  53.6 0.0 collective-permute-done.13.refs_0_
  53.6 0.3 collective-permute-done.14.refs_1_
  53.9 1.0 %readout.3 = f32[128,2048]{1,0:T(8,128)} custom-call(bf16[128,4096]{1,0:T(8,128)(2,1)S(1)} %get-tuple-element.32.x_ref, f32[128,2048]{1,0:T(8,128)S(1)} %get-tuple-element.33.near_ref, f32[384,128]{1,0:T(8,128)S(1)} %collective-permute-done.13.refs_0_, f32[384,128]{1,0:T(8,128)S(1)} %collective-permute-done.14.refs_1_, ...), custom_call_target="tpu_custom_call", output_to_operand_aliasing={{}: (4, {})} | custom-call | flops 536870912 | tf_op jit(solution)/shard_map/readout/pallas_call | solution.py:287
Async XLA Ops:
  0.0 5.1 %copy-start.1 = (bf16[128,2048]{1,0:T(8,128)(2,1)S(1)}, bf16[128,2048]{1,0:T(8,128)(2,1)}, u32[]{:S(2)}) copy-start(bf16[128,2048]{1,0:T(8,128)(2,1)} %k_ref.3) | copy-start | bytes 1572868
  0.0 5.1 %copy-start.2 = (bf16[128,2048]{1,0:T(8,128)(2,1)S(1)}, bf16[128,2048]{1,0:T(8,128)(2,1)}, u32[]{:S(2)}) copy-start(bf16[128,2048]{1,0:T(8,128)(2,1)} %v_ref.3) | copy-start | bytes 1572868
  1.8 3.3 %copy-start.4 = (s32[128]{0:T(128)S(1)}, s32[128]{0:T(128)}, u32[]{:S(2)}) copy-start(s32[128]{0:T(128)} %param.8) | copy-start | bytes 1540
  1.8 7.8 %collective-permute-start = (f32[392,128]{1,0:T(8,128)S(1)}, f32[392,128]{1,0:T(8,128)S(1)}, u32[]{:S(2)}, u32[]{:S(2)}) collective-permute-start(f32[392,128]{1,0:T(8,128)S(1)} %get-tuple-element.25), channel_id=1, source_target_pairs={{0,3},{1,2},{2,1},{3,0},{4,7},{5,6},{6,5},{7,4},{8,11},{9,10},{10,... | collective-permute-start | bytes 602120 | tf_op jit(solution)/shard_map/ppermute | solution.py:317
  4.9 8.9 %collective-permute-start.1 = (f32[392,128]{1,0:T(8,128)S(1)}, f32[392,128]{1,0:T(8,128)S(1)}, u32[]{:S(2)}, u32[]{:S(2)}) collective-permute-start(f32[392,128]{1,0:T(8,128)S(1)} %get-tuple-element.26), channel_id=1, source_target_pairs={{0,2},{1,3},{2,0},{3,1},{4,6},{5,7},{6,4},{7,5},{8,10},{9,11},{10,... | collective-permute-start | bytes 602120 | tf_op jit(solution)/shard_map/ppermute | solution.py:317
  6.1 8.1 %collective-permute-start.2 = (f32[392,128]{1,0:T(8,128)S(1)}, f32[392,128]{1,0:T(8,128)S(1)}, u32[]{:S(2)}, u32[]{:S(2)}) collective-permute-start(f32[392,128]{1,0:T(8,128)S(1)} %get-tuple-element.27), channel_id=1, source_target_pairs={{0,1},{1,0},{2,3},{3,2},{4,5},{5,4},{6,7},{7,6},{8,9},{9,8},{10,11... | collective-permute-start | bytes 602120 | tf_op jit(solution)/shard_map/ppermute | solution.py:317
  6.4 13.7 %collective-permute-start.8 = (f32[384,128]{1,0:T(8,128)S(1)}, f32[384,128]{1,0:T(8,128)S(1)}, u32[]{:S(2)}, u32[]{:S(2)}) collective-permute-start(f32[384,128]{1,0:T(8,128)S(1)} %get-tuple-element.35), channel_id=1, source_target_pairs={{0,1},{1,0},{2,3},{3,2},{4,5},{5,4},{6,7},{7,6},{8,9},{9,8},{10,11... | collective-permute-start | bytes 589832 | tf_op jit(solution)/shard_map/ppermute | solution.py:317
  7.6 12.4 %collective-permute-start.9 = (f32[384,128]{1,0:T(8,128)S(1)}, f32[384,128]{1,0:T(8,128)S(1)}, u32[]{:S(2)}, u32[]{:S(2)}) collective-permute-start(f32[384,128]{1,0:T(8,128)S(1)} %get-tuple-element.36), channel_id=1, source_target_pairs={{0,2},{1,3},{2,0},{3,1},{4,6},{5,7},{6,4},{7,5},{8,10},{9,11},{10,... | collective-permute-start | bytes 589832 | tf_op jit(solution)/shard_map/ppermute | solution.py:317
  9.6 16.7 %collective-permute-start.10 = (f32[384,128]{1,0:T(8,128)S(1)}, f32[384,128]{1,0:T(8,128)S(1)}, u32[]{:S(2)}, u32[]{:S(2)}) collective-permute-start(f32[384,128]{1,0:T(8,128)S(1)} %get-tuple-element.37), channel_id=1, source_target_pairs={{0,3},{1,2},{2,1},{3,0},{4,7},{5,6},{6,5},{7,4},{8,11},{9,10},{10,... | collective-permute-start | bytes 589832 | tf_op jit(solution)/shard_map/ppermute | solution.py:317
  14.3 15.0 %collective-permute-start.4 = (f32[392,128]{1,0:T(8,128)S(1)}, f32[392,128]{1,0:T(8,128)S(1)}, u32[]{:S(2)}, u32[]{:S(2)}) collective-permute-start(f32[392,128]{1,0:T(8,128)S(1)} %block_total.2), channel_id=1, source_target_pairs={{0,8},{4,12},{8,16},{12,20},{16,24},{20,28},{24,0},{28,4},{1,9},{5... | collective-permute-start | bytes 602120 | tf_op jit(solution)/shard_map/ppermute | solution.py:323
  17.7 11.9 %collective-permute-start.3 = (f32[392,128]{1,0:T(8,128)S(1)}, f32[392,128]{1,0:T(8,128)S(1)}, u32[]{:S(2)}, u32[]{:S(2)}) collective-permute-start(f32[392,128]{1,0:T(8,128)S(1)} %block_total.2), channel_id=1, source_target_pairs={{0,4},{4,8},{8,12},{12,16},{16,20},{20,24},{24,28},{28,0},{1,5},{5... | collective-permute-start | bytes 602120 | tf_op jit(solution)/shard_map/ppermute | solution.py:323
  26.4 6.7 %collective-permute-start.12 = (f32[384,128]{1,0:T(8,128)S(1)}, f32[384,128]{1,0:T(8,128)S(1)}, u32[]{:S(2)}, u32[]{:S(2)}) collective-permute-start(f32[384,128]{1,0:T(8,128)S(1)} %block_total.3), channel_id=1, source_target_pairs={{0,8},{4,12},{8,16},{12,20},{16,24},{20,28},{24,0},{28,4},{1,9},{5... | collective-permute-start | bytes 589832 | tf_op jit(solution)/shard_map/ppermute | solution.py:323
  29.3 11.4 %collective-permute-start.11 = (f32[384,128]{1,0:T(8,128)S(1)}, f32[384,128]{1,0:T(8,128)S(1)}, u32[]{:S(2)}, u32[]{:S(2)}) collective-permute-start(f32[384,128]{1,0:T(8,128)S(1)} %block_total.3), channel_id=1, source_target_pairs={{0,4},{4,8},{8,12},{12,16},{16,20},{20,24},{24,28},{28,0},{1,5},{5... | collective-permute-start | bytes 589832 | tf_op jit(solution)/shard_map/ppermute | solution.py:323
  29.9 12.8 %collective-permute-start.5 = (f32[392,128]{1,0:T(8,128)S(1)}, f32[392,128]{1,0:T(8,128)S(1)}, u32[]{:S(2)}, u32[]{:S(2)}) collective-permute-start(f32[392,128]{1,0:T(8,128)S(1)} %get-tuple-element.29), channel_id=1, source_target_pairs={{0,3},{1,2},{2,1},{3,0},{4,7},{5,6},{6,5},{7,4},{8,11},{9,10},{10,... | collective-permute-start | bytes 602120 | tf_op jit(solution)/shard_map/ppermute | solution.py:317
  32.7 13.3 %collective-permute-start.6 = (f32[392,128]{1,0:T(8,128)S(1)}, f32[392,128]{1,0:T(8,128)S(1)}, u32[]{:S(2)}, u32[]{:S(2)}) collective-permute-start(f32[392,128]{1,0:T(8,128)S(1)} %get-tuple-element.30), channel_id=1, source_target_pairs={{0,2},{1,3},{2,0},{3,1},{4,6},{5,7},{6,4},{7,5},{8,10},{9,11},{10,... | collective-permute-start | bytes 602120 | tf_op jit(solution)/shard_map/ppermute | solution.py:317
  32.7 13.3 %copy-start = (bf16[128,2048]{1,0:T(8,128)(2,1)S(1)}, bf16[128,2048]{1,0:T(8,128)(2,1)}, u32[]{:S(2)}) copy-start(bf16[128,2048]{1,0:T(8,128)(2,1)} %q_ref.1) | copy-start | bytes 1572868
  32.7 13.3 %collective-permute-start.7 = (f32[392,128]{1,0:T(8,128)S(1)}, f32[392,128]{1,0:T(8,128)S(1)}, u32[]{:S(2)}, u32[]{:S(2)}) collective-permute-start(f32[392,128]{1,0:T(8,128)S(1)} %get-tuple-element.31), channel_id=1, source_target_pairs={{0,1},{1,0},{2,3},{3,2},{4,5},{5,4},{6,7},{7,6},{8,9},{9,8},{10,11... | collective-permute-start | bytes 602120 | tf_op jit(solution)/shard_map/ppermute | solution.py:317
  40.9 12.7 %collective-permute-start.13 = (f32[384,128]{1,0:T(8,128)S(1)}, f32[384,128]{1,0:T(8,128)S(1)}, u32[]{:S(2)}, u32[]{:S(2)}) collective-permute-start(f32[384,128]{1,0:T(8,128)S(1)} %get-tuple-element.38), channel_id=1, source_target_pairs={{0,2},{1,3},{2,0},{3,1},{4,6},{5,7},{6,4},{7,5},{8,10},{9,11},{10,... | collective-permute-start | bytes 589832 | tf_op jit(solution)/shard_map/ppermute | solution.py:317
  41.0 12.9 %collective-permute-start.14 = (f32[384,128]{1,0:T(8,128)S(1)}, f32[384,128]{1,0:T(8,128)S(1)}, u32[]{:S(2)}, u32[]{:S(2)}) collective-permute-start(f32[384,128]{1,0:T(8,128)S(1)} %get-tuple-element.39), channel_id=1, source_target_pairs={{0,3},{1,2},{2,1},{3,0},{4,7},{5,6},{6,5},{7,4},{8,11},{9,10},{10,... | collective-permute-start | bytes 589832 | tf_op jit(solution)/shard_map/ppermute | solution.py:317
  42.7 3.3 %copy-start.3 = (f32[16]{0:T(128)S(1)}, f32[16]{0:T(128)}, u32[]{:S(2)}) copy-start(f32[16]{0:T(128)} %ridge_ref.1) | copy-start | bytes 196
  42.7 9.8 %collective-permute-start.15 = (f32[384,128]{1,0:T(8,128)S(1)}, f32[384,128]{1,0:T(8,128)S(1)}, u32[]{:S(2)}, u32[]{:S(2)}) collective-permute-start(f32[384,128]{1,0:T(8,128)S(1)} %get-tuple-element.41), channel_id=1, source_target_pairs={{0,1},{1,0},{2,3},{3,2},{4,5},{5,4},{6,7},{7,6},{8,9},{9,8},{10,11... | collective-permute-start | bytes 589832 | tf_op jit(solution)/shard_map/ppermute | solution.py:317

commit v9 on v8

--- a/solution.py
+++ b/solution.py
@@ -262,16 +262,18 @@
 def readout_kernel(width, heads, early, masks, x_ref, near_ref, *refs):
     slots, (out_hbm, out, sems) = refs[: len(masks)], refs[-3:]
     copies = []
+    group = heads - early
     for slot, state in enumerate(slots):
-        for head in range(early, heads):
-            at = (lax.axis_index("near") ^ masks[slot]) * heads + head
+        start = (lax.axis_index("near") ^ masks[slot]) * heads + early
+        for head in range(group):
+            at = start + head
             lanes = pl.ds(pl.multiple_of(at * width, width), width)
             pair = x_ref[:, pl.ds(pl.multiple_of(at * 2 * width, 2 * width), 2 * width)]
-            far = far_part(pair, pair[:, :width], state[pl.ds((head - early) * width, width), :])
-            number = len(copies)
-            out[number] = near_ref[:, lanes] + far
-            copies.append(pltpu.make_async_copy(out.at[number], out_hbm.at[:, lanes], sems.at[number]))
-            copies[-1].start()
+            far = far_part(pair, pair[:, :width], state[pl.ds(head * width, width), :])
+            out[slot, :, pl.ds(head * width, width)] = near_ref[:, lanes] + far
+        span = pl.ds(pl.multiple_of(start * width, width), group * width)
+        copies.append(pltpu.make_async_copy(out.at[slot], out_hbm.at[:, span], sems.at[slot]))
+        copies[-1].start()
     for copy in copies:
         copy.wait()
 
@@ -392,7 +394,6 @@
         ],
     )
     for slots in (range(near // 2), range(near // 2, near)):
-        count = len(slots) * (heads - early)
         out = call(
             functools.partial(readout_kernel, width, heads, early, [orders[3][slot] for slot in slots]),
             "readout",
@@ -401,7 +402,10 @@
             [VMEM] * (2 + len(slots)) + [HBM],
             (solved, local, *[states[1][slot] for slot in slots], out),
             out_specs=HBM,
-            scratch_shapes=[pltpu.VMEM((count, row_count, width), jnp.float32), pltpu.SemaphoreType.DMA((count,))],
+            scratch_shapes=[
+                pltpu.VMEM((len(slots), row_count, (heads - early) * width), jnp.float32),
+                pltpu.SemaphoreType.DMA((len(slots),)),
+            ],
             input_output_aliases={2 + len(slots): 0},
         )
     return out

time: 55.2 us -> 55.2 us (level)
  no operation moved by 1% of the time
where the time goes in v9:
time: 55.2 us; the launch traced here: 54.9 us
  starting transfers between devices  22.7 us (41%)
  waiting for transfers between devices  20.2 us (37%)
  Pallas kernels  12 us (22%)
    ppermute x12, starting transfers between devices, exchange(): lax.ppermute(slot, 'near', [(i, i ^ mask) for i in range(near)])  14.1 us
    ppermute x12, waiting for transfers between devices, exchange(): lax.ppermute(slot, 'near', [(i, i ^ mask) for i in range(near)])  12.3 us
    pallas_call x9, Pallas kernels, call(): pl.pallas_call(kernel, out_shape=out_shape, in_specs=in_specs, compiler_p...  12 us
    ppermute x4, starting transfers between devices, onward(): lax.ppermute(value, ('outer', 'half'), [(i, (i + step) % blocks) for i in...  8.61 us
    ppermute x4, waiting for transfers between devices, onward(): lax.ppermute(value, ('outer', 'half'), [(i, (i + step) % blocks) for i in...  7.9 us
  transfers between devices with their start and end apart: 16, of which 8 were waited for; matrix products, arithmetic and copies ran while one was open for 0% of the time, Pallas kernels for 17%

profile of v9, /device:TPU:1, one launch (start us, length us, event | category | flops | bytes accessed | tf_op | source)
XLA Modules:
  0.0 54.9 jit_solution(10468531840893594836)
XLA Ops:
  0.0 0.0 copy-start.1
  0.0 0.0 copy-start.2
  0.0 1.8 %own_first.1 = (f32[392,128]{1,0:T(8,128)S(1)}, f32[392,128]{1,0:T(8,128)S(1)}) custom-call(s32[1,128]{1,0:T(1,128)} %bitcast.1, bf16[128,2048]{1,0:T(8,128)(2,1)} %k_ref.3, bf16[128,2048]{1,0:T(8,128)(2,1)} %v_ref.3), custom_call_target="tpu_custom_call" | custom-call | flops 536870912 | tf_op jit(solution)/shard_map/own_first/pallas_call | solution.py:289
  1.8 0.0 copy-start.4
  1.8 3.1 %collective-permute-start = (f32[392,128]{1,0:T(8,128)S(1)}, f32[392,128]{1,0:T(8,128)S(1)}, u32[]{:S(2)}, u32[]{:S(2)}) collective-permute-start(f32[392,128]{1,0:T(8,128)S(1)} %get-tuple-element.25), channel_id=1, source_target_pairs={{0,3},{1,2},{2,1},{3,0},{4,7},{5,6},{6,5},{7,4},{8,11},{9,10},{10,... | collective-permute-start | bytes 602120 | tf_op jit(solution)/shard_map/ppermute | solution.py:319
  4.9 0.2 collective-permute-start.1
  5.1 0.0 copy-done.1
  5.1 0.0 copy-done.2
  5.1 0.0 copy-done.4
  5.1 1.0 %own_rest.1 = (f32[384,128]{1,0:T(8,128)S(1)}, f32[384,128]{1,0:T(8,128)S(1)}, f32[384,128]{1,0:T(8,128)S(1)}, f32[384,128]{1,0:T(8,128)S(1)}, f32[392,128]{1,0:T(8,128)S(1)}, /*index=5*/f32[392,128]{1,0:T(8,128)S(1)}) custom-call(s32[1,128]{1,0:T(1,128)S(1)} %bitcast.2, bf16[128,2048]{1,0:T(8,128)(2,1)S(1)} %copy-done.1, bf16[128,2048]{1,0:T(8,128)(2,1)S(1)} %copy-done.2), custom_call_target="tpu_custom_call" | custom-call | flops 536870912 | tf_op jit(solution)/shard_map/own_rest/pallas_call | solution.py:289
  6.1 0.3 collective-permute-start.2
  6.4 1.3 %collective-permute-start.8 = (f32[384,128]{1,0:T(8,128)S(1)}, f32[384,128]{1,0:T(8,128)S(1)}, u32[]{:S(2)}, u32[]{:S(2)}) collective-permute-start(f32[384,128]{1,0:T(8,128)S(1)} %get-tuple-element.35), channel_id=1, source_target_pairs={{0,1},{1,0},{2,3},{3,2},{4,5},{5,4},{6,7},{7,6},{8,9},{9,8},{10,11... | collective-permute-start | bytes 589832 | tf_op jit(solution)/shard_map/ppermute | solution.py:319
  7.6 1.3 %collective-permute-start.9 = (f32[384,128]{1,0:T(8,128)S(1)}, f32[384,128]{1,0:T(8,128)S(1)}, u32[]{:S(2)}, u32[]{:S(2)}) collective-permute-start(f32[384,128]{1,0:T(8,128)S(1)} %get-tuple-element.36), channel_id=1, source_target_pairs={{0,2},{1,3},{2,0},{3,1},{4,6},{5,7},{6,4},{7,5},{8,10},{9,11},{10,... | collective-permute-start | bytes 589832 | tf_op jit(solution)/shard_map/ppermute | solution.py:319
  8.9 0.7 %collective-permute-done.refs_1_.refs_3_ = f32[392,128]{1,0:T(8,128)S(1)} collective-permute-done((f32[392,128]{1,0:T(8,128)S(1)}, f32[392,128]{1,0:T(8,128)S(1)}, u32[]{:S(2)}, u32[]{:S(2)}) %collective-permute-start) | collective-permute-done | bytes 200736 | tf_op jit(solution)/shard_map/ppermute | solution.py:319
  9.6 2.0 %collective-permute-start.10 = (f32[384,128]{1,0:T(8,128)S(1)}, f32[384,128]{1,0:T(8,128)S(1)}, u32[]{:S(2)}, u32[]{:S(2)}) collective-permute-start(f32[384,128]{1,0:T(8,128)S(1)} %get-tuple-element.37), channel_id=1, source_target_pairs={{0,3},{1,2},{2,1},{3,0},{4,7},{5,6},{6,5},{7,4},{8,11},{9,10},{10,... | collective-permute-start | bytes 589832 | tf_op jit(solution)/shard_map/ppermute | solution.py:319
  11.7 2.1 %collective-permute-done.1.refs_2_ = f32[392,128]{1,0:T(8,128)S(1)} collective-permute-done((f32[392,128]{1,0:T(8,128)S(1)}, f32[392,128]{1,0:T(8,128)S(1)}, u32[]{:S(2)}, u32[]{:S(2)}) %collective-permute-start.1) | collective-permute-done | bytes 200736 | tf_op jit(solution)/shard_map/ppermute | solution.py:319
  13.8 0.4 collective-permute-done.2.refs_3_.refs_1_
  14.2 0.1 block_total.2
  14.3 3.4 %collective-permute-start.4 = (f32[392,128]{1,0:T(8,128)S(1)}, f32[392,128]{1,0:T(8,128)S(1)}, u32[]{:S(2)}, u32[]{:S(2)}) collective-permute-start(f32[392,128]{1,0:T(8,128)S(1)} %block_total.2), channel_id=1, source_target_pairs={{0,8},{4,12},{8,16},{12,20},{16,24},{20,28},{24,0},{28,4},{1,9},{5... | collective-permute-start | bytes 602120 | tf_op jit(solution)/shard_map/ppermute | solution.py:325
  17.7 2.3 %collective-permute-start.3 = (f32[392,128]{1,0:T(8,128)S(1)}, f32[392,128]{1,0:T(8,128)S(1)}, u32[]{:S(2)}, u32[]{:S(2)}) collective-permute-start(f32[392,128]{1,0:T(8,128)S(1)} %block_total.2), channel_id=1, source_target_pairs={{0,4},{4,8},{8,12},{12,16},{16,20},{20,24},{24,28},{28,0},{1,5},{5... | collective-permute-start | bytes 602120 | tf_op jit(solution)/shard_map/ppermute | solution.py:325
  20.0 0.0 collective-permute-done.8.refs_5_.refs_7_
  20.0 0.0 collective-permute-done.9.refs_6_.refs_8_
  20.0 6.3 %collective-permute-done.10.refs_7_.refs_9_ = f32[384,128]{1,0:T(8,128)S(1)} collective-permute-done((f32[384,128]{1,0:T(8,128)S(1)}, f32[384,128]{1,0:T(8,128)S(1)}, u32[]{:S(2)}, u32[]{:S(2)}) %collective-permute-start.10) | collective-permute-done | bytes 196640 | tf_op jit(solution)/shard_map/ppermute | solution.py:319
  26.3 0.1 block_total.3
  26.4 2.9 %collective-permute-start.12 = (f32[384,128]{1,0:T(8,128)S(1)}, f32[384,128]{1,0:T(8,128)S(1)}, u32[]{:S(2)}, u32[]{:S(2)}) collective-permute-start(f32[384,128]{1,0:T(8,128)S(1)} %block_total.3), channel_id=1, source_target_pairs={{0,8},{4,12},{8,16},{12,20},{16,24},{20,28},{24,0},{28,4},{1,9},{5... | collective-permute-start | bytes 589832 | tf_op jit(solution)/shard_map/ppermute | solution.py:325
  29.3 0.0 collective-permute-start.11
  29.3 0.0 collective-permute-done.4.refs_5_
  29.3 0.3 collective-permute-done.3.refs_4_
  29.6 0.3 prefixes.2
  29.9 2.8 %collective-permute-start.5 = (f32[392,128]{1,0:T(8,128)S(1)}, f32[392,128]{1,0:T(8,128)S(1)}, u32[]{:S(2)}, u32[]{:S(2)}) collective-permute-start(f32[392,128]{1,0:T(8,128)S(1)} %get-tuple-element.29), channel_id=1, source_target_pairs={{0,3},{1,2},{2,1},{3,0},{4,7},{5,6},{6,5},{7,4},{8,11},{9,10},{10,... | collective-permute-start | bytes 602120 | tf_op jit(solution)/shard_map/ppermute | solution.py:319
  32.7 0.0 collective-permute-start.6
  32.7 0.0 copy-start
  32.7 0.4 collective-permute-start.7
  33.1 0.0 collective-permute-done.12.refs_11_
  33.1 7.6 %collective-permute-done.11.refs_10_ = f32[384,128]{1,0:T(8,128)S(1)} collective-permute-done((f32[384,128]{1,0:T(8,128)S(1)}, f32[384,128]{1,0:T(8,128)S(1)}, u32[]{:S(2)}, u32[]{:S(2)}) %collective-permute-start.11) | collective-permute-done | bytes 196640 | tf_op jit(solution)/shard_map/ppermute | solution.py:325
  40.6 0.2 prefixes.3
  40.9 0.1 collective-permute-start.13
  41.0 1.7 %collective-permute-start.14 = (f32[384,128]{1,0:T(8,128)S(1)}, f32[384,128]{1,0:T(8,128)S(1)}, u32[]{:S(2)}, u32[]{:S(2)}) collective-permute-start(f32[384,128]{1,0:T(8,128)S(1)} %get-tuple-element.39), channel_id=1, source_target_pairs={{0,3},{1,2},{2,1},{3,0},{4,7},{5,6},{6,5},{7,4},{8,11},{9,10},{10,... | collective-permute-start | bytes 589832 | tf_op jit(solution)/shard_map/ppermute | solution.py:319
  42.7 0.0 collective-permute-done.5.refs_1_
  42.7 0.0 copy-start.3
  42.7 0.9 %collective-permute-start.15 = (f32[384,128]{1,0:T(8,128)S(1)}, f32[384,128]{1,0:T(8,128)S(1)}, u32[]{:S(2)}, u32[]{:S(2)}) collective-permute-start(f32[384,128]{1,0:T(8,128)S(1)} %get-tuple-element.41), channel_id=1, source_target_pairs={{0,1},{1,0},{2,3},{3,2},{4,5},{5,4},{6,7},{7,6},{8,9},{9,8},{10,11... | collective-permute-start | bytes 589832 | tf_op jit(solution)/shard_map/ppermute | solution.py:319
  43.6 2.4 %collective-permute-done.6.refs_2_ = f32[392,128]{1,0:T(8,128)S(1)} collective-permute-done((f32[392,128]{1,0:T(8,128)S(1)}, f32[392,128]{1,0:T(8,128)S(1)}, u32[]{:S(2)}, u32[]{:S(2)}) %collective-permute-start.6) | collective-permute-done | bytes 200736 | tf_op jit(solution)/shard_map/ppermute | solution.py:319
  46.0 0.0 collective-permute-done.7.refs_3_
  46.0 0.0 copy-done
  46.0 0.0 copy-done.3
  46.0 6.5 %solve.1 = (bf16[128,4096]{1,0:T(8,128)(2,1)S(1)}, f32[128,2048]{1,0:T(8,128)S(1)}, f32[128,2048]{1,0:T(8,128)}) custom-call(f32[16]{0:T(128)S(1)} %copy-done.3, s32[1,128]{1,0:T(1,128)S(1)} %bitcast.3, bf16[128,2048]{1,0:T(8,128)(2,1)S(1)} %copy-done, bf16[128,2048]{1,0:T(8,128)(2,1)S(1)} %copy-done.1, bf16[128,2048]{1,0:T(8,128)(2,1)S(1)} %copy-done.2, ...), custom_call_target="tpu_custom_call" | custom-call | flops 6442450944 | tf_op jit(solution)/shard_map/solve/pallas_call | solution.py:289
  52.5 0.0 collective-permute-done.15.refs_1_
  52.5 1.0 %readout.2.refs_2_ = f32[128,2048]{1,0:T(8,128)} custom-call(bf16[128,4096]{1,0:T(8,128)(2,1)S(1)} %get-tuple-element.32.x_ref, f32[128,2048]{1,0:T(8,128)S(1)} %get-tuple-element.33.near_ref, f32[384,128]{1,0:T(8,128)S(1)} %get-tuple-element.40.refs_0_, f32[384,128]{1,0:T(8,128)S(1)} %collective-permute-done.15.refs_1_, ...), custom_call_target="tpu_custom_call", output_to_operand_aliasing={{}: (4, {})} | custom-call | flops 536870912 | tf_op jit(solution)/shard_map/readout/pallas_call | solution.py:289
  53.6 0.0 collective-permute-done.13.refs_0_
  53.6 0.3 collective-permute-done.14.refs_1_
  53.9 1.0 %readout.3 = f32[128,2048]{1,0:T(8,128)} custom-call(bf16[128,4096]{1,0:T(8,128)(2,1)S(1)} %get-tuple-element.32.x_ref, f32[128,2048]{1,0:T(8,128)S(1)} %get-tuple-element.33.near_ref, f32[384,128]{1,0:T(8,128)S(1)} %collective-permute-done.13.refs_0_, f32[384,128]{1,0:T(8,128)S(1)} %collective-permute-done.14.refs_1_, ...), custom_call_target="tpu_custom_call", output_to_operand_aliasing={{}: (4, {})} | custom-call | flops 536870912 | tf_op jit(solution)/shard_map/readout/pallas_call | solution.py:289
Async XLA Ops:
  0.0 5.1 %copy-start.1 = (bf16[128,2048]{1,0:T(8,128)(2,1)S(1)}, bf16[128,2048]{1,0:T(8,128)(2,1)}, u32[]{:S(2)}) copy-start(bf16[128,2048]{1,0:T(8,128)(2,1)} %k_ref.3) | copy-start | bytes 1572868
  0.0 5.1 %copy-start.2 = (bf16[128,2048]{1,0:T(8,128)(2,1)S(1)}, bf16[128,2048]{1,0:T(8,128)(2,1)}, u32[]{:S(2)}) copy-start(bf16[128,2048]{1,0:T(8,128)(2,1)} %v_ref.3) | copy-start | bytes 1572868
  1.8 3.3 %copy-start.4 = (s32[128]{0:T(128)S(1)}, s32[128]{0:T(128)}, u32[]{:S(2)}) copy-start(s32[128]{0:T(128)} %param.8) | copy-start | bytes 1540
  1.8 7.8 %collective-permute-start = (f32[392,128]{1,0:T(8,128)S(1)}, f32[392,128]{1,0:T(8,128)S(1)}, u32[]{:S(2)}, u32[]{:S(2)}) collective-permute-start(f32[392,128]{1,0:T(8,128)S(1)} %get-tuple-element.25), channel_id=1, source_target_pairs={{0,3},{1,2},{2,1},{3,0},{4,7},{5,6},{6,5},{7,4},{8,11},{9,10},{10,... | collective-permute-start | bytes 602120 | tf_op jit(solution)/shard_map/ppermute | solution.py:319
  4.9 8.9 %collective-permute-start.1 = (f32[392,128]{1,0:T(8,128)S(1)}, f32[392,128]{1,0:T(8,128)S(1)}, u32[]{:S(2)}, u32[]{:S(2)}) collective-permute-start(f32[392,128]{1,0:T(8,128)S(1)} %get-tuple-element.26), channel_id=1, source_target_pairs={{0,2},{1,3},{2,0},{3,1},{4,6},{5,7},{6,4},{7,5},{8,10},{9,11},{10,... | collective-permute-start | bytes 602120 | tf_op jit(solution)/shard_map/ppermute | solution.py:319
  6.1 8.1 %collective-permute-start.2 = (f32[392,128]{1,0:T(8,128)S(1)}, f32[392,128]{1,0:T(8,128)S(1)}, u32[]{:S(2)}, u32[]{:S(2)}) collective-permute-start(f32[392,128]{1,0:T(8,128)S(1)} %get-tuple-element.27), channel_id=1, source_target_pairs={{0,1},{1,0},{2,3},{3,2},{4,5},{5,4},{6,7},{7,6},{8,9},{9,8},{10,11... | collective-permute-start | bytes 602120 | tf_op jit(solution)/shard_map/ppermute | solution.py:319
  6.4 13.7 %collective-permute-start.8 = (f32[384,128]{1,0:T(8,128)S(1)}, f32[384,128]{1,0:T(8,128)S(1)}, u32[]{:S(2)}, u32[]{:S(2)}) collective-permute-start(f32[384,128]{1,0:T(8,128)S(1)} %get-tuple-element.35), channel_id=1, source_target_pairs={{0,1},{1,0},{2,3},{3,2},{4,5},{5,4},{6,7},{7,6},{8,9},{9,8},{10,11... | collective-permute-start | bytes 589832 | tf_op jit(solution)/shard_map/ppermute | solution.py:319
  7.6 12.4 %collective-permute-start.9 = (f32[384,128]{1,0:T(8,128)S(1)}, f32[384,128]{1,0:T(8,128)S(1)}, u32[]{:S(2)}, u32[]{:S(2)}) collective-permute-start(f32[384,128]{1,0:T(8,128)S(1)} %get-tuple-element.36), channel_id=1, source_target_pairs={{0,2},{1,3},{2,0},{3,1},{4,6},{5,7},{6,4},{7,5},{8,10},{9,11},{10,... | collective-permute-start | bytes 589832 | tf_op jit(solution)/shard_map/ppermute | solution.py:319
  9.6 16.7 %collective-permute-start.10 = (f32[384,128]{1,0:T(8,128)S(1)}, f32[384,128]{1,0:T(8,128)S(1)}, u32[]{:S(2)}, u32[]{:S(2)}) collective-permute-start(f32[384,128]{1,0:T(8,128)S(1)} %get-tuple-element.37), channel_id=1, source_target_pairs={{0,3},{1,2},{2,1},{3,0},{4,7},{5,6},{6,5},{7,4},{8,11},{9,10},{10,... | collective-permute-start | bytes 589832 | tf_op jit(solution)/shard_map/ppermute | solution.py:319
  14.3 15.0 %collective-permute-start.4 = (f32[392,128]{1,0:T(8,128)S(1)}, f32[392,128]{1,0:T(8,128)S(1)}, u32[]{:S(2)}, u32[]{:S(2)}) collective-permute-start(f32[392,128]{1,0:T(8,128)S(1)} %block_total.2), channel_id=1, source_target_pairs={{0,8},{4,12},{8,16},{12,20},{16,24},{20,28},{24,0},{28,4},{1,9},{5... | collective-permute-start | bytes 602120 | tf_op jit(solution)/shard_map/ppermute | solution.py:325
  17.7 11.9 %collective-permute-start.3 = (f32[392,128]{1,0:T(8,128)S(1)}, f32[392,128]{1,0:T(8,128)S(1)}, u32[]{:S(2)}, u32[]{:S(2)}) collective-permute-start(f32[392,128]{1,0:T(8,128)S(1)} %block_total.2), channel_id=1, source_target_pairs={{0,4},{4,8},{8,12},{12,16},{16,20},{20,24},{24,28},{28,0},{1,5},{5... | collective-permute-start | bytes 602120 | tf_op jit(solution)/shard_map/ppermute | solution.py:325
  26.4 6.7 %collective-permute-start.12 = (f32[384,128]{1,0:T(8,128)S(1)}, f32[384,128]{1,0:T(8,128)S(1)}, u32[]{:S(2)}, u32[]{:S(2)}) collective-permute-start(f32[384,128]{1,0:T(8,128)S(1)} %block_total.3), channel_id=1, source_target_pairs={{0,8},{4,12},{8,16},{12,20},{16,24},{20,28},{24,0},{28,4},{1,9},{5... | collective-permute-start | bytes 589832 | tf_op jit(solution)/shard_map/ppermute | solution.py:325
  29.3 11.4 %collective-permute-start.11 = (f32[384,128]{1,0:T(8,128)S(1)}, f32[384,128]{1,0:T(8,128)S(1)}, u32[]{:S(2)}, u32[]{:S(2)}) collective-permute-start(f32[384,128]{1,0:T(8,128)S(1)} %block_total.3), channel_id=1, source_target_pairs={{0,4},{4,8},{8,12},{12,16},{16,20},{20,24},{24,28},{28,0},{1,5},{5... | collective-permute-start | bytes 589832 | tf_op jit(solution)/shard_map/ppermute | solution.py:325
  29.9 12.8 %collective-permute-start.5 = (f32[392,128]{1,0:T(8,128)S(1)}, f32[392,128]{1,0:T(8,128)S(1)}, u32[]{:S(2)}, u32[]{:S(2)}) collective-permute-start(f32[392,128]{1,0:T(8,128)S(1)} %get-tuple-element.29), channel_id=1, source_target_pairs={{0,3},{1,2},{2,1},{3,0},{4,7},{5,6},{6,5},{7,4},{8,11},{9,10},{10,... | collective-permute-start | bytes 602120 | tf_op jit(solution)/shard_map/ppermute | solution.py:319
  32.7 13.3 %collective-permute-start.6 = (f32[392,128]{1,0:T(8,128)S(1)}, f32[392,128]{1,0:T(8,128)S(1)}, u32[]{:S(2)}, u32[]{:S(2)}) collective-permute-start(f32[392,128]{1,0:T(8,128)S(1)} %get-tuple-element.30), channel_id=1, source_target_pairs={{0,2},{1,3},{2,0},{3,1},{4,6},{5,7},{6,4},{7,5},{8,10},{9,11},{10,... | collective-permute-start | bytes 602120 | tf_op jit(solution)/shard_map/ppermute | solution.py:319
  32.7 13.3 %copy-start = (bf16[128,2048]{1,0:T(8,128)(2,1)S(1)}, bf16[128,2048]{1,0:T(8,128)(2,1)}, u32[]{:S(2)}) copy-start(bf16[128,2048]{1,0:T(8,128)(2,1)} %q_ref.1) | copy-start | bytes 1572868
  32.7 13.3 %collective-permute-start.7 = (f32[392,128]{1,0:T(8,128)S(1)}, f32[392,128]{1,0:T(8,128)S(1)}, u32[]{:S(2)}, u32[]{:S(2)}) collective-permute-start(f32[392,128]{1,0:T(8,128)S(1)} %get-tuple-element.31), channel_id=1, source_target_pairs={{0,1},{1,0},{2,3},{3,2},{4,5},{5,4},{6,7},{7,6},{8,9},{9,8},{10,11... | collective-permute-start | bytes 602120 | tf_op jit(solution)/shard_map/ppermute | solution.py:319
  40.9 12.7 %collective-permute-start.13 = (f32[384,128]{1,0:T(8,128)S(1)}, f32[384,128]{1,0:T(8,128)S(1)}, u32[]{:S(2)}, u32[]{:S(2)}) collective-permute-start(f32[384,128]{1,0:T(8,128)S(1)} %get-tuple-element.38), channel_id=1, source_target_pairs={{0,2},{1,3},{2,0},{3,1},{4,6},{5,7},{6,4},{7,5},{8,10},{9,11},{10,... | collective-permute-start | bytes 589832 | tf_op jit(solution)/shard_map/ppermute | solution.py:319
  41.0 12.9 %collective-permute-start.14 = (f32[384,128]{1,0:T(8,128)S(1)}, f32[384,128]{1,0:T(8,128)S(1)}, u32[]{:S(2)}, u32[]{:S(2)}) collective-permute-start(f32[384,128]{1,0:T(8,128)S(1)} %get-tuple-element.39), channel_id=1, source_target_pairs={{0,3},{1,2},{2,1},{3,0},{4,7},{5,6},{6,5},{7,4},{8,11},{9,10},{10,... | collective-permute-start | bytes 589832 | tf_op jit(solution)/shard_map/ppermute | solution.py:319
  42.7 3.3 %copy-start.3 = (f32[16]{0:T(128)S(1)}, f32[16]{0:T(128)}, u32[]{:S(2)}) copy-start(f32[16]{0:T(128)} %ridge_ref.1) | copy-start | bytes 196
  42.7 9.8 %collective-permute-start.15 = (f32[384,128]{1,0:T(8,128)S(1)}, f32[384,128]{1,0:T(8,128)S(1)}, u32[]{:S(2)}, u32[]{:S(2)}) collective-permute-start(f32[384,128]{1,0:T(8,128)S(1)} %get-tuple-element.41), channel_id=1, source_target_pairs={{0,1},{1,0},{2,3},{3,2},{4,5},{5,4},{6,7},{7,6},{8,9},{9,8},{10,11... | collective-permute-start | bytes 589832 | tf_op jit(solution)/shard_map/ppermute | solution.py:319

commit v10 on v9

--- a/solution.py
+++ b/solution.py
@@ -328,7 +328,7 @@
 
     rising = list(range(near))
     falling = rising[:1] + rising[:0:-1]
-    orders = falling, rising, falling, rising
+    orders = falling, rising, rising[:1] + rising[-1:] + rising[1:-1], rising
     soon, later = orders[0][1 : 1 + near // 2], orders[0][1 + near // 2 :] + [0]
     own_soon = call(
         functools.partial(own_first_kernel, width, packs, early, soon),

time: 55.2 us -> 55.2 us (level)
  no operation moved by 1% of the time
where the time goes in v10:
time: 55.2 us; the launch traced here: 54.9 us
  starting transfers between devices  22.7 us (41%)
  waiting for transfers between devices  20.2 us (37%)
  Pallas kernels  11.9 us (22%)
    ppermute x12, starting transfers between devices, exchange(): lax.ppermute(slot, 'near', [(i, i ^ mask) for i in range(near)])  14.1 us
    ppermute x12, waiting for transfers between devices, exchange(): lax.ppermute(slot, 'near', [(i, i ^ mask) for i in range(near)])  12.3 us
    pallas_call x9, Pallas kernels, call(): pl.pallas_call(kernel, out_shape=out_shape, in_specs=in_specs, compiler_p...  11.9 us
    ppermute x4, starting transfers between devices, onward(): lax.ppermute(value, ('outer', 'half'), [(i, (i + step) % blocks) for i in...  8.61 us
    ppermute x4, waiting for transfers between devices, onward(): lax.ppermute(value, ('outer', 'half'), [(i, (i + step) % blocks) for i in...  7.9 us
  transfers between devices with their start and end apart: 16, of which 8 were waited for; matrix products, arithmetic and copies ran while one was open for 0% of the time, Pallas kernels for 17%

profile of v10, /device:TPU:1, one launch (start us, length us, event | category | flops | bytes accessed | tf_op | source)
XLA Modules:
  0.0 54.9 jit_solution(8651230007077483706)
XLA Ops:
  0.0 0.0 copy-start.1
  0.0 0.0 copy-start.2
  0.0 1.8 %own_first.1 = (f32[392,128]{1,0:T(8,128)S(1)}, f32[392,128]{1,0:T(8,128)S(1)}) custom-call(s32[1,128]{1,0:T(1,128)} %bitcast.1, bf16[128,2048]{1,0:T(8,128)(2,1)} %k_ref.3, bf16[128,2048]{1,0:T(8,128)(2,1)} %v_ref.3), custom_call_target="tpu_custom_call" | custom-call | flops 536870912 | tf_op jit(solution)/shard_map/own_first/pallas_call | solution.py:289
  1.8 0.0 copy-start.4
  1.8 3.1 %collective-permute-start = (f32[392,128]{1,0:T(8,128)S(1)}, f32[392,128]{1,0:T(8,128)S(1)}, u32[]{:S(2)}, u32[]{:S(2)}) collective-permute-start(f32[392,128]{1,0:T(8,128)S(1)} %get-tuple-element.25), channel_id=1, source_target_pairs={{0,3},{1,2},{2,1},{3,0},{4,7},{5,6},{6,5},{7,4},{8,11},{9,10},{10,... | collective-permute-start | bytes 602120 | tf_op jit(solution)/shard_map/ppermute | solution.py:319
  4.9 0.2 collective-permute-start.1
  5.1 0.0 copy-done.1
  5.1 0.0 copy-done.2
  5.1 0.0 copy-done.4
  5.1 1.0 %own_rest.1 = (f32[384,128]{1,0:T(8,128)S(1)}, f32[384,128]{1,0:T(8,128)S(1)}, f32[384,128]{1,0:T(8,128)S(1)}, f32[384,128]{1,0:T(8,128)S(1)}, f32[392,128]{1,0:T(8,128)S(1)}, /*index=5*/f32[392,128]{1,0:T(8,128)S(1)}) custom-call(s32[1,128]{1,0:T(1,128)S(1)} %bitcast.2, bf16[128,2048]{1,0:T(8,128)(2,1)S(1)} %copy-done.1, bf16[128,2048]{1,0:T(8,128)(2,1)S(1)} %copy-done.2), custom_call_target="tpu_custom_call" | custom-call | flops 536870912 | tf_op jit(solution)/shard_map/own_rest/pallas_call | solution.py:289
  6.1 0.3 collective-permute-start.2
  6.4 1.3 %collective-permute-start.8 = (f32[384,128]{1,0:T(8,128)S(1)}, f32[384,128]{1,0:T(8,128)S(1)}, u32[]{:S(2)}, u32[]{:S(2)}) collective-permute-start(f32[384,128]{1,0:T(8,128)S(1)} %get-tuple-element.35), channel_id=1, source_target_pairs={{0,1},{1,0},{2,3},{3,2},{4,5},{5,4},{6,7},{7,6},{8,9},{9,8},{10,11... | collective-permute-start | bytes 589832 | tf_op jit(solution)/shard_map/ppermute | solution.py:319
  7.6 1.3 %collective-permute-start.9 = (f32[384,128]{1,0:T(8,128)S(1)}, f32[384,128]{1,0:T(8,128)S(1)}, u32[]{:S(2)}, u32[]{:S(2)}) collective-permute-start(f32[384,128]{1,0:T(8,128)S(1)} %get-tuple-element.36), channel_id=1, source_target_pairs={{0,2},{1,3},{2,0},{3,1},{4,6},{5,7},{6,4},{7,5},{8,10},{9,11},{10,... | collective-permute-start | bytes 589832 | tf_op jit(solution)/shard_map/ppermute | solution.py:319
  8.9 0.7 %collective-permute-done.refs_1_.refs_3_ = f32[392,128]{1,0:T(8,128)S(1)} collective-permute-done((f32[392,128]{1,0:T(8,128)S(1)}, f32[392,128]{1,0:T(8,128)S(1)}, u32[]{:S(2)}, u32[]{:S(2)}) %collective-permute-start) | collective-permute-done | bytes 200736 | tf_op jit(solution)/shard_map/ppermute | solution.py:319
  9.6 2.0 %collective-permute-start.10 = (f32[384,128]{1,0:T(8,128)S(1)}, f32[384,128]{1,0:T(8,128)S(1)}, u32[]{:S(2)}, u32[]{:S(2)}) collective-permute-start(f32[384,128]{1,0:T(8,128)S(1)} %get-tuple-element.37), channel_id=1, source_target_pairs={{0,3},{1,2},{2,1},{3,0},{4,7},{5,6},{6,5},{7,4},{8,11},{9,10},{10,... | collective-permute-start | bytes 589832 | tf_op jit(solution)/shard_map/ppermute | solution.py:319
  11.7 2.1 %collective-permute-done.1.refs_2_ = f32[392,128]{1,0:T(8,128)S(1)} collective-permute-done((f32[392,128]{1,0:T(8,128)S(1)}, f32[392,128]{1,0:T(8,128)S(1)}, u32[]{:S(2)}, u32[]{:S(2)}) %collective-permute-start.1) | collective-permute-done | bytes 200736 | tf_op jit(solution)/shard_map/ppermute | solution.py:319
  13.8 0.4 collective-permute-done.2.refs_3_.refs_1_
  14.2 0.1 block_total.2
  14.3 3.4 %collective-permute-start.4 = (f32[392,128]{1,0:T(8,128)S(1)}, f32[392,128]{1,0:T(8,128)S(1)}, u32[]{:S(2)}, u32[]{:S(2)}) collective-permute-start(f32[392,128]{1,0:T(8,128)S(1)} %block_total.2), channel_id=1, source_target_pairs={{0,8},{4,12},{8,16},{12,20},{16,24},{20,28},{24,0},{28,4},{1,9},{5... | collective-permute-start | bytes 602120 | tf_op jit(solution)/shard_map/ppermute | solution.py:325
  17.7 2.3 %collective-permute-start.3 = (f32[392,128]{1,0:T(8,128)S(1)}, f32[392,128]{1,0:T(8,128)S(1)}, u32[]{:S(2)}, u32[]{:S(2)}) collective-permute-start(f32[392,128]{1,0:T(8,128)S(1)} %block_total.2), channel_id=1, source_target_pairs={{0,4},{4,8},{8,12},{12,16},{16,20},{20,24},{24,28},{28,0},{1,5},{5... | collective-permute-start | bytes 602120 | tf_op jit(solution)/shard_map/ppermute | solution.py:325
  20.0 0.0 collective-permute-done.8.refs_5_.refs_7_
  20.0 0.0 collective-permute-done.9.refs_6_.refs_8_
  20.0 6.3 %collective-permute-done.10.refs_7_.refs_9_ = f32[384,128]{1,0:T(8,128)S(1)} collective-permute-done((f32[384,128]{1,0:T(8,128)S(1)}, f32[384,128]{1,0:T(8,128)S(1)}, u32[]{:S(2)}, u32[]{:S(2)}) %collective-permute-start.10) | collective-permute-done | bytes 196640 | tf_op jit(solution)/shard_map/ppermute | solution.py:319
  26.3 0.1 block_total.3
  26.4 2.9 %collective-permute-start.12 = (f32[384,128]{1,0:T(8,128)S(1)}, f32[384,128]{1,0:T(8,128)S(1)}, u32[]{:S(2)}, u32[]{:S(2)}) collective-permute-start(f32[384,128]{1,0:T(8,128)S(1)} %block_total.3), channel_id=1, source_target_pairs={{0,8},{4,12},{8,16},{12,20},{16,24},{20,28},{24,0},{28,4},{1,9},{5... | collective-permute-start | bytes 589832 | tf_op jit(solution)/shard_map/ppermute | solution.py:325
  29.3 0.0 collective-permute-start.11
  29.3 0.0 collective-permute-done.4.refs_5_
  29.3 0.3 collective-permute-done.3.refs_4_
  29.6 0.3 prefixes.2
  29.9 2.8 %collective-permute-start.5 = (f32[392,128]{1,0:T(8,128)S(1)}, f32[392,128]{1,0:T(8,128)S(1)}, u32[]{:S(2)}, u32[]{:S(2)}) collective-permute-start(f32[392,128]{1,0:T(8,128)S(1)} %get-tuple-element.29), channel_id=1, source_target_pairs={{0,3},{1,2},{2,1},{3,0},{4,7},{5,6},{6,5},{7,4},{8,11},{9,10},{10,... | collective-permute-start | bytes 602120 | tf_op jit(solution)/shard_map/ppermute | solution.py:319
  32.7 0.3 collective-permute-start.6
  33.0 0.0 copy-start
  33.0 0.1 collective-permute-start.7
  33.1 0.0 collective-permute-done.12.refs_11_
  33.1 7.6 %collective-permute-done.11.refs_10_ = f32[384,128]{1,0:T(8,128)S(1)} collective-permute-done((f32[384,128]{1,0:T(8,128)S(1)}, f32[384,128]{1,0:T(8,128)S(1)}, u32[]{:S(2)}, u32[]{:S(2)}) %collective-permute-start.11) | collective-permute-done | bytes 196640 | tf_op jit(solution)/shard_map/ppermute | solution.py:325
  40.6 0.2 prefixes.3
  40.9 0.1 collective-permute-start.13
  41.0 1.7 %collective-permute-start.14 = (f32[384,128]{1,0:T(8,128)S(1)}, f32[384,128]{1,0:T(8,128)S(1)}, u32[]{:S(2)}, u32[]{:S(2)}) collective-permute-start(f32[384,128]{1,0:T(8,128)S(1)} %get-tuple-element.39), channel_id=1, source_target_pairs={{0,3},{1,2},{2,1},{3,0},{4,7},{5,6},{6,5},{7,4},{8,11},{9,10},{10,... | collective-permute-start | bytes 589832 | tf_op jit(solution)/shard_map/ppermute | solution.py:319
  42.7 0.0 collective-permute-done.5.refs_1_
  42.7 0.0 copy-start.3
  42.7 0.9 %collective-permute-start.15 = (f32[384,128]{1,0:T(8,128)S(1)}, f32[384,128]{1,0:T(8,128)S(1)}, u32[]{:S(2)}, u32[]{:S(2)}) collective-permute-start(f32[384,128]{1,0:T(8,128)S(1)} %get-tuple-element.41), channel_id=1, source_target_pairs={{0,1},{1,0},{2,3},{3,2},{4,5},{5,4},{6,7},{7,6},{8,9},{9,8},{10,11... | collective-permute-start | bytes 589832 | tf_op jit(solution)/shard_map/ppermute | solution.py:319
  43.6 0.0 collective-permute-done.6.refs_2_
  43.6 2.4 %collective-permute-done.7.refs_3_ = f32[392,128]{1,0:T(8,128)S(1)} collective-permute-done((f32[392,128]{1,0:T(8,128)S(1)}, f32[392,128]{1,0:T(8,128)S(1)}, u32[]{:S(2)}, u32[]{:S(2)}) %collective-permute-start.7) | collective-permute-done | bytes 200736 | tf_op jit(solution)/shard_map/ppermute | solution.py:319
  46.0 0.0 copy-done
  46.0 0.0 copy-done.3
  46.0 6.5 %solve.1 = (bf16[128,4096]{1,0:T(8,128)(2,1)S(1)}, f32[128,2048]{1,0:T(8,128)S(1)}, f32[128,2048]{1,0:T(8,128)}) custom-call(f32[16]{0:T(128)S(1)} %copy-done.3, s32[1,128]{1,0:T(1,128)S(1)} %bitcast.3, bf16[128,2048]{1,0:T(8,128)(2,1)S(1)} %copy-done, bf16[128,2048]{1,0:T(8,128)(2,1)S(1)} %copy-done.1, bf16[128,2048]{1,0:T(8,128)(2,1)S(1)} %copy-done.2, ...), custom_call_target="tpu_custom_call" | custom-call | flops 6442450944 | tf_op jit(solution)/shard_map/solve/pallas_call | solution.py:289
  52.5 0.0 collective-permute-done.15.refs_1_
  52.5 1.0 %readout.2.refs_2_ = f32[128,2048]{1,0:T(8,128)} custom-call(bf16[128,4096]{1,0:T(8,128)(2,1)S(1)} %get-tuple-element.32.x_ref, f32[128,2048]{1,0:T(8,128)S(1)} %get-tuple-element.33.near_ref, f32[384,128]{1,0:T(8,128)S(1)} %get-tuple-element.40.refs_0_, f32[384,128]{1,0:T(8,128)S(1)} %collective-permute-done.15.refs_1_, ...), custom_call_target="tpu_custom_call", output_to_operand_aliasing={{}: (4, {})} | custom-call | flops 536870912 | tf_op jit(solution)/shard_map/readout/pallas_call | solution.py:289
  53.5 0.0 collective-permute-done.13.refs_0_
  53.6 0.3 collective-permute-done.14.refs_1_
  53.9 1.0 %readout.3 = f32[128,2048]{1,0:T(8,128)} custom-call(bf16[128,4096]{1,0:T(8,128)(2,1)S(1)} %get-tuple-element.32.x_ref, f32[128,2048]{1,0:T(8,128)S(1)} %get-tuple-element.33.near_ref, f32[384,128]{1,0:T(8,128)S(1)} %collective-permute-done.13.refs_0_, f32[384,128]{1,0:T(8,128)S(1)} %collective-permute-done.14.refs_1_, ...), custom_call_target="tpu_custom_call", output_to_operand_aliasing={{}: (4, {})} | custom-call | flops 536870912 | tf_op jit(solution)/shard_map/readout/pallas_call | solution.py:289
Async XLA Ops:
  0.0 5.1 %copy-start.1 = (bf16[128,2048]{1,0:T(8,128)(2,1)S(1)}, bf16[128,2048]{1,0:T(8,128)(2,1)}, u32[]{:S(2)}) copy-start(bf16[128,2048]{1,0:T(8,128)(2,1)} %k_ref.3) | copy-start | bytes 1572868
  0.0 5.1 %copy-start.2 = (bf16[128,2048]{1,0:T(8,128)(2,1)S(1)}, bf16[128,2048]{1,0:T(8,128)(2,1)}, u32[]{:S(2)}) copy-start(bf16[128,2048]{1,0:T(8,128)(2,1)} %v_ref.3) | copy-start | bytes 1572868
  1.8 3.3 %copy-start.4 = (s32[128]{0:T(128)S(1)}, s32[128]{0:T(128)}, u32[]{:S(2)}) copy-start(s32[128]{0:T(128)} %param.8) | copy-start | bytes 1540
  1.8 7.8 %collective-permute-start = (f32[392,128]{1,0:T(8,128)S(1)}, f32[392,128]{1,0:T(8,128)S(1)}, u32[]{:S(2)}, u32[]{:S(2)}) collective-permute-start(f32[392,128]{1,0:T(8,128)S(1)} %get-tuple-element.25), channel_id=1, source_target_pairs={{0,3},{1,2},{2,1},{3,0},{4,7},{5,6},{6,5},{7,4},{8,11},{9,10},{10,... | collective-permute-start | bytes 602120 | tf_op jit(solution)/shard_map/ppermute | solution.py:319
  4.9 8.9 %collective-permute-start.1 = (f32[392,128]{1,0:T(8,128)S(1)}, f32[392,128]{1,0:T(8,128)S(1)}, u32[]{:S(2)}, u32[]{:S(2)}) collective-permute-start(f32[392,128]{1,0:T(8,128)S(1)} %get-tuple-element.26), channel_id=1, source_target_pairs={{0,2},{1,3},{2,0},{3,1},{4,6},{5,7},{6,4},{7,5},{8,10},{9,11},{10,... | collective-permute-start | bytes 602120 | tf_op jit(solution)/shard_map/ppermute | solution.py:319
  6.1 8.1 %collective-permute-start.2 = (f32[392,128]{1,0:T(8,128)S(1)}, f32[392,128]{1,0:T(8,128)S(1)}, u32[]{:S(2)}, u32[]{:S(2)}) collective-permute-start(f32[392,128]{1,0:T(8,128)S(1)} %get-tuple-element.27), channel_id=1, source_target_pairs={{0,1},{1,0},{2,3},{3,2},{4,5},{5,4},{6,7},{7,6},{8,9},{9,8},{10,11... | collective-permute-start | bytes 602120 | tf_op jit(solution)/shard_map/ppermute | solution.py:319
  6.4 13.7 %collective-permute-start.8 = (f32[384,128]{1,0:T(8,128)S(1)}, f32[384,128]{1,0:T(8,128)S(1)}, u32[]{:S(2)}, u32[]{:S(2)}) collective-permute-start(f32[384,128]{1,0:T(8,128)S(1)} %get-tuple-element.35), channel_id=1, source_target_pairs={{0,1},{1,0},{2,3},{3,2},{4,5},{5,4},{6,7},{7,6},{8,9},{9,8},{10,11... | collective-permute-start | bytes 589832 | tf_op jit(solution)/shard_map/ppermute | solution.py:319
  7.6 12.4 %collective-permute-start.9 = (f32[384,128]{1,0:T(8,128)S(1)}, f32[384,128]{1,0:T(8,128)S(1)}, u32[]{:S(2)}, u32[]{:S(2)}) collective-permute-start(f32[384,128]{1,0:T(8,128)S(1)} %get-tuple-element.36), channel_id=1, source_target_pairs={{0,2},{1,3},{2,0},{3,1},{4,6},{5,7},{6,4},{7,5},{8,10},{9,11},{10,... | collective-permute-start | bytes 589832 | tf_op jit(solution)/shard_map/ppermute | solution.py:319
  9.6 16.7 %collective-permute-start.10 = (f32[384,128]{1,0:T(8,128)S(1)}, f32[384,128]{1,0:T(8,128)S(1)}, u32[]{:S(2)}, u32[]{:S(2)}) collective-permute-start(f32[384,128]{1,0:T(8,128)S(1)} %get-tuple-element.37), channel_id=1, source_target_pairs={{0,3},{1,2},{2,1},{3,0},{4,7},{5,6},{6,5},{7,4},{8,11},{9,10},{10,... | collective-permute-start | bytes 589832 | tf_op jit(solution)/shard_map/ppermute | solution.py:319
  14.3 15.0 %collective-permute-start.4 = (f32[392,128]{1,0:T(8,128)S(1)}, f32[392,128]{1,0:T(8,128)S(1)}, u32[]{:S(2)}, u32[]{:S(2)}) collective-permute-start(f32[392,128]{1,0:T(8,128)S(1)} %block_total.2), channel_id=1, source_target_pairs={{0,8},{4,12},{8,16},{12,20},{16,24},{20,28},{24,0},{28,4},{1,9},{5... | collective-permute-start | bytes 602120 | tf_op jit(solution)/shard_map/ppermute | solution.py:325
  17.7 11.9 %collective-permute-start.3 = (f32[392,128]{1,0:T(8,128)S(1)}, f32[392,128]{1,0:T(8,128)S(1)}, u32[]{:S(2)}, u32[]{:S(2)}) collective-permute-start(f32[392,128]{1,0:T(8,128)S(1)} %block_total.2), channel_id=1, source_target_pairs={{0,4},{4,8},{8,12},{12,16},{16,20},{20,24},{24,28},{28,0},{1,5},{5... | collective-permute-start | bytes 602120 | tf_op jit(solution)/shard_map/ppermute | solution.py:325
  26.4 6.7 %collective-permute-start.12 = (f32[384,128]{1,0:T(8,128)S(1)}, f32[384,128]{1,0:T(8,128)S(1)}, u32[]{:S(2)}, u32[]{:S(2)}) collective-permute-start(f32[384,128]{1,0:T(8,128)S(1)} %block_total.3), channel_id=1, source_target_pairs={{0,8},{4,12},{8,16},{12,20},{16,24},{20,28},{24,0},{28,4},{1,9},{5... | collective-permute-start | bytes 589832 | tf_op jit(solution)/shard_map/ppermute | solution.py:325
  29.3 11.4 %collective-permute-start.11 = (f32[384,128]{1,0:T(8,128)S(1)}, f32[384,128]{1,0:T(8,128)S(1)}, u32[]{:S(2)}, u32[]{:S(2)}) collective-permute-start(f32[384,128]{1,0:T(8,128)S(1)} %block_total.3), channel_id=1, source_target_pairs={{0,4},{4,8},{8,12},{12,16},{16,20},{20,24},{24,28},{28,0},{1,5},{5... | collective-permute-start | bytes 589832 | tf_op jit(solution)/shard_map/ppermute | solution.py:325
  29.9 12.8 %collective-permute-start.5 = (f32[392,128]{1,0:T(8,128)S(1)}, f32[392,128]{1,0:T(8,128)S(1)}, u32[]{:S(2)}, u32[]{:S(2)}) collective-permute-start(f32[392,128]{1,0:T(8,128)S(1)} %get-tuple-element.29), channel_id=1, source_target_pairs={{0,3},{1,2},{2,1},{3,0},{4,7},{5,6},{6,5},{7,4},{8,11},{9,10},{10,... | collective-permute-start | bytes 602120 | tf_op jit(solution)/shard_map/ppermute | solution.py:319
  32.7 10.9 %collective-permute-start.6 = (f32[392,128]{1,0:T(8,128)S(1)}, f32[392,128]{1,0:T(8,128)S(1)}, u32[]{:S(2)}, u32[]{:S(2)}) collective-permute-start(f32[392,128]{1,0:T(8,128)S(1)} %get-tuple-element.30), channel_id=1, source_target_pairs={{0,1},{1,0},{2,3},{3,2},{4,5},{5,4},{6,7},{7,6},{8,9},{9,8},{10,11... | collective-permute-start | bytes 602120 | tf_op jit(solution)/shard_map/ppermute | solution.py:319
  33.0 13.0 %copy-start = (bf16[128,2048]{1,0:T(8,128)(2,1)S(1)}, bf16[128,2048]{1,0:T(8,128)(2,1)}, u32[]{:S(2)}) copy-start(bf16[128,2048]{1,0:T(8,128)(2,1)} %q_ref.1) | copy-start | bytes 1572868
  33.0 13.0 %collective-permute-start.7 = (f32[392,128]{1,0:T(8,128)S(1)}, f32[392,128]{1,0:T(8,128)S(1)}, u32[]{:S(2)}, u32[]{:S(2)}) collective-permute-start(f32[392,128]{1,0:T(8,128)S(1)} %get-tuple-element.31), channel_id=1, source_target_pairs={{0,2},{1,3},{2,0},{3,1},{4,6},{5,7},{6,4},{7,5},{8,10},{9,11},{10,... | collective-permute-start | bytes 602120 | tf_op jit(solution)/shard_map/ppermute | solution.py:319
  40.9 12.7 %collective-permute-start.13 = (f32[384,128]{1,0:T(8,128)S(1)}, f32[384,128]{1,0:T(8,128)S(1)}, u32[]{:S(2)}, u32[]{:S(2)}) collective-permute-start(f32[384,128]{1,0:T(8,128)S(1)} %get-tuple-element.38), channel_id=1, source_target_pairs={{0,2},{1,3},{2,0},{3,1},{4,6},{5,7},{6,4},{7,5},{8,10},{9,11},{10,... | collective-permute-start | bytes 589832 | tf_op jit(solution)/shard_map/ppermute | solution.py:319
  41.0 12.9 %collective-permute-start.14 = (f32[384,128]{1,0:T(8,128)S(1)}, f32[384,128]{1,0:T(8,128)S(1)}, u32[]{:S(2)}, u32[]{:S(2)}) collective-permute-start(f32[384,128]{1,0:T(8,128)S(1)} %get-tuple-element.39), channel_id=1, source_target_pairs={{0,3},{1,2},{2,1},{3,0},{4,7},{5,6},{6,5},{7,4},{8,11},{9,10},{10,... | collective-permute-start | bytes 589832 | tf_op jit(solution)/shard_map/ppermute | solution.py:319
  42.7 3.3 %copy-start.3 = (f32[16]{0:T(128)S(1)}, f32[16]{0:T(128)}, u32[]{:S(2)}) copy-start(f32[16]{0:T(128)} %ridge_ref.1) | copy-start | bytes 196
  42.7 9.8 %collective-permute-start.15 = (f32[384,128]{1,0:T(8,128)S(1)}, f32[384,128]{1,0:T(8,128)S(1)}, u32[]{:S(2)}, u32[]{:S(2)}) collective-permute-start(f32[384,128]{1,0:T(8,128)S(1)} %get-tuple-element.41), channel_id=1, source_target_pairs={{0,1},{1,0},{2,3},{3,2},{4,5},{5,4},{6,7},{7,6},{8,9},{9,8},{10,11... | collective-permute-start | bytes 589832 | tf_op jit(solution)/shard_map/ppermute | solution.py:319
